TPU v7x, 32 devices: a whole 2x2x4 slice. The times are simulated.
32 devices in a mesh: ctx: 16 (over z, x, core), fsdp: 2 (over y).
Axes of the slice: x: 2, y: 2, z: 4, core: 2. Of those that a mesh axis runs over, the one named last changes fastest.
Arguments:
- tokens: bfloat16 [2, 2048, 1024], P('fsdp', 'ctx'), may hold values from -6 to 6
- cotangent: bfloat16 [2, 2048, 1024], P('fsdp', 'ctx'), may hold values from -6 to 6
- positions: int32 [2, 2048], P('fsdp'), may hold values from 0 to 2047, as said below
- seq_lengths: int32 [2, 2], P('fsdp'), may hold values from 512 to 1536, as said below
- attention_gain: bfloat16 [1024], P('fsdp'), may hold values from 0.25 to 1.75
- query_weight: bfloat16 [1024, 2048], P('fsdp'), may hold values from -0.1875 to 0.1875
- key_weight: bfloat16 [1024, 1024], P('fsdp'), may hold values from -0.1875 to 0.1875
- value_weight: bfloat16 [1024, 1024], P('fsdp'), may hold values from -0.1875 to 0.1875
- headgate_weight: bfloat16 [1024, 16], P('fsdp'), may hold values from -0.1875 to 0.1875
- query_gain: bfloat16 [128], P('fsdp'), may hold values from 0.25 to 1.75
- key_gain: bfloat16 [128], P('fsdp'), may hold values from 0.25 to 1.75
- out_weight: bfloat16 [2048, 1024], P('fsdp'), may hold values from -3 to 3
- feedforward_gain: bfloat16 [1024], P('fsdp'), may hold values from 0.25 to 1.75
- gate_weight: bfloat16 [1024, 3072], P('fsdp'), may hold values from -0.1875 to 0.1875
- up_weight: bfloat16 [1024, 3072], P('fsdp'), may hold values from -0.1875 to 0.1875
- down_weight: bfloat16 [3072, 1024], P('fsdp'), may hold values from -0.109375 to 0.109375
Outputs:
- mixed: bfloat16 [2, 2048, 1024], P('fsdp', 'ctx')
- token_grad: bfloat16 [2, 2048, 1024], P('fsdp', 'ctx')
- attention_gain_grad: float32 [1024], P('fsdp')
- query_weight_grad: float32 [1024, 2048], P('fsdp')
- key_weight_grad: float32 [1024, 1024], P('fsdp')
- value_weight_grad: float32 [1024, 1024], P('fsdp')
- headgate_weight_grad: float32 [1024, 16], P('fsdp')
- query_gain_grad: float32 [128], P('fsdp')
- key_gain_grad: float32 [128], P('fsdp')
- out_weight_grad: float32 [2048, 1024], P('fsdp')
- feedforward_gain_grad: float32 [1024], P('fsdp')
- gate_weight_grad: float32 [1024, 3072], P('fsdp')
- up_weight_grad: float32 [1024, 3072], P('fsdp')
- down_weight_grad: float32 [3072, 1024], P('fsdp')
Inputs may be any that keep to these rules, and one draw needn't show every extreme that they name: For each group, a permutation of its 2048 packed positions; every aligned run of 64 rows holds 64 consecutive positions in rising order; the first and the last row of each group lie in one sequence. `seq_lengths`: each group's 2 lengths sum to 2048; every length is a multiple of 64.
All inputs are finite; a program needn't handle non-finite values.
Results may differ from a plain program's by a relative error of at most 0.023.
Values may be sent and summed in bfloat16 or wider, within the bound.
A program may use at most 320 MiB of HBM per device.

v0:
```python
import jax
import jax.numpy as jnp
from jax import lax
from jax.sharding import PartitionSpec as P

HEADS = 16
KV_HEADS = 8
HEAD_DIM = 128


EPS = 1e-06
THETA = 1000000.0
NEG = -1e30


def from_behind(value, axis, steps):
    count = lax.axis_size(axis)
    pairs = [(source, (source + steps) % count) for source in range(count)]
    return lax.ppermute(value, axis, pairs)


def norm_rows(values, gain):
    return values * lax.rsqrt(jnp.mean(values * values, axis=-1, keepdims=True) + EPS) * gain


def rotary(place):
    freqs = THETA ** (-jnp.arange(0, HEAD_DIM, 2).astype(jnp.float32) / HEAD_DIM)
    angles = place.astype(jnp.float32)[:, None] * freqs[None, :]
    return (jnp.cos(angles)[:, None, :], jnp.sin(angles)[:, None, :])


def prepare(raw, gain, cosine, sine, factor):
    count = raw.shape[0]
    heads = norm_rows(raw.reshape(count, -1, HEAD_DIM), gain)
    half = HEAD_DIM // 2
    first = heads[..., :half]
    second = heads[..., half:]
    turned = jnp.concatenate(
        [first * cosine - second * sine, second * cosine + first * sine], axis=-1
    )
    return turned * factor


def sequence_info(place_all, lengths):
    ends = jnp.cumsum(lengths)
    after = place_all[:, None] >= ends[None, :]
    segment = jnp.sum(after.astype(jnp.int32), axis=1)
    begin = jnp.sum(jnp.where(after, lengths[None, :], 0), axis=1)
    return (segment, place_all - begin)


def allowed_pairs(query_pos, query_seg, key_pos, key_seg):
    return (query_seg[:, None] == key_seg[None, :]) & (key_pos[None, :] <= query_pos[:, None])


def pair_terms(query_part, grad_part, log_part, delta_part, key_part, value_part, allowed):
    scores = jnp.einsum("tkgd,skd->kgts", query_part, key_part, preferred_element_type=jnp.float32)
    scores = jnp.where(allowed, scores, NEG)
    weights = jnp.where(allowed, jnp.exp(scores - log_part[..., None]), 0.0)
    weight_grad = jnp.einsum(
        "tkgd,skd->kgts", grad_part, value_part, preferred_element_type=jnp.float32
    )
    score_grad = weights * (weight_grad - delta_part[..., None])
    return (score_grad.astype(jnp.bfloat16), weights.astype(jnp.bfloat16))


def per_device(
    tokens,
    cotangent,
    positions,
    seq_lengths,
    attention_gain,
    query_weight,
    key_weight,
    value_weight,
    headgate_weight,
    query_gain,
    key_gain,
    out_weight,
    feedforward_gain,
    gate_weight,
    up_weight,
    down_weight,
):
    (
        query_full,
        key_full,
        value_full,
        headgate_full,
        out_full,
        gate_full,
        up_full,
        down_full,
        gain_one,
        gain_query,
        gain_key,
        gain_two,
    ) = (
        lax.all_gather(query_weight, "fsdp", axis=0, tiled=True),
        lax.all_gather(key_weight, "fsdp", axis=0, tiled=True),
        lax.all_gather(value_weight, "fsdp", axis=0, tiled=True),
        lax.all_gather(headgate_weight, "fsdp", axis=0, tiled=True),
        lax.all_gather(out_weight, "fsdp", axis=0, tiled=True),
        lax.all_gather(gate_weight, "fsdp", axis=0, tiled=True),
        lax.all_gather(up_weight, "fsdp", axis=0, tiled=True),
        lax.all_gather(down_weight, "fsdp", axis=0, tiled=True),
        lax.all_gather(attention_gain, "fsdp", axis=0, tiled=True),
        lax.all_gather(query_gain, "fsdp", axis=0, tiled=True),
        lax.all_gather(key_gain, "fsdp", axis=0, tiled=True),
        lax.all_gather(feedforward_gain, "fsdp", axis=0, tiled=True),
    )
    gain_one = gain_one.astype(jnp.float32)
    gain_query = gain_query.astype(jnp.float32)
    gain_key = gain_key.astype(jnp.float32)
    gain_two = gain_two.astype(jnp.float32)
    inputs = tokens[0].astype(jnp.float32)
    count = inputs.shape[0]
    groups = HEADS // KV_HEADS
    place_all = positions[0]
    seg_all, place_rel = sequence_info(place_all, seq_lengths[0])
    first_row = lax.axis_index("ctx") * count
    my_pos = lax.dynamic_slice_in_dim(place_all, first_row, count)
    my_seg = lax.dynamic_slice_in_dim(seg_all, first_row, count)
    my_rel = lax.dynamic_slice_in_dim(place_rel, first_row, count)
    cosine, sine = rotary(my_rel)

    def slices(start, size):
        return (
            lax.dynamic_slice_in_dim(place_all, start, size),
            lax.dynamic_slice_in_dim(seg_all, start, size),
        )

    normed, first_back = jax.vjp(norm_rows, inputs, gain_one)
    lowered = normed.astype(jnp.bfloat16)
    query_raw = jnp.dot(lowered, query_full, preferred_element_type=jnp.float32)
    key_raw = jnp.dot(lowered, key_full, preferred_element_type=jnp.float32)
    value_raw = jnp.dot(lowered, value_full, preferred_element_type=jnp.float32)
    gate_logit = jnp.dot(lowered, headgate_full, preferred_element_type=jnp.float32)
    head_gate = jax.nn.sigmoid(gate_logit)
    query_val, query_back = jax.vjp(
        lambda raw, gain: prepare(raw, gain, cosine, sine, HEAD_DIM ** (-0.5)),
        query_raw,
        gain_query,
    )
    key_val, key_back = jax.vjp(
        lambda raw, gain: prepare(raw, gain, cosine, sine, 1.0), key_raw, gain_key
    )
    queries = query_val.astype(jnp.bfloat16).reshape(count, KV_HEADS, groups, HEAD_DIM)
    keys = key_val.astype(jnp.bfloat16).reshape(count, KV_HEADS * HEAD_DIM)
    values = value_raw.astype(jnp.bfloat16)
    key_piece = lax.all_gather(keys, "ctx", axis=0, tiled=True)
    value_piece = lax.all_gather(values, "ctx", axis=0, tiled=True)
    size = key_piece.shape[0]
    key_pos, key_seg = slices(jnp.int32(0), size)
    allowed = allowed_pairs(my_pos, my_seg, key_pos, key_seg)
    top = jnp.full((KV_HEADS, groups, count), NEG, jnp.float32)
    scores = jnp.einsum(
        "tkgd,skd->kgts",
        queries,
        key_piece.reshape(size, KV_HEADS, HEAD_DIM),
        preferred_element_type=jnp.float32,
    )
    scores = jnp.where(allowed, scores, NEG)
    new_top = jnp.maximum(top, jnp.max(scores, axis=-1))
    weights = jnp.where(allowed, jnp.exp(scores - new_top[..., None]), 0.0)
    total = jnp.sum(weights, axis=-1)
    summed = jnp.einsum(
        "kgts,skd->kgtd",
        weights.astype(jnp.bfloat16),
        value_piece.reshape(size, KV_HEADS, HEAD_DIM),
        preferred_element_type=jnp.float32,
    )
    top, total, summed = (new_top, total, summed)
    attended = summed / total[..., None]
    log_total = top + jnp.log(total)
    heads_out = attended.transpose(2, 0, 1, 3).reshape(count, HEADS, HEAD_DIM)
    mixed_in = (
        (heads_out * head_gate[:, :, None]).reshape(count, HEADS * HEAD_DIM).astype(jnp.bfloat16)
    )
    middle = inputs + jnp.dot(mixed_in, out_full, preferred_element_type=jnp.float32)
    normed_two, second_back = jax.vjp(norm_rows, middle, gain_two)
    lowered_two = normed_two.astype(jnp.bfloat16)
    gate_proj = jnp.dot(lowered_two, gate_full, preferred_element_type=jnp.float32)
    up_proj = jnp.dot(lowered_two, up_full, preferred_element_type=jnp.float32)
    activation = jax.nn.silu(gate_proj)
    hidden = (activation * up_proj).astype(jnp.bfloat16)
    result = middle + jnp.dot(hidden, down_full, preferred_element_type=jnp.float32)
    mixed = result.astype(jnp.bfloat16)[None]
    upstream_low = cotangent[0]
    upstream = upstream_low.astype(jnp.float32)
    down_grad = jnp.einsum("tf,td->fd", hidden, upstream_low, preferred_element_type=jnp.float32)
    hidden_grad = jnp.einsum(
        "td,fd->tf", upstream_low, down_full, preferred_element_type=jnp.float32
    )
    sigma = jax.nn.sigmoid(gate_proj)
    gate_rows = (hidden_grad * up_proj * sigma * (1.0 + gate_proj * (1.0 - sigma))).astype(
        jnp.bfloat16
    )
    up_rows = (hidden_grad * activation).astype(jnp.bfloat16)
    gate_weight_grad = jnp.einsum(
        "td,tf->df", lowered_two, gate_rows, preferred_element_type=jnp.float32
    )
    up_weight_grad = jnp.einsum(
        "td,tf->df", lowered_two, up_rows, preferred_element_type=jnp.float32
    )
    lowered_two_grad = jnp.einsum(
        "tf,df->td", gate_rows, gate_full, preferred_element_type=jnp.float32
    ) + jnp.einsum("tf,df->td", up_rows, up_full, preferred_element_type=jnp.float32)
    middle_part, gain_two_grad = second_back(lowered_two_grad)
    middle_grad = upstream + middle_part
    middle_low = middle_grad.astype(jnp.bfloat16)
    out_weight_grad = jnp.einsum(
        "ti,td->id", mixed_in, middle_low, preferred_element_type=jnp.float32
    )
    mixed_grad = jnp.einsum(
        "td,id->ti", middle_low, out_full, preferred_element_type=jnp.float32
    ).reshape(count, HEADS, HEAD_DIM)
    heads_grad = (mixed_grad * head_gate[:, :, None]).astype(jnp.bfloat16)
    logit_grad = (jnp.sum(mixed_grad * heads_out, axis=-1) * head_gate * (1.0 - head_gate)).astype(
        jnp.bfloat16
    )
    headgate_weight_grad = jnp.einsum(
        "td,th->dh", lowered, logit_grad, preferred_element_type=jnp.float32
    )
    out_grad = heads_grad.reshape(count, KV_HEADS, groups, HEAD_DIM)
    delta = jnp.sum(
        out_grad.astype(jnp.float32) * heads_out.reshape(count, KV_HEADS, groups, HEAD_DIM), axis=-1
    ).transpose(1, 2, 0)
    cycle_size = lax.axis_size("ctx")
    my_index = lax.axis_index("ctx")

    def cycle_step(step, carry):
        pair_piece, grad_piece, query_sum = carry
        anchor = lax.rem(my_index - step + cycle_size, cycle_size)
        key_pos, key_seg = slices(anchor * count, count)
        allowed = allowed_pairs(my_pos, my_seg, key_pos, key_seg)
        key_heads = pair_piece[0].reshape(count, KV_HEADS, HEAD_DIM)
        value_heads = pair_piece[1].reshape(count, KV_HEADS, HEAD_DIM)
        score_grad, weights = pair_terms(
            queries, out_grad, log_total, delta, key_heads, value_heads, allowed
        )
        key_term = jnp.einsum(
            "kgts,tkgd->skd", score_grad, queries, preferred_element_type=jnp.float32
        ).reshape(count, KV_HEADS * HEAD_DIM)
        value_term = jnp.einsum(
            "kgts,tkgd->skd", weights, out_grad, preferred_element_type=jnp.float32
        ).reshape(count, KV_HEADS * HEAD_DIM)
        query_sum, grad_piece = (
            query_sum
            + jnp.einsum(
                "kgts,skd->tkgd", score_grad, key_heads, preferred_element_type=jnp.float32
            ),
            grad_piece + jnp.stack([key_term, value_term]),
        )
        pair_piece = from_behind(pair_piece, "ctx", 1)
        grad_piece = from_behind(grad_piece.astype(jnp.bfloat16), "ctx", 1).astype(grad_piece.dtype)
        return (pair_piece, grad_piece, query_sum)

    cycle_start = (
        jnp.stack([keys, values]),
        jnp.zeros((2, count, KV_HEADS * HEAD_DIM), jnp.float32),
        jnp.zeros((count, KV_HEADS, groups, HEAD_DIM), jnp.float32),
    )
    last_pair, home_grads, query_grad = lax.fori_loop(0, cycle_size, cycle_step, cycle_start)
    key_grad = home_grads[0].reshape(count, KV_HEADS, HEAD_DIM)
    value_grad = home_grads[1].reshape(count, KV_HEADS, HEAD_DIM)
    query_raw_grad, query_gain_grad = query_back(query_grad.reshape(count, HEADS, HEAD_DIM))
    key_raw_grad, key_gain_grad = key_back(key_grad)
    query_low = query_raw_grad.astype(jnp.bfloat16)
    key_low = key_raw_grad.astype(jnp.bfloat16)
    value_low = value_grad.reshape(count, KV_HEADS * HEAD_DIM).astype(jnp.bfloat16)
    query_weight_grad = jnp.einsum(
        "td,tf->df", lowered, query_low, preferred_element_type=jnp.float32
    )
    key_weight_grad = jnp.einsum("td,tf->df", lowered, key_low, preferred_element_type=jnp.float32)
    value_weight_grad = jnp.einsum(
        "td,tf->df", lowered, value_low, preferred_element_type=jnp.float32
    )
    lowered_grad = (
        jnp.einsum("tf,df->td", query_low, query_full, preferred_element_type=jnp.float32)
        + jnp.einsum("tf,df->td", key_low, key_full, preferred_element_type=jnp.float32)
        + jnp.einsum("tf,df->td", value_low, value_full, preferred_element_type=jnp.float32)
        + jnp.einsum("th,dh->td", logit_grad, headgate_full, preferred_element_type=jnp.float32)
    )
    input_part, gain_one_grad = first_back(lowered_grad)
    token_grad = (middle_grad + input_part).astype(jnp.bfloat16)[None]
    gradients = (
        gain_one_grad,
        query_weight_grad,
        key_weight_grad,
        value_weight_grad,
        headgate_weight_grad,
        query_gain_grad,
        key_gain_grad,
        out_weight_grad,
        gain_two_grad,
        gate_weight_grad,
        up_weight_grad,
        down_grad,
    )
    shards = (
        lax.psum_scatter(
            gradients[0].astype(jnp.bfloat16), "fsdp", scatter_dimension=0, tiled=True
        ).astype(jnp.float32),
        lax.psum_scatter(
            gradients[1].astype(jnp.bfloat16), "fsdp", scatter_dimension=0, tiled=True
        ).astype(jnp.float32),
        lax.psum_scatter(
            gradients[2].astype(jnp.bfloat16), "fsdp", scatter_dimension=0, tiled=True
        ).astype(jnp.float32),
        lax.psum_scatter(
            gradients[3].astype(jnp.bfloat16), "fsdp", scatter_dimension=0, tiled=True
        ).astype(jnp.float32),
        lax.psum_scatter(
            gradients[4].astype(jnp.bfloat16), "fsdp", scatter_dimension=0, tiled=True
        ).astype(jnp.float32),
        lax.psum_scatter(
            gradients[5].astype(jnp.bfloat16), "fsdp", scatter_dimension=0, tiled=True
        ).astype(jnp.float32),
        lax.psum_scatter(
            gradients[6].astype(jnp.bfloat16), "fsdp", scatter_dimension=0, tiled=True
        ).astype(jnp.float32),
        lax.psum_scatter(
            gradients[7].astype(jnp.bfloat16), "fsdp", scatter_dimension=0, tiled=True
        ).astype(jnp.float32),
        lax.psum_scatter(
            gradients[8].astype(jnp.bfloat16), "fsdp", scatter_dimension=0, tiled=True
        ).astype(jnp.float32),
        lax.psum_scatter(
            gradients[9].astype(jnp.bfloat16), "fsdp", scatter_dimension=0, tiled=True
        ).astype(jnp.float32),
        lax.psum_scatter(
            gradients[10].astype(jnp.bfloat16), "fsdp", scatter_dimension=0, tiled=True
        ).astype(jnp.float32),
        lax.psum_scatter(
            gradients[11].astype(jnp.bfloat16), "fsdp", scatter_dimension=0, tiled=True
        ).astype(jnp.float32),
    )
    totals = lax.psum(
        (
            shards[0],
            shards[1],
            shards[2],
            shards[3],
            shards[4],
            shards[5],
            shards[6],
            shards[7],
            shards[8],
            shards[9],
            shards[10],
            shards[11],
        ),
        "ctx",
    )
    return (mixed, token_grad) + tuple(totals)


def solution(mesh):
    in_specs = (
        P("fsdp", "ctx", None),
        P("fsdp", "ctx", None),
        P("fsdp", None),
        P("fsdp", None),
        P("fsdp"),
        P("fsdp", None),
        P("fsdp", None),
        P("fsdp", None),
        P("fsdp", None),
        P("fsdp"),
        P("fsdp"),
        P("fsdp", None),
        P("fsdp"),
        P("fsdp", None),
        P("fsdp", None),
        P("fsdp", None),
    )
    out_specs = (
        P("fsdp", "ctx", None),
        P("fsdp", "ctx", None),
        P("fsdp"),
        P("fsdp", None),
        P("fsdp", None),
        P("fsdp", None),
        P("fsdp", None),
        P("fsdp"),
        P("fsdp"),
        P("fsdp", None),
        P("fsdp"),
        P("fsdp", None),
        P("fsdp", None),
        P("fsdp", None),
    )
    return jax.shard_map(
        per_device, mesh=mesh, in_specs=in_specs, out_specs=out_specs, check_vma=False
    )
```

profile of v0, /device:TPU:0, one launch (start us, length us, event | category | flops | bytes accessed | tf_op | source)
XLA Modules:
  0.0 2038.7 jit_solution(3579083288201514936)
XLA Ops:
  9.5 5.3 all-gather
  14.9 30.5 %all-gather.18.cloned.1.call-done = bf16[1024,1024]{1,0:T(8,128)(2,1)} async-done(((bf16[512,1024]{1,0:T(8,128)(2,1)}), bf16[1024,1024]{1,0:T(8,128)(2,1)}) %all-gather.18.cloned.1.call-update) | async-done | bytes 2097168 | tf_op jit(solution)/shard_map/all_gather | solution.py:101
  50.3 4.9 all-reduce.12
  57.6 22.6 %all-gather.12.cloned.1.call-done = bf16[1024,1024]{1,0:T(8,128)(2,1)} async-done(((bf16[512,1024]{1,0:T(8,128)(2,1)}), bf16[1024,1024]{1,0:T(8,128)(2,1)}) %all-gather.12.cloned.1.call-update) | async-done | bytes 2097168 | tf_op jit(solution)/shard_map/all_gather | solution.py:100
  94.4 4.9 all_gather.50
  103.0 35.9 %all-gather.16.cloned.1.call-done = bf16[1024,2048]{1,0:T(8,128)(2,1)} async-done(((bf16[512,2048]{1,0:T(8,128)(2,1)}), bf16[1024,2048]{1,0:T(8,128)(2,1)}) %all-gather.16.cloned.1.call-update) | async-done | bytes 4194320 | tf_op jit(solution)/shard_map/all_gather | solution.py:99
  138.9 6.4 copy.97
  156.7 35.6 %all-gather.20.cloned.1.call-done = bf16[2048,1024]{1,0:T(8,128)(2,1)} async-done(((bf16[128,1024]{1,0:T(8,128)(2,1)}), bf16[2048,1024]{1,0:T(8,128)(2,1)}) %all-gather.20.cloned.1.call-update) | async-done | bytes 4194320 | tf_op jit(solution)/shard_map/all_gather | solution.py:152
  192.3 6.4 copy.124
  198.7 47.9 %all-gather.14.cloned.1.call-done = bf16[2048,1024]{0,1:T(8,128)(2,1)} async-done(((bf16[128,1024]{0,1:T(8,128)(2,1)}), bf16[2048,1024]{0,1:T(8,128)(2,1)}) %all-gather.14.cloned.1.call-update) | async-done | bytes 4194320 | tf_op jit(solution)/shard_map/all_gather | solution.py:151
  246.6 12.2 fusion.11
  258.8 9.2 fusion.12
  268.6 9.9 fusion.31
  278.6 24.4 %all-gather.22.cloned.1.call-done = bf16[2048,1024]{1,0:T(8,128)(2,1)} async-done(((bf16[1024,1024]{1,0:T(8,128)(2,1)}), bf16[2048,1024]{1,0:T(8,128)(2,1)}) %all-gather.22.cloned.1.call-update) | async-done | bytes 4194320 | tf_op jit(solution)/shard_map/all_gather | solution.py:103
  306.9 78.0 %all-gather.26.cloned.1.call-done = bf16[1024,3072]{1,0:T(8,128)(2,1)} async-done(((bf16[512,3072]{1,0:T(8,128)(2,1)}), bf16[1024,3072]{1,0:T(8,128)(2,1)}) %all-gather.26.cloned.1.call-update) | async-done | bytes 6291472 | tf_op jit(solution)/shard_map/all_gather | solution.py:105
  384.9 4.9 fusion.89
  389.8 77.0 %all-gather.24.cloned.1.call-done = bf16[1024,3072]{1,0:T(8,128)(2,1)} async-done(((bf16[512,3072]{1,0:T(8,128)(2,1)}), bf16[1024,3072]{1,0:T(8,128)(2,1)}) %all-gather.24.cloned.1.call-update) | async-done | bytes 6291472 | tf_op jit(solution)/shard_map/all_gather | solution.py:104
  466.9 4.9 fusion.88
  471.8 77.0 %all-gather.28.cloned.1.call-done = bf16[3072,1024]{1,0:T(8,128)(2,1)} async-done(((bf16[1536,1024]{1,0:T(8,128)(2,1)}), bf16[3072,1024]{1,0:T(8,128)(2,1)}) %all-gather.28.cloned.1.call-update) | async-done | bytes 6291472 | tf_op jit(solution)/shard_map/all_gather | solution.py:106
  548.8 7.2 multiply_convert_fusion
  558.2 5.9 multiply_reduce_fusion.4
  569.0 398.5 %while.18 = (s32[]{:T(128)}, bf16[2,128,1024]{1,2,0:T(8,128)(2,1)}, f32[2,128,1024]{1,2,0:T(8,128)S(1)}, f32[128,8,2,128]{3,0,2,1:T(8,128)}, s32[128]{0:T(128)},...) while((s32[]{:T(128)}, bf16[2,128,1024]{1,2,0:T(8,128)(2,1)}, ...), condition=%wide.region_12.13_spmd.clone, body=%wide.region_11.12_spmd.clone.sunk | while | flops 339263488 | bytes 21287316 | solution.py:264
  580.0 8.7 collective-permute-done.1
  604.6 9.1 collective-permute-done.1
  629.4 9.1 collective-permute-done.1
  654.3 9.1 collective-permute-done.1
  679.2 9.1 collective-permute-done.1
  704.1 9.1 collective-permute-done.1
  729.0 9.1 collective-permute-done.1
  753.9 9.1 collective-permute-done.1
  778.7 9.1 collective-permute-done.1
  803.6 9.1 collective-permute-done.1
  828.5 9.1 collective-permute-done.1
  853.4 9.1 collective-permute-done.1
  878.3 9.1 collective-permute-done.1
  903.1 9.1 collective-permute-done.1
  928.0 9.1 collective-permute-done.1
  952.9 9.1 collective-permute-done.1
  994.0 5.7 convolution_convert_fusion.1
  1000.0 5.7 convolution_convert_fusion.2
  1014.1 5.2 all-reduce.11
  1024.9 7.6 reduce-scatter.11.cloned.1.call-done
  1032.5 57.2 %reduce-scatter.17.cloned.1.call-done = bf16[1024,1024]{1,0:T(8,128)(2,1)} async-done(((bf16[2048,1024]{1,0:T(8,128)(2,1)}), bf16[1024,1024]{1,0:T(8,128)(2,1)}) %reduce-scatter.17.cloned.1.call-update) | async-done | bytes 2097168 | tf_op jit(solution)/shard_map/reduce_scatter | solution.py:323
  1089.7 57.1 %reduce-scatter.9.cloned.1.call-done = bf16[512,2048]{1,0:T(8,128)(2,1)} async-done(((bf16[1024,2048]{1,0:T(8,128)(2,1)}), bf16[512,2048]{1,0:T(8,128)(2,1)}) %reduce-scatter.9.cloned.1.call-update) | async-done | bytes 2097168 | tf_op jit(solution)/shard_map/reduce_scatter | solution.py:305
  1146.9 79.8 %reduce-scatter.23.cloned.1.call-done = bf16[1536,1024]{1,0:T(8,128)(2,1)} async-done(((bf16[3072,1024]{1,0:T(8,128)(2,1)}), bf16[1536,1024]{1,0:T(8,128)(2,1)}) %reduce-scatter.23.cloned.1.call-update) | async-done | bytes 3145744 | tf_op jit(solution)/shard_map/reduce_scatter | solution.py:335
  1226.7 79.9 %reduce-scatter.21.cloned.1.call-done = bf16[512,3072]{1,0:T(8,128)(2,1)} async-done(((bf16[1024,3072]{1,0:T(8,128)(2,1)}), bf16[512,3072]{1,0:T(8,128)(2,1)}) %reduce-scatter.21.cloned.1.call-update) | async-done | bytes 3145744 | tf_op jit(solution)/shard_map/reduce_scatter | solution.py:332
  1306.6 79.8 %reduce-scatter.19.cloned.1.call-done = bf16[512,3072]{1,0:T(8,128)(2,1)} async-done(((bf16[1024,3072]{1,0:T(8,128)(2,1)}), bf16[512,3072]{1,0:T(8,128)(2,1)}) %reduce-scatter.19.cloned.1.call-update) | async-done | bytes 3145744 | tf_op jit(solution)/shard_map/reduce_scatter | solution.py:329
  1386.4 645.5 %all-reduce.14 = (f32[512]{0:T(512)}, f32[512,2048]{1,0:T(8,128)}, f32[512,1024]{1,0:T(8,128)}, f32[512,1024]{1,0:T(8,128)}, f32[512,16]{0,1:T(8,128)}, /*index=...) all-reduce(f32[512]{0:T(512)S(1)} %get-tuple-element.411, ...), channel_id=1, replica_groups=mesh['ctx'=16,'fsdp'=2] {'ctx'}, use_global_device_ids=true, to_apply=%region_19.20 | all-reduce | flops 7873664 | bytes 47244288 | tf_op jit(solution)/shard_map/psum | solution.py:339
  (465 shorter events, 341.2 us)
Async XLA Ops:
  7.2 38.2 %all-gather.18.cloned.1.call-start = ((), (), s32[]{:S(2)}) async-start(), calls=%async_computation.11 | async-start | bytes 3145728 | tf_op jit(solution)/shard_map/all_gather | solution.py:101
  8.0 72.2 %all-gather.12.cloned.1.call-start = ((), (), s32[]{:S(2)}) async-start(), calls=%async_computation.8 | async-start | bytes 3145728 | tf_op jit(solution)/shard_map/all_gather | solution.py:100
  8.7 130.2 %all-gather.16.cloned.1.call-start = ((), (), s32[]{:S(2)}) async-start(), calls=%async_computation.10 | async-start | bytes 6291456 | tf_op jit(solution)/shard_map/all_gather | solution.py:99
  9.5 182.8 %all-gather.20.cloned.1.call-start = ((), (), s32[]{:S(2)}) async-start(), calls=%async_computation.12 | async-start | bytes 4456448 | tf_op jit(solution)/shard_map/all_gather | solution.py:152
  48.3 198.3 %all-gather.14.cloned.1.call-start = ((), (), s32[]{:S(2)}) async-start(), calls=%async_computation.9 | async-start | bytes 4456448 | tf_op jit(solution)/shard_map/all_gather | solution.py:151
  85.6 217.3 %all-gather.22.cloned.1.call-start = ((), (), s32[]{:S(2)}) async-start(), calls=%async_computation.13 | async-start | bytes 6291456 | tf_op jit(solution)/shard_map/all_gather | solution.py:103
  86.2 298.7 %all-gather.26.cloned.1.call-start = ((), (), s32[]{:S(2)}) async-start(), calls=%async_computation.15 | async-start | bytes 9437184 | tf_op jit(solution)/shard_map/all_gather | solution.py:105
  87.0 379.9 %all-gather.24.cloned.1.call-start = ((), (), s32[]{:S(2)}) async-start(), calls=%async_computation.14 | async-start | bytes 9437184 | tf_op jit(solution)/shard_map/all_gather | solution.py:104
  87.8 461.1 %all-gather.28.cloned.1.call-start = ((), (), s32[]{:S(2)}) async-start(), calls=%async_computation.16 | async-start | bytes 9437184 | tf_op jit(solution)/shard_map/all_gather | solution.py:106
  88.5 936.4 %reduce-scatter.15.cloned.1.call-start = ((), (), s32[]{:S(2)}) async-start(), calls=%async_computation.20 | async-start | bytes 49152 | tf_op jit(solution)/shard_map/reduce_scatter | solution.py:314
  567.5 457.4 %reduce-scatter.13.cloned.1.call-start = ((), (), s32[]{:S(2)}) async-start(), calls=%async_computation.19 | async-start | bytes 3145728 | tf_op jit(solution)/shard_map/reduce_scatter | solution.py:311
  577.1 11.6 collective-permute-start.1
  577.1 17.2 collective-permute-start
  602.0 11.6 collective-permute-start.1
  602.0 17.2 collective-permute-start
  626.9 11.6 collective-permute-start.1
  626.9 17.2 collective-permute-start
  651.8 11.6 collective-permute-start.1
  651.8 17.2 collective-permute-start
  676.7 11.6 collective-permute-start.1
  676.7 17.2 collective-permute-start
  701.5 11.6 collective-permute-start.1
  701.5 17.2 collective-permute-start
  726.4 11.6 collective-permute-start.1
  726.4 17.2 collective-permute-start
  751.3 11.6 collective-permute-start.1
  751.3 17.2 collective-permute-start
  776.2 11.6 collective-permute-start.1
  776.2 17.2 collective-permute-start
  801.1 11.6 collective-permute-start.1
  801.1 17.2 collective-permute-start
  826.0 11.6 collective-permute-start.1
  826.0 17.2 collective-permute-start
  850.8 11.6 collective-permute-start.1
  850.8 17.2 collective-permute-start
  875.7 11.6 collective-permute-start.1
  875.7 17.2 collective-permute-start
  900.6 11.6 collective-permute-start.1
  900.6 17.2 collective-permute-start
  925.5 17.2 collective-permute-start
  950.3 11.6 collective-permute-start.1
  950.3 17.2 collective-permute-start
  969.7 62.8 %reduce-scatter.11.cloned.1.call-start = ((), (), s32[]{:S(2)}) async-start(), calls=%async_computation.18 | async-start | bytes 3145728 | tf_op jit(solution)/shard_map/reduce_scatter | solution.py:308
  973.7 116.1 %reduce-scatter.17.cloned.1.call-start = ((), (), s32[]{:S(2)}) async-start(), calls=%async_computation.21 | async-start | bytes 6291456 | tf_op jit(solution)/shard_map/reduce_scatter | solution.py:323
  977.0 169.8 %reduce-scatter.9.cloned.1.call-start = ((), (), s32[]{:S(2)}) async-start(), calls=%async_computation.17 | async-start | bytes 6291456 | tf_op jit(solution)/shard_map/reduce_scatter | solution.py:305
  989.4 237.3 %reduce-scatter.23.cloned.1.call-start = ((), (), s32[]{:S(2)}) async-start(), calls=%async_computation.24 | async-start | bytes 9437184 | tf_op jit(solution)/shard_map/reduce_scatter | solution.py:335
  994.0 312.6 %reduce-scatter.21.cloned.1.call-start = ((), (), s32[]{:S(2)}) async-start(), calls=%async_computation.23 | async-start | bytes 9437184 | tf_op jit(solution)/shard_map/reduce_scatter | solution.py:332
  999.7 386.7 %reduce-scatter.19.cloned.1.call-start = ((), (), s32[]{:S(2)}) async-start(), calls=%async_computation.22 | async-start | bytes 9437184 | tf_op jit(solution)/shard_map/reduce_scatter | solution.py:329
  (55 other events, 1049.3 us)
Sparse Core Ops, SparseCore 0:
  9.6 35.8 all-gather.17
  47.0 33.1 all-gather.11
  81.8 57.1 all-gather.15
  141.5 50.7 all-gather.19
  194.8 51.7 all-gather.13
  248.0 54.9 all-gather.21
  304.5 80.3 all-gather.25
  386.4 80.3 all-gather.23
  468.4 80.3 all-gather.27
  567.6 9.8 reduce-scatter.14
  969.9 27.8 reduce-scatter.12
  1000.5 31.9 reduce-scatter.10
  1035.4 54.3 reduce-scatter.16
  1092.6 54.2 reduce-scatter.8
  1149.6 77.0 reduce-scatter.22
  1229.5 77.0 reduce-scatter.20
  1309.3 77.0 reduce-scatter.18
where the time goes:
time: 2060 us; the launch traced here: 2040 us
  waiting for transfers between devices  1010 us (49%)
  blocking collectives  670 us (33%)
  matrix products  193 us (9%)
  local copies, waits for them, and re-layouts  72.3 us (4%)
  other arithmetic  70.1 us (3%)
    psum x1, blocking collectives, per_device(): lax.psum((shards[0], shards[1], shards[2], shards[3], shards[4], shards[5...  646 us
    ppermute x32, waiting for transfers between devices, from_behind(): return lax.ppermute(value, axis, pairs)  217 us
    reduce_scatter x1, waiting for transfers between devices, per_device(): lax.psum_scatter(gradients[10].astype(jnp.bfloat16), 'fsdp', scatter_dime...  79.9 us
    reduce_scatter x1, waiting for transfers between devices, per_device(): lax.psum_scatter(gradients[11].astype(jnp.bfloat16), 'fsdp', scatter_dime...  79.8 us
    reduce_scatter x1, waiting for transfers between devices, per_device(): lax.psum_scatter(gradients[9].astype(jnp.bfloat16), 'fsdp', scatter_dimen...  79.8 us
    all_gather x1, waiting for transfers between devices, per_device(): lax.all_gather(up_weight, 'fsdp', axis=0, tiled=True)  78 us
    all_gather x1, waiting for transfers between devices, per_device(): lax.all_gather(down_weight, 'fsdp', axis=0, tiled=True)  77 us
    all_gather x1, waiting for transfers between devices, per_device(): lax.all_gather(gate_weight, 'fsdp', axis=0, tiled=True)  77 us
  transfers between devices with their start and end apart: 49, of which 47 were waited for; matrix products, arithmetic and copies ran while one was open for 15% of the time, Pallas kernels for 0%

commit v1 on v0

--- a/solution.py
+++ b/solution.py
@@ -1,6 +1,10 @@
+from functools import partial
+
 import jax
 import jax.numpy as jnp
 from jax import lax
+from jax.experimental import pallas as pl
+from jax.experimental.pallas import tpu as pltpu
 from jax.sharding import PartitionSpec as P
 
 HEADS = 16
@@ -62,6 +66,270 @@
     )
     score_grad = weights * (weight_grad - delta_part[..., None])
     return (score_grad.astype(jnp.bfloat16), weights.astype(jnp.bfloat16))
+
+
+MESH = pl.DeviceIdType.MESH
+UNITS = 15
+SIDE = 512
+PART = 256
+
+
+def place_of(index):
+    return (lax.div(index, 4), lax.rem(lax.div(index, 2), 2), lax.rem(index, 2))
+
+
+def unit_blocks(unit):
+    past = [lax.div(unit + 16 - edge, 16) for edge in (3, 9, 11)]
+    rows = (
+        unit * (1 - past[0]) + 3 * (past[0] - past[1]) + (unit - 5) * (past[1] - past[2]) + 6 * past[2]
+    )
+    columns = (unit - 2) * (past[0] - past[1]) + 7 * (past[1] - past[2]) + (unit - 3) * past[2]
+    return (rows, columns)
+
+
+def block_of(ref, index, size):
+    return ref[:, pl.ds(pl.multiple_of(index * size, size), size)]
+
+
+def sum_kernel(
+    depth,
+    rows_ref,
+    cols_ref,
+    out_ref,
+    out_x,
+    in_x,
+    out_z,
+    in_z,
+    done,
+    send_x,
+    recv_x,
+    send_z,
+    recv_z,
+    send_done,
+    recv_done,
+    keep_done,
+    send_half,
+    recv_half,
+    send_core,
+    recv_core,
+):
+    index = lax.axis_index("ctx")
+    group = lax.axis_index("fsdp")
+    z, x, core = place_of(index)
+    piece = SIDE // depth
+
+    def device(at_z, at_x, at_core):
+        return ((at_z * 2 + at_x) * 2 + at_core, group)
+
+    def ahead(offset):
+        return lax.rem(z + offset, depth)
+
+    def behind(offset):
+        return lax.rem(z + depth - offset, depth)
+
+    across = device(z, 1 - x, core)
+    beside = device(z, x, 1 - core)
+    barrier = pltpu.get_barrier_semaphore()
+    for offset in range(1, depth):
+        pl.semaphore_signal(
+            barrier, inc=1, device_id=device(ahead(offset), x, core), device_id_type=MESH
+        )
+    pl.semaphore_signal(barrier, inc=1, device_id=across, device_id_type=MESH)
+    pl.semaphore_signal(barrier, inc=1, device_id=beside, device_id_type=MESH)
+    pl.semaphore_wait(barrier, depth + 1)
+
+    def copy_to(target, source, destination, send, recv):
+        return pltpu.make_async_remote_copy(
+            src_ref=source,
+            dst_ref=destination,
+            send_sem=send,
+            recv_sem=recv,
+            device_id=target,
+            device_id_type=MESH,
+        )
+
+    def product(unit, half):
+        a, g = unit_blocks(unit)
+        left = block_of(rows_ref, a, SIDE)
+        right = block_of(cols_ref, g * 2 + half, PART)
+        return lax.dot_general(
+            left, right, (((0,), (0,)), ((), ())), preferred_element_type=jnp.float32
+        )
+
+    def rows_at(at_z):
+        return pl.ds(pl.multiple_of(at_z * piece, piece), piece)
+
+    def columns_at(at_x, at_core):
+        return pl.ds(pl.multiple_of((at_core * 2 + at_x) * PART, PART), PART)
+
+    def x_copy(unit):
+        return copy_to(across, out_x.at[unit], in_x.at[unit], send_x.at[unit], recv_x.at[unit])
+
+    def z_copy(unit, offset):
+        return copy_to(
+            device(ahead(offset), x, core),
+            out_z.at[unit, rows_at(ahead(offset))],
+            in_z.at[unit, offset - 1],
+            send_z.at[unit, offset - 1],
+            recv_z.at[unit, offset - 1],
+        )
+
+    def done_copy(unit, offset):
+        return copy_to(
+            device(ahead(offset), x, core),
+            done.at[unit],
+            out_ref.at[unit, rows_at(z), columns_at(x, core)],
+            send_done.at[unit, offset - 1],
+            recv_done.at[unit, offset - 1],
+        )
+
+    def done_wait(unit, offset):
+        return copy_to(
+            device(ahead(offset), x, core),
+            done.at[unit],
+            out_ref.at[unit, rows_at(behind(offset)), columns_at(x, core)],
+            send_done.at[unit, offset - 1],
+            recv_done.at[unit, offset - 1],
+        )
+
+    def keep_copy(unit):
+        return pltpu.make_async_copy(
+            done.at[unit], out_ref.at[unit, rows_at(z), columns_at(x, core)], keep_done.at[unit]
+        )
+
+    def half_copy(unit, at_x):
+        part = out_ref.at[unit, :, columns_at(at_x, core)]
+        return copy_to(across, part, part, send_half.at[unit], recv_half.at[unit])
+
+    def core_copy(unit, which, at_x, at_core):
+        part = out_ref.at[unit, :, columns_at(at_x, at_core)]
+        return copy_to(beside, part, part, send_core.at[unit, which], recv_core.at[unit, which])
+
+    def stage_send(unit):
+        out_x[unit] = product(unit, 1 - x).astype(jnp.bfloat16)
+        x_copy(unit).start()
+
+    def stage_pair(unit):
+        own = product(unit, x)
+        x_copy(unit).wait_recv()
+        out_z[unit] = (own + in_x[unit].astype(jnp.float32)).astype(jnp.bfloat16)
+        for offset in range(1, depth):
+            z_copy(unit, offset).start()
+
+    def stage_total(unit):
+        total = out_z[unit, rows_at(z)].astype(jnp.float32)
+        for offset in range(1, depth):
+            z_copy(unit, offset).wait_recv()
+            total = total + in_z[unit, offset - 1].astype(jnp.float32)
+        done[unit] = total.astype(jnp.bfloat16)
+        for offset in range(1, depth):
+            done_copy(unit, offset).start()
+        keep_copy(unit).start()
+
+    def stage_half(unit):
+        keep_copy(unit).wait()
+        for offset in range(1, depth):
+            done_wait(unit, offset).wait_recv()
+        half_copy(unit, x).start()
+        core_copy(unit, 0, x, core).start()
+
+    def stage_core(unit):
+        half_copy(unit, 1 - x).wait_recv()
+        core_copy(unit, 1, 1 - x, core).start()
+
+    def stage_end(unit):
+        core_copy(unit, 0, x, 1 - core).wait_recv()
+        core_copy(unit, 1, 1 - x, 1 - core).wait_recv()
+        x_copy(unit).wait_send()
+        for offset in range(1, depth):
+            z_copy(unit, offset).wait_send()
+            done_copy(unit, offset).wait_send()
+        half_copy(unit, x).wait_send()
+        core_copy(unit, 0, x, core).wait_send()
+        core_copy(unit, 1, 1 - x, core).wait_send()
+
+    stages = (stage_send, stage_pair, stage_total, stage_half, stage_core, stage_end)
+
+    def body(step, carry):
+        for late, stage in enumerate(stages):
+            unit = step - late
+
+            @pl.when((unit >= 0) & (unit < UNITS))
+            def run(stage=stage, unit=unit):
+                stage(unit)
+
+        return carry
+
+    lax.fori_loop(0, UNITS + len(stages) - 1, body, 0)
+
+
+def sum_grads(rows, columns, depth):
+    piece = SIDE // depth
+    dma = pltpu.SemaphoreType.DMA
+    return pl.pallas_call(
+        partial(sum_kernel, depth),
+        out_shape=jax.ShapeDtypeStruct((UNITS, SIDE, 2 * SIDE), jnp.bfloat16),
+        in_specs=[pl.BlockSpec(memory_space=pltpu.VMEM)] * 2,
+        out_specs=pl.BlockSpec(memory_space=pl.ANY),
+        scratch_shapes=[
+            pltpu.VMEM((UNITS, SIDE, PART), jnp.bfloat16),
+            pltpu.VMEM((UNITS, SIDE, PART), jnp.bfloat16),
+            pltpu.VMEM((UNITS, SIDE, PART), jnp.bfloat16),
+            pltpu.VMEM((UNITS, depth - 1, piece, PART), jnp.bfloat16),
+            pltpu.VMEM((UNITS, piece, PART), jnp.bfloat16),
+            dma((UNITS,)),
+            dma((UNITS,)),
+            dma((UNITS, depth - 1)),
+            dma((UNITS, depth - 1)),
+            dma((UNITS, depth - 1)),
+            dma((UNITS, depth - 1)),
+            dma((UNITS,)),
+            dma((UNITS,)),
+            dma((UNITS,)),
+            dma((UNITS, 2)),
+            dma((UNITS, 2)),
+        ],
+        compiler_params=pltpu.CompilerParams(
+            collective_id=1, has_side_effects=True, vmem_limit_bytes=48 * 2**20
+        ),
+        name="sum_grads",
+    )(rows, columns)
+
+
+def swap(value, axis, stride):
+    count = lax.axis_size(axis)
+    return lax.ppermute(value, axis, [(i, i ^ stride) for i in range(count)])
+
+
+def gather_tokens(pieces, blocks):
+    group = lax.axis_index("fsdp")
+    core = lax.rem(lax.axis_index("ctx"), 2)
+    count = pieces[0].shape[0]
+    halves = [p.reshape(count, 2, -1) for p in pieces]
+    mine = [lax.dynamic_index_in_dim(h, group, 1, keepdims=False) for h in halves]
+    others = [lax.dynamic_index_in_dim(h, 1 - group, 1, keepdims=False) for h in halves]
+    mine, others = (jnp.concatenate(mine, axis=1), jnp.concatenate(others, axis=1))
+    columns = jnp.concatenate([b.reshape(count, -1, 2, SIDE) for b in blocks], axis=1)
+    mine = jnp.concatenate([mine, swap(others, "fsdp", 1)], axis=0)
+    columns = jnp.concatenate([columns, swap(columns, "fsdp", 1)], axis=0)
+    own = lax.dynamic_index_in_dim(columns, core, 2, keepdims=False)
+    other = lax.dynamic_index_in_dim(columns, 1 - core, 2, keepdims=False)
+    rows = jnp.concatenate([mine, swap(mine, "ctx", 1)], axis=0)
+    columns = jnp.concatenate([own, swap(other, "ctx", 1)], axis=0)
+    return (rows, columns.reshape(columns.shape[0], -1))
+
+
+def beside_blocks(units):
+    return jnp.concatenate([units[i] for i in range(units.shape[0])], axis=1).astype(jnp.float32)
+
+
+def stacked_blocks(units):
+    return units.reshape(-1, units.shape[2]).astype(jnp.float32)
+
+
+def own_half(value):
+    half = value.shape[0] // 2
+    return lax.dynamic_slice_in_dim(value, lax.axis_index("fsdp") * half, half)
 
 
 def per_device(
@@ -188,7 +456,6 @@
     mixed = result.astype(jnp.bfloat16)[None]
     upstream_low = cotangent[0]
     upstream = upstream_low.astype(jnp.float32)
-    down_grad = jnp.einsum("tf,td->fd", hidden, upstream_low, preferred_element_type=jnp.float32)
     hidden_grad = jnp.einsum(
         "td,fd->tf", upstream_low, down_full, preferred_element_type=jnp.float32
     )
@@ -197,21 +464,12 @@
         jnp.bfloat16
     )
     up_rows = (hidden_grad * activation).astype(jnp.bfloat16)
-    gate_weight_grad = jnp.einsum(
-        "td,tf->df", lowered_two, gate_rows, preferred_element_type=jnp.float32
-    )
-    up_weight_grad = jnp.einsum(
-        "td,tf->df", lowered_two, up_rows, preferred_element_type=jnp.float32
-    )
     lowered_two_grad = jnp.einsum(
         "tf,df->td", gate_rows, gate_full, preferred_element_type=jnp.float32
     ) + jnp.einsum("tf,df->td", up_rows, up_full, preferred_element_type=jnp.float32)
     middle_part, gain_two_grad = second_back(lowered_two_grad)
     middle_grad = upstream + middle_part
     middle_low = middle_grad.astype(jnp.bfloat16)
-    out_weight_grad = jnp.einsum(
-        "ti,td->id", mixed_in, middle_low, preferred_element_type=jnp.float32
-    )
     mixed_grad = jnp.einsum(
         "td,id->ti", middle_low, out_full, preferred_element_type=jnp.float32
     ).reshape(count, HEADS, HEAD_DIM)
@@ -266,16 +524,9 @@
     value_grad = home_grads[1].reshape(count, KV_HEADS, HEAD_DIM)
     query_raw_grad, query_gain_grad = query_back(query_grad.reshape(count, HEADS, HEAD_DIM))
     key_raw_grad, key_gain_grad = key_back(key_grad)
-    query_low = query_raw_grad.astype(jnp.bfloat16)
-    key_low = key_raw_grad.astype(jnp.bfloat16)
+    query_low = query_raw_grad.astype(jnp.bfloat16).reshape(count, -1)
+    key_low = key_raw_grad.astype(jnp.bfloat16).reshape(count, -1)
     value_low = value_grad.reshape(count, KV_HEADS * HEAD_DIM).astype(jnp.bfloat16)
-    query_weight_grad = jnp.einsum(
-        "td,tf->df", lowered, query_low, preferred_element_type=jnp.float32
-    )
-    key_weight_grad = jnp.einsum("td,tf->df", lowered, key_low, preferred_element_type=jnp.float32)
-    value_weight_grad = jnp.einsum(
-        "td,tf->df", lowered, value_low, preferred_element_type=jnp.float32
-    )
     lowered_grad = (
         jnp.einsum("tf,df->td", query_low, query_full, preferred_element_type=jnp.float32)
         + jnp.einsum("tf,df->td", key_low, key_full, preferred_element_type=jnp.float32)
@@ -284,76 +535,34 @@
     )
     input_part, gain_one_grad = first_back(lowered_grad)
     token_grad = (middle_grad + input_part).astype(jnp.bfloat16)[None]
-    gradients = (
-        gain_one_grad,
-        query_weight_grad,
-        key_weight_grad,
-        value_weight_grad,
-        headgate_weight_grad,
-        query_gain_grad,
-        key_gain_grad,
-        out_weight_grad,
-        gain_two_grad,
-        gate_weight_grad,
-        up_weight_grad,
-        down_grad,
-    )
-    shards = (
-        lax.psum_scatter(
-            gradients[0].astype(jnp.bfloat16), "fsdp", scatter_dimension=0, tiled=True
-        ).astype(jnp.float32),
-        lax.psum_scatter(
-            gradients[1].astype(jnp.bfloat16), "fsdp", scatter_dimension=0, tiled=True
-        ).astype(jnp.float32),
-        lax.psum_scatter(
-            gradients[2].astype(jnp.bfloat16), "fsdp", scatter_dimension=0, tiled=True
-        ).astype(jnp.float32),
-        lax.psum_scatter(
-            gradients[3].astype(jnp.bfloat16), "fsdp", scatter_dimension=0, tiled=True
-        ).astype(jnp.float32),
-        lax.psum_scatter(
-            gradients[4].astype(jnp.bfloat16), "fsdp", scatter_dimension=0, tiled=True
-        ).astype(jnp.float32),
-        lax.psum_scatter(
-            gradients[5].astype(jnp.bfloat16), "fsdp", scatter_dimension=0, tiled=True
-        ).astype(jnp.float32),
-        lax.psum_scatter(
-            gradients[6].astype(jnp.bfloat16), "fsdp", scatter_dimension=0, tiled=True
-        ).astype(jnp.float32),
-        lax.psum_scatter(
-            gradients[7].astype(jnp.bfloat16), "fsdp", scatter_dimension=0, tiled=True
-        ).astype(jnp.float32),
-        lax.psum_scatter(
-            gradients[8].astype(jnp.bfloat16), "fsdp", scatter_dimension=0, tiled=True
-        ).astype(jnp.float32),
-        lax.psum_scatter(
-            gradients[9].astype(jnp.bfloat16), "fsdp", scatter_dimension=0, tiled=True
-        ).astype(jnp.float32),
-        lax.psum_scatter(
-            gradients[10].astype(jnp.bfloat16), "fsdp", scatter_dimension=0, tiled=True
-        ).astype(jnp.float32),
-        lax.psum_scatter(
-            gradients[11].astype(jnp.bfloat16), "fsdp", scatter_dimension=0, tiled=True
-        ).astype(jnp.float32),
-    )
-    totals = lax.psum(
-        (
-            shards[0],
-            shards[1],
-            shards[2],
-            shards[3],
-            shards[4],
-            shards[5],
-            shards[6],
-            shards[7],
-            shards[8],
-            shards[9],
-            shards[10],
-            shards[11],
-        ),
-        "ctx",
-    )
-    return (mixed, token_grad) + tuple(totals)
+    rows, columns = gather_tokens(
+        [hidden, lowered_two, mixed_in, lowered],
+        [upstream_low, gate_rows, up_rows, middle_low, query_low, key_low, value_low],
+    )
+    units = sum_grads(rows, columns, lax.axis_size("ctx") // 4)
+    small = [gain_one_grad, query_gain_grad, key_gain_grad, gain_two_grad, headgate_weight_grad]
+    flat = lax.psum(jnp.concatenate([s.reshape(-1) for s in small]), ("ctx", "fsdp"))
+    totals = []
+    start = 0
+    for s in small:
+        totals.append(own_half(flat[start : start + s.size].reshape(s.shape)))
+        start += s.size
+    return (
+        mixed,
+        token_grad,
+        totals[0],
+        beside_blocks(units[11:13]),
+        beside_blocks(units[13:14]),
+        beside_blocks(units[14:15]),
+        totals[4],
+        totals[1],
+        totals[2],
+        stacked_blocks(units[9:11]),
+        totals[3],
+        beside_blocks(units[3:6]),
+        beside_blocks(units[6:9]),
+        stacked_blocks(units[0:3]),
+    )
 
 
 def solution(mesh):

time: 2060 us -> 1440 us (0.70)
  blocking collectives: 670 us -> 19.4 us
  waiting for transfers between devices: 1010 us -> 813 us
  Pallas kernels: 0 us -> 195 us
  local copies, waits for them, and re-layouts: 72.3 us -> 110 us
  other arithmetic: 70.1 us -> 97.7 us
  matrix products: 193 us -> 169 us
    psum x1 -> x0, blocking collectives: 646 us -> none  [per_device(): lax.psum((shards[0], shards[1], shards[2], shards[3], shards[4], shards[5...]
    reduce_scatter x8 -> x0, waiting for transfers between devices: 362 us -> none  [the longest x1 79.9 us: per_device(): lax.psum_scatter(gradients[10].astype(jnp.bfloat16), 'fsdp', scatter_dime...]
    pallas_call x0 -> x1, Pallas kernels: none -> 195 us  [sum_grads(): pl.pallas_call(partial(sum_kernel, depth), out_shape=jax.ShapeDtypeStruct...]
    psum x0 -> x1, waiting for transfers between devices: none -> 114 us  [per_device(): lax.psum(jnp.concatenate([s.reshape(-1) for s in small]), ('ctx', 'fsdp'))]
    ppermute x0 -> x4, waiting for transfers between devices: none -> 46.5 us  [swap(): return lax.ppermute(value, axis, [(i, i ^ stride) for i in range(count)])]
    dot_general x7 -> x0, matrix products: 26.8 us -> none  [the longest x1 5.66 us: per_device(): jnp.einsum('td,tf->df', lowered_two, gate_rows, preferred_element_type=jn...]
  transfers between devices with their start and end apart: 49 -> 46, of which waited for: 47 -> 44; matrix products, arithmetic and copies ran while one was open for 15% -> 13% of each run, Pallas kernels for 0% -> 0%
where the time goes in v1:
time: 1440 us; the launch traced here: 1430 us
  waiting for transfers between devices  813 us (56%)
  Pallas kernels  195 us (14%)
  matrix products  169 us (12%)
  local copies, waits for them, and re-layouts  110 us (8%)
  other arithmetic  97.7 us (7%)
  blocking collectives  19.4 us (1%)
  between operations  16.2 us (1%)
    ppermute x32, waiting for transfers between devices, from_behind(): return lax.ppermute(value, axis, pairs)  217 us
    pallas_call x1, Pallas kernels, sum_grads(): pl.pallas_call(partial(sum_kernel, depth), out_shape=jax.ShapeDtypeStruct...  195 us
    psum x1, waiting for transfers between devices, per_device(): lax.psum(jnp.concatenate([s.reshape(-1) for s in small]), ('ctx', 'fsdp'))  114 us
    all_gather x1, waiting for transfers between devices, per_device(): lax.all_gather(gate_weight, 'fsdp', axis=0, tiled=True)  78.1 us
    all_gather x1, waiting for transfers between devices, per_device(): lax.all_gather(down_weight, 'fsdp', axis=0, tiled=True)  77 us
    all_gather x1, waiting for transfers between devices, per_device(): lax.all_gather(up_weight, 'fsdp', axis=0, tiled=True)  77 us
    all_gather x1, waiting for transfers between devices, per_device(): key_piece = lax.all_gather(keys, 'ctx', axis=0, tiled=True)  47.9 us
    ppermute x4, waiting for transfers between devices, swap(): return lax.ppermute(value, axis, [(i, i ^ stride) for i in range(count)])  46.5 us
  transfers between devices with their start and end apart: 46, of which 44 were waited for; matrix products, arithmetic and copies ran while one was open for 13% of the time, Pallas kernels for 0%

profile of v1, /device:TPU:0, one launch (start us, length us, event | category | flops | bytes accessed | tf_op | source)
XLA Modules:
  0.0 1426.7 jit_solution(8577150021255049331)
XLA Ops:
  9.5 5.3 all-gather
  15.0 30.5 %all-gather.18.cloned.1.call-done = bf16[1024,1024]{1,0:T(8,128)(2,1)} async-done(((bf16[512,1024]{1,0:T(8,128)(2,1)}), bf16[1024,1024]{1,0:T(8,128)(2,1)}) %all-gather.18.cloned.1.call-update) | async-done | bytes 2097168 | tf_op jit(solution)/shard_map/all_gather | solution.py:369
  50.3 4.9 all-reduce.6
  55.7 24.5 %all-gather.12.cloned.1.call-done = bf16[1024,1024]{1,0:T(8,128)(2,1)} async-done(((bf16[512,1024]{1,0:T(8,128)(2,1)}), bf16[1024,1024]{1,0:T(8,128)(2,1)}) %all-gather.12.cloned.1.call-update) | async-done | bytes 2097168 | tf_op jit(solution)/shard_map/all_gather | solution.py:368
  90.6 4.6 all_gather.50
  95.4 4.6 all-gather.1
  103.6 35.3 %all-gather.16.cloned.1.call-done = bf16[1024,2048]{1,0:T(8,128)(2,1)} async-done(((bf16[512,2048]{1,0:T(8,128)(2,1)}), bf16[1024,2048]{1,0:T(8,128)(2,1)}) %all-gather.16.cloned.1.call-update) | async-done | bytes 4194320 | tf_op jit(solution)/shard_map/all_gather | solution.py:367
  138.9 6.4 copy.144
  156.3 35.9 %all-gather.20.cloned.1.call-done = bf16[2048,1024]{1,0:T(8,128)(2,1)} async-done(((bf16[128,1024]{1,0:T(8,128)(2,1)}), bf16[2048,1024]{1,0:T(8,128)(2,1)}) %all-gather.20.cloned.1.call-update) | async-done | bytes 4194320 | tf_op jit(solution)/shard_map/all_gather | solution.py:420
  192.2 6.4 copy.189
  198.7 47.9 %all-gather.14.cloned.1.call-done = bf16[2048,1024]{0,1:T(8,128)(2,1)} async-done(((bf16[128,1024]{0,1:T(8,128)(2,1)}), bf16[2048,1024]{0,1:T(8,128)(2,1)}) %all-gather.14.cloned.1.call-update) | async-done | bytes 4194320 | tf_op jit(solution)/shard_map/all_gather | solution.py:419
  246.6 12.2 fusion.11
  258.8 9.2 fusion.12
  268.0 10.2 fusion.35
  278.3 24.6 %all-gather.22.cloned.1.call-done = bf16[2048,1024]{1,0:T(8,128)(2,1)} async-done(((bf16[1024,1024]{1,0:T(8,128)(2,1)}), bf16[2048,1024]{1,0:T(8,128)(2,1)}) %all-gather.22.cloned.1.call-update) | async-done | bytes 4194320 | tf_op jit(solution)/shard_map/all_gather | solution.py:371
  306.8 78.1 %all-gather.24.cloned.1.call-done = bf16[1024,3072]{1,0:T(8,128)(2,1)} async-done(((bf16[512,3072]{1,0:T(8,128)(2,1)}), bf16[1024,3072]{1,0:T(8,128)(2,1)}) %all-gather.24.cloned.1.call-update) | async-done | bytes 6291472 | tf_op jit(solution)/shard_map/all_gather | solution.py:372
  384.9 4.9 fusion.82
  389.8 77.0 %all-gather.26.cloned.1.call-done = bf16[1024,3072]{1,0:T(8,128)(2,1)} async-done(((bf16[512,3072]{1,0:T(8,128)(2,1)}), bf16[1024,3072]{1,0:T(8,128)(2,1)}) %all-gather.26.cloned.1.call-update) | async-done | bytes 6291472 | tf_op jit(solution)/shard_map/all_gather | solution.py:373
  466.8 4.9 fusion.83
  471.8 77.0 %all-gather.28.cloned.1.call-done = bf16[3072,1024]{1,0:T(8,128)(2,1)} async-done(((bf16[1536,1024]{1,0:T(8,128)(2,1)}), bf16[3072,1024]{1,0:T(8,128)(2,1)}) %all-gather.28.cloned.1.call-update) | async-done | bytes 6291472 | tf_op jit(solution)/shard_map/all_gather | solution.py:374
  548.8 7.5 multiply_convert_fusion
  563.0 5.4 fusion.84
  577.5 378.1 %while.18 = (s32[]{:T(128)}, bf16[2,128,1024]{1,2,0:T(8,128)(2,1)}, f32[2,128,1024]{1,2,0:T(8,128)S(1)}, f32[128,8,2,128]{3,0,2,1:T(8,128)}, s32[128]{0:T(128)S(...) while((s32[]{:T(128)}, bf16[2,128,1024]{1,2,0:T(8,128)(2,1)}, ...), condition=%wide.region_12.13_spmd.clone, body=%wide.region_11.12_spmd.clone.sunk | while | flops 339263488 | bytes 21287316 | solution.py:522
  586.8 8.7 collective-permute-done.1
  610.1 9.1 collective-permute-done.1
  633.7 9.1 collective-permute-done.1
  657.3 9.1 collective-permute-done.1
  681.0 9.1 collective-permute-done.1
  704.6 9.1 collective-permute-done.1
  728.2 9.1 collective-permute-done.1
  751.9 9.1 collective-permute-done.1
  775.5 9.1 collective-permute-done.1
  799.1 9.1 collective-permute-done.1
  822.8 9.1 collective-permute-done.1
  846.4 9.1 collective-permute-done.1
  870.0 9.1 collective-permute-done.1
  893.6 9.1 collective-permute-done.1
  917.3 9.1 collective-permute-done.1
  940.9 9.1 collective-permute-done.1
  1003.7 41.3 %collective-permute-done.4 = bf16[128,12,2,512]{0,3,1,2:T(8,128)(2,1)} collective-permute-done((bf16[128,12,2,512]{0,3,1,2:T(8,128)(2,1)}, bf16[128,12,2,512]{0,3,1,2:T(8,128)(2,1)}, u32[]{:S(2)}, u32[]{:S(2)}) %collective-permute-start.4) | collective-permute-done | bytes 3145760 | tf_op jit(solution)/shard_map/ppermute | solution.py:301
  1049.6 5.2 collective-permute-done.2
  1064.1 114.3 %all-reduce.9.cloned.1.call-done = f32[18688]{0:T(1024)} async-done(((f32[18688]{0:T(1024)}), f32[18688]{0:T(1024)}) %all-reduce.9.cloned.1.call-update) | async-done | bytes 74768 | tf_op jit(solution)/shard_map/psum | solution.py:544
  1184.1 5.1 pad_maximum_fusion.1.rows_ref
  1192.3 4.8 copy.171
  1197.1 5.3 pad_maximum_fusion.cols_ref
  1202.4 195.2 %sum_grads.1 = bf16[15,512,1024]{2,1,0:T(8,128)(2,1)} custom-call(bf16[512,3584]{1,0:T(8,128)(2,1)S(1)} %copy-done, bf16[512,6144]{1,0:T(8,128)(2,1)} %pad_maximum_fusion.cols_ref), custom_call_target="tpu_custom_call" | custom-call | tf_op jit(solution)/shard_map/sum_grads/pallas_call | solution.py:269
  1397.6 6.1 slice_bitcast_fusion.2
  1414.1 5.5 maximum_convert_fusion
  (545 shorter events, 364.5 us)
Async XLA Ops:
  7.3 38.2 %all-gather.18.cloned.1.call-start = ((), (), s32[]{:S(2)}) async-start(), calls=%async_computation.3 | async-start | bytes 3145728 | tf_op jit(solution)/shard_map/all_gather | solution.py:369
  8.0 72.2 %all-gather.12.cloned.1.call-start = ((), (), s32[]{:S(2)}) async-start(), calls=%async_computation | async-start | bytes 3145728 | tf_op jit(solution)/shard_map/all_gather | solution.py:368
  8.7 130.2 %all-gather.16.cloned.1.call-start = ((), (), s32[]{:S(2)}) async-start(), calls=%async_computation.2 | async-start | bytes 6291456 | tf_op jit(solution)/shard_map/all_gather | solution.py:367
  9.5 182.8 %all-gather.20.cloned.1.call-start = ((), (), s32[]{:S(2)}) async-start(), calls=%async_computation.4 | async-start | bytes 4456448 | tf_op jit(solution)/shard_map/all_gather | solution.py:420
  15.0 963.4 %copy-start.46 = (f32[128]{0:T(128)}, f32[128]{0:T(128)S(1)}, u32[]{:S(2)}) copy-start(f32[128]{0:T(128)S(1)} %fusion.68) | copy-start | bytes 1540
  48.3 198.3 %all-gather.14.cloned.1.call-start = ((), (), s32[]{:S(2)}) async-start(), calls=%async_computation.1 | async-start | bytes 4456448 | tf_op jit(solution)/shard_map/all_gather | solution.py:419
  85.6 217.3 %all-gather.22.cloned.1.call-start = ((), (), s32[]{:S(2)}) async-start(), calls=%async_computation.5 | async-start | bytes 6291456 | tf_op jit(solution)/shard_map/all_gather | solution.py:371
  86.2 298.7 %all-gather.24.cloned.1.call-start = ((), (), s32[]{:S(2)}) async-start(), calls=%async_computation.6 | async-start | bytes 9437184 | tf_op jit(solution)/shard_map/all_gather | solution.py:372
  87.0 379.9 %all-gather.26.cloned.1.call-start = ((), (), s32[]{:S(2)}) async-start(), calls=%async_computation.7 | async-start | bytes 9437184 | tf_op jit(solution)/shard_map/all_gather | solution.py:373
  87.8 461.0 %all-gather.28.cloned.1.call-start = ((), (), s32[]{:S(2)}) async-start(), calls=%async_computation.8 | async-start | bytes 9437184 | tf_op jit(solution)/shard_map/all_gather | solution.py:374
  88.5 1089.9 %all-reduce.9.cloned.1.call-start = ((), (), s32[]{:S(2)}) async-start(), calls=%async_computation.9 | async-start | bytes 155648 | tf_op jit(solution)/shard_map/psum | solution.py:544
  577.5 379.0 %copy-start.58 = (f32[128]{0:T(128)S(1)}, f32[128]{0:T(128)}, u32[]{:S(2)}) copy-start(f32[128]{0:T(128)} %copy-done.57) | copy-start | bytes 1540
  583.9 11.6 collective-permute-start.1
  583.9 17.2 %collective-permute-start = (bf16[2,128,1024]{1,2,0:T(8,128)(2,1)S(1)}, bf16[2,128,1024]{1,2,0:T(8,128)(2,1)}, u32[]{:S(2)}, u32[]{:S(2)}) collective-permute-start(bf16[2,128,1024]{1,2,0:T(8,128)(2,1)S(1)} %copy.226), channel_id=1, source_target_pairs={{0,2},{2,4},{4,6},{6,8},{8,10},{10,12},{12,14},{14,16},{16,18},{18... | collective-permute-start | bytes 1572872 | tf_op jit(solution)/shard_map/while/body/eval_jaxpr/ppermute | solution.py:23
  607.5 11.6 collective-permute-start.1
  607.5 17.2 %collective-permute-start = (bf16[2,128,1024]{1,2,0:T(8,128)(2,1)S(1)}, bf16[2,128,1024]{1,2,0:T(8,128)(2,1)}, u32[]{:S(2)}, u32[]{:S(2)}) collective-permute-start(bf16[2,128,1024]{1,2,0:T(8,128)(2,1)S(1)} %copy.226), channel_id=1, source_target_pairs={{0,2},{2,4},{4,6},{6,8},{8,10},{10,12},{12,14},{14,16},{16,18},{18... | collective-permute-start | bytes 1572872 | tf_op jit(solution)/shard_map/while/body/eval_jaxpr/ppermute | solution.py:23
  631.2 11.6 collective-permute-start.1
  631.2 17.2 %collective-permute-start = (bf16[2,128,1024]{1,2,0:T(8,128)(2,1)S(1)}, bf16[2,128,1024]{1,2,0:T(8,128)(2,1)}, u32[]{:S(2)}, u32[]{:S(2)}) collective-permute-start(bf16[2,128,1024]{1,2,0:T(8,128)(2,1)S(1)} %copy.226), channel_id=1, source_target_pairs={{0,2},{2,4},{4,6},{6,8},{8,10},{10,12},{12,14},{14,16},{16,18},{18... | collective-permute-start | bytes 1572872 | tf_op jit(solution)/shard_map/while/body/eval_jaxpr/ppermute | solution.py:23
  654.8 11.6 collective-permute-start.1
  654.8 17.2 %collective-permute-start = (bf16[2,128,1024]{1,2,0:T(8,128)(2,1)S(1)}, bf16[2,128,1024]{1,2,0:T(8,128)(2,1)}, u32[]{:S(2)}, u32[]{:S(2)}) collective-permute-start(bf16[2,128,1024]{1,2,0:T(8,128)(2,1)S(1)} %copy.226), channel_id=1, source_target_pairs={{0,2},{2,4},{4,6},{6,8},{8,10},{10,12},{12,14},{14,16},{16,18},{18... | collective-permute-start | bytes 1572872 | tf_op jit(solution)/shard_map/while/body/eval_jaxpr/ppermute | solution.py:23
  678.4 11.6 collective-permute-start.1
  678.4 17.2 %collective-permute-start = (bf16[2,128,1024]{1,2,0:T(8,128)(2,1)S(1)}, bf16[2,128,1024]{1,2,0:T(8,128)(2,1)}, u32[]{:S(2)}, u32[]{:S(2)}) collective-permute-start(bf16[2,128,1024]{1,2,0:T(8,128)(2,1)S(1)} %copy.226), channel_id=1, source_target_pairs={{0,2},{2,4},{4,6},{6,8},{8,10},{10,12},{12,14},{14,16},{16,18},{18... | collective-permute-start | bytes 1572872 | tf_op jit(solution)/shard_map/while/body/eval_jaxpr/ppermute | solution.py:23
  702.0 11.6 collective-permute-start.1
  702.1 17.2 %collective-permute-start = (bf16[2,128,1024]{1,2,0:T(8,128)(2,1)S(1)}, bf16[2,128,1024]{1,2,0:T(8,128)(2,1)}, u32[]{:S(2)}, u32[]{:S(2)}) collective-permute-start(bf16[2,128,1024]{1,2,0:T(8,128)(2,1)S(1)} %copy.226), channel_id=1, source_target_pairs={{0,2},{2,4},{4,6},{6,8},{8,10},{10,12},{12,14},{14,16},{16,18},{18... | collective-permute-start | bytes 1572872 | tf_op jit(solution)/shard_map/while/body/eval_jaxpr/ppermute | solution.py:23
  725.7 11.6 collective-permute-start.1
  725.7 17.2 %collective-permute-start = (bf16[2,128,1024]{1,2,0:T(8,128)(2,1)S(1)}, bf16[2,128,1024]{1,2,0:T(8,128)(2,1)}, u32[]{:S(2)}, u32[]{:S(2)}) collective-permute-start(bf16[2,128,1024]{1,2,0:T(8,128)(2,1)S(1)} %copy.226), channel_id=1, source_target_pairs={{0,2},{2,4},{4,6},{6,8},{8,10},{10,12},{12,14},{14,16},{16,18},{18... | collective-permute-start | bytes 1572872 | tf_op jit(solution)/shard_map/while/body/eval_jaxpr/ppermute | solution.py:23
  749.3 11.6 collective-permute-start.1
  749.3 17.2 %collective-permute-start = (bf16[2,128,1024]{1,2,0:T(8,128)(2,1)S(1)}, bf16[2,128,1024]{1,2,0:T(8,128)(2,1)}, u32[]{:S(2)}, u32[]{:S(2)}) collective-permute-start(bf16[2,128,1024]{1,2,0:T(8,128)(2,1)S(1)} %copy.226), channel_id=1, source_target_pairs={{0,2},{2,4},{4,6},{6,8},{8,10},{10,12},{12,14},{14,16},{16,18},{18... | collective-permute-start | bytes 1572872 | tf_op jit(solution)/shard_map/while/body/eval_jaxpr/ppermute | solution.py:23
  772.9 11.6 collective-permute-start.1
  772.9 17.2 %collective-permute-start = (bf16[2,128,1024]{1,2,0:T(8,128)(2,1)S(1)}, bf16[2,128,1024]{1,2,0:T(8,128)(2,1)}, u32[]{:S(2)}, u32[]{:S(2)}) collective-permute-start(bf16[2,128,1024]{1,2,0:T(8,128)(2,1)S(1)} %copy.226), channel_id=1, source_target_pairs={{0,2},{2,4},{4,6},{6,8},{8,10},{10,12},{12,14},{14,16},{16,18},{18... | collective-permute-start | bytes 1572872 | tf_op jit(solution)/shard_map/while/body/eval_jaxpr/ppermute | solution.py:23
  796.6 11.6 collective-permute-start.1
  796.6 17.2 %collective-permute-start = (bf16[2,128,1024]{1,2,0:T(8,128)(2,1)S(1)}, bf16[2,128,1024]{1,2,0:T(8,128)(2,1)}, u32[]{:S(2)}, u32[]{:S(2)}) collective-permute-start(bf16[2,128,1024]{1,2,0:T(8,128)(2,1)S(1)} %copy.226), channel_id=1, source_target_pairs={{0,2},{2,4},{4,6},{6,8},{8,10},{10,12},{12,14},{14,16},{16,18},{18... | collective-permute-start | bytes 1572872 | tf_op jit(solution)/shard_map/while/body/eval_jaxpr/ppermute | solution.py:23
  820.2 11.6 collective-permute-start.1
  820.2 17.2 %collective-permute-start = (bf16[2,128,1024]{1,2,0:T(8,128)(2,1)S(1)}, bf16[2,128,1024]{1,2,0:T(8,128)(2,1)}, u32[]{:S(2)}, u32[]{:S(2)}) collective-permute-start(bf16[2,128,1024]{1,2,0:T(8,128)(2,1)S(1)} %copy.226), channel_id=1, source_target_pairs={{0,2},{2,4},{4,6},{6,8},{8,10},{10,12},{12,14},{14,16},{16,18},{18... | collective-permute-start | bytes 1572872 | tf_op jit(solution)/shard_map/while/body/eval_jaxpr/ppermute | solution.py:23
  843.8 11.6 collective-permute-start.1
  843.8 17.2 %collective-permute-start = (bf16[2,128,1024]{1,2,0:T(8,128)(2,1)S(1)}, bf16[2,128,1024]{1,2,0:T(8,128)(2,1)}, u32[]{:S(2)}, u32[]{:S(2)}) collective-permute-start(bf16[2,128,1024]{1,2,0:T(8,128)(2,1)S(1)} %copy.226), channel_id=1, source_target_pairs={{0,2},{2,4},{4,6},{6,8},{8,10},{10,12},{12,14},{14,16},{16,18},{18... | collective-permute-start | bytes 1572872 | tf_op jit(solution)/shard_map/while/body/eval_jaxpr/ppermute | solution.py:23
  867.5 11.6 collective-permute-start.1
  867.5 17.2 %collective-permute-start = (bf16[2,128,1024]{1,2,0:T(8,128)(2,1)S(1)}, bf16[2,128,1024]{1,2,0:T(8,128)(2,1)}, u32[]{:S(2)}, u32[]{:S(2)}) collective-permute-start(bf16[2,128,1024]{1,2,0:T(8,128)(2,1)S(1)} %copy.226), channel_id=1, source_target_pairs={{0,2},{2,4},{4,6},{6,8},{8,10},{10,12},{12,14},{14,16},{16,18},{18... | collective-permute-start | bytes 1572872 | tf_op jit(solution)/shard_map/while/body/eval_jaxpr/ppermute | solution.py:23
  891.1 11.6 collective-permute-start.1
  891.1 17.2 %collective-permute-start = (bf16[2,128,1024]{1,2,0:T(8,128)(2,1)S(1)}, bf16[2,128,1024]{1,2,0:T(8,128)(2,1)}, u32[]{:S(2)}, u32[]{:S(2)}) collective-permute-start(bf16[2,128,1024]{1,2,0:T(8,128)(2,1)S(1)} %copy.226), channel_id=1, source_target_pairs={{0,2},{2,4},{4,6},{6,8},{8,10},{10,12},{12,14},{14,16},{16,18},{18... | collective-permute-start | bytes 1572872 | tf_op jit(solution)/shard_map/while/body/eval_jaxpr/ppermute | solution.py:23
  914.7 11.6 collective-permute-start.1
  914.7 17.2 %collective-permute-start = (bf16[2,128,1024]{1,2,0:T(8,128)(2,1)S(1)}, bf16[2,128,1024]{1,2,0:T(8,128)(2,1)}, u32[]{:S(2)}, u32[]{:S(2)}) collective-permute-start(bf16[2,128,1024]{1,2,0:T(8,128)(2,1)S(1)} %copy.226), channel_id=1, source_target_pairs={{0,2},{2,4},{4,6},{6,8},{8,10},{10,12},{12,14},{14,16},{16,18},{18... | collective-permute-start | bytes 1572872 | tf_op jit(solution)/shard_map/while/body/eval_jaxpr/ppermute | solution.py:23
  938.3 11.6 collective-permute-start.1
  938.3 17.2 %collective-permute-start = (bf16[2,128,1024]{1,2,0:T(8,128)(2,1)S(1)}, bf16[2,128,1024]{1,2,0:T(8,128)(2,1)}, u32[]{:S(2)}, u32[]{:S(2)}) collective-permute-start(bf16[2,128,1024]{1,2,0:T(8,128)(2,1)S(1)} %copy.226), channel_id=1, source_target_pairs={{0,2},{2,4},{4,6},{6,8},{8,10},{10,12},{12,14},{14,16},{16,18},{18... | collective-permute-start | bytes 1572872 | tf_op jit(solution)/shard_map/while/body/eval_jaxpr/ppermute | solution.py:23
  978.0 67.0 %collective-permute-start.4 = (bf16[128,12,2,512]{0,3,1,2:T(8,128)(2,1)}, bf16[128,12,2,512]{0,3,1,2:T(8,128)(2,1)}, u32[]{:S(2)}, u32[]{:S(2)}) collective-permute-start(bf16[128,12,2,512]{0,3,1,2:T(8,128)(2,1)} %constant_dynamic-update-slice_fusion.1), channel_id=1, source_target_pairs={{0,1},{1,0},{2,3},{3,2},{4,5},{5,4},{6,7},{7,6},{8,9},{9,8},{10,11... | collective-permute-start | bytes 9437192 | tf_op jit(solution)/shard_map/ppermute | solution.py:301
  990.0 64.9 %collective-permute-start.2 = (bf16[128,3584]{1,0:T(8,128)(2,1)}, bf16[128,3584]{1,0:T(8,128)(2,1)}, u32[]{:S(2)}, u32[]{:S(2)}) collective-permute-start(bf16[128,3584]{1,0:T(8,128)(2,1)} %pad_maximum_fusion.3), channel_id=1, source_target_pairs={{0,1},{1,0},{2,3},{3,2},{4,5},{5,4},{6,7},{7,6},{8,9},{9,8},{10,11... | collective-permute-start | bytes 2752520 | tf_op jit(solution)/shard_map/ppermute | solution.py:301
  1049.5 142.7 %collective-permute-start.5 = (bf16[256,12,512]{0,2,1:T(8,128)(2,1)}, bf16[256,12,512]{0,2,1:T(8,128)(2,1)}, u32[]{:S(2)}, u32[]{:S(2)}) collective-permute-start(bf16[256,12,512]{0,2,1:T(8,128)(2,1)} %get-tuple-element.420), channel_id=1, source_target_pairs={{0,2},{2,0},{4,6},{6,4},{8,10},{10,8},{12,14},{14,12},{16,18},{18,... | collective-permute-start | bytes 9437192 | tf_op jit(solution)/shard_map/ppermute | solution.py:301
  1057.4 126.7 %collective-permute-start.3 = (bf16[256,3584]{1,0:T(8,128)(2,1)}, bf16[256,3584]{1,0:T(8,128)(2,1)}, u32[]{:S(2)}, u32[]{:S(2)}) collective-permute-start(bf16[256,3584]{1,0:T(8,128)(2,1)} %pad_maximum_fusion.2), channel_id=1, source_target_pairs={{0,2},{2,0},{4,6},{6,4},{8,10},{10,8},{12,14},{14,12},{16,18},{18,... | collective-permute-start | bytes 5505032 | tf_op jit(solution)/shard_map/ppermute | solution.py:301
  (74 other events, 2411.9 us)
Sparse Core Ops, SparseCore 0:
  9.6 35.8 all-gather.17
  47.0 33.1 all-gather.11
  81.7 57.1 all-gather.15
  141.5 50.7 all-gather.19
  194.8 51.7 all-gather.13
  248.0 54.9 all-gather.21
  304.5 80.3 all-gather.23
  386.4 80.3 all-gather.25
  468.4 80.3 all-gather.27
  1058.5 119.8 all-reduce.8

commit v2 on v1

--- a/solution.py
+++ b/solution.py
@@ -70,12 +70,191 @@
 
 MESH = pl.DeviceIdType.MESH
 UNITS = 15
+VECTOR_ROWS = 80
 SIDE = 512
 PART = 256
 
 
 def place_of(index):
     return (lax.div(index, 4), lax.rem(lax.div(index, 2), 2), lax.rem(index, 2))
+
+
+def remote(target, source, destination, send, recv):
+    return pltpu.make_async_remote_copy(
+        src_ref=source,
+        dst_ref=destination,
+        send_sem=send,
+        recv_sem=recv,
+        device_id=target,
+        device_id_type=MESH,
+    )
+
+
+def greet(targets):
+    barrier = pltpu.get_barrier_semaphore()
+    for target in targets:
+        pl.semaphore_signal(barrier, inc=1, device_id=target, device_id_type=MESH)
+    pl.semaphore_wait(barrier, len(targets))
+
+
+def gather_kernel(count, *refs):
+    shards = refs[:count]
+    small = refs[count]
+    fulls = refs[count + 1 : 2 * count + 1]
+    small_all = refs[2 * count + 1]
+    held = refs[2 * count + 2 : 3 * count + 2]
+    keep, send, recv, small_sems = refs[3 * count + 2 :]
+    index = lax.axis_index("ctx")
+    group = lax.axis_index("fsdp")
+    z, x, core = place_of(index)
+    near = lax.rem(z, 2)
+    pair = z + 1 - 2 * near
+    over = (index, 1 - group)
+    across = ((z * 2 + 1 - x) * 2 + core, group)
+    along = ((pair * 2 + x) * 2 + core, group)
+    beside = (z * 4 + x * 2 + 1 - core, group)
+    greet([over, across, along, beside])
+
+    def rows(w, start, size, half=None):
+        piece = shards[w].shape[0] // 16
+        first = start * piece
+        if half is not None:
+            first = first + half * shards[w].shape[0]
+        return pl.ds(pl.multiple_of(first, piece), size * piece)
+
+    def own(at_core, sub):
+        if sub == 0:
+            return at_core * 8 + near * 2 + x
+        return at_core * 8 + 4 + x * 2 + near
+
+    def over_copy(w, sub):
+        return remote(
+            over,
+            shards[w].at[rows(w, own(core, sub), 1)],
+            fulls[w].at[rows(w, own(core, sub), 1, group)],
+            send.at[w, sub],
+            recv.at[w, sub],
+        )
+
+    def over_wait(w, sub):
+        part = fulls[w].at[rows(w, own(core, sub), 1, 1 - group)]
+        remote(over, part, part, send.at[w, sub], recv.at[w, sub]).wait_recv()
+
+    def pass_on(w, slot, target, start, size):
+        part = fulls[w].at[rows(w, start, size, 1 - group)]
+        return remote(target, part, part, send.at[w, slot], recv.at[w, slot])
+
+    def first_x(w, at_x):
+        return pass_on(w, 2, across, core * 8 + near * 2 + at_x, 1)
+
+    def first_z(w, at_near):
+        return pass_on(w, 3, along, core * 8 + 4 + x * 2 + at_near, 1)
+
+    def second_z(w, at_near):
+        return pass_on(w, 4, along, core * 8 + at_near * 2, 2)
+
+    def second_x(w, at_x):
+        return pass_on(w, 5, across, core * 8 + 4 + at_x * 2, 2)
+
+    def core_copy(w, sub, at_core):
+        return pass_on(w, 6 + sub, beside, at_core * 8 + sub * 4, 4)
+
+    def small_copy(at):
+        return remote(over, small, small_all.at[at], small_sems.at[0], small_sems.at[1])
+
+    small_copy(group).start()
+    small_all[group] = small[...]
+    for w in range(count):
+        over_copy(w, 0).start()
+        over_copy(w, 1).start()
+    takes = [pltpu.make_async_copy(shards[w], held[w], keep.at[w, 0]) for w in range(count)]
+    keeps = [
+        pltpu.make_async_copy(held[w], fulls[w].at[rows(w, 0, 16, group)], keep.at[w, 1])
+        for w in range(count)
+    ]
+    for w in range(count):
+        takes[w].start()
+
+    def stage_one(w):
+        takes[w].wait()
+        keeps[w].start()
+        over_wait(w, 0)
+        first_x(w, x).start()
+        over_wait(w, 1)
+        first_z(w, near).start()
+
+    def stage_two(w):
+        first_x(w, 1 - x).wait_recv()
+        second_z(w, near).start()
+        first_z(w, 1 - near).wait_recv()
+        second_x(w, x).start()
+
+    def stage_three(w):
+        second_z(w, 1 - near).wait_recv()
+        core_copy(w, 0, core).start()
+        second_x(w, 1 - x).wait_recv()
+        core_copy(w, 1, core).start()
+
+    def stage_end(w):
+        core_copy(w, 0, 1 - core).wait_recv()
+        core_copy(w, 1, 1 - core).wait_recv()
+        over_copy(w, 0).wait_send()
+        over_copy(w, 1).wait_send()
+        first_x(w, x).wait_send()
+        first_z(w, near).wait_send()
+        second_z(w, near).wait_send()
+        second_x(w, x).wait_send()
+        core_copy(w, 0, core).wait_send()
+        core_copy(w, 1, core).wait_send()
+        keeps[w].wait()
+
+    stages = (stage_one, stage_two, stage_three, stage_end)
+    for step in range(count + len(stages) - 1):
+        for late, stage in enumerate(stages):
+            if 0 <= step - late < count:
+                stage(step - late)
+    small_copy(1 - group).wait_recv()
+    small_copy(group).wait_send()
+
+
+def gather_weights(shards, small):
+    count = len(shards)
+    dma = pltpu.SemaphoreType.DMA
+    return pl.pallas_call(
+        partial(gather_kernel, count),
+        out_shape=[
+            jax.ShapeDtypeStruct((2 * s.shape[0], s.shape[1]), jnp.bfloat16) for s in shards
+        ]
+        + [jax.ShapeDtypeStruct((2,) + small.shape, jnp.bfloat16)],
+        in_specs=[pl.BlockSpec(memory_space=pl.ANY)] * count
+        + [pl.BlockSpec(memory_space=pltpu.VMEM)],
+        out_specs=[pl.BlockSpec(memory_space=pl.ANY)] * count
+        + [pl.BlockSpec(memory_space=pltpu.VMEM)],
+        scratch_shapes=[pltpu.VMEM(s.shape, jnp.bfloat16) for s in shards]
+        + [dma((count, 2)), dma((count, 8)), dma((count, 8)), dma((2,))],
+        compiler_params=pltpu.CompilerParams(
+            collective_id=2, has_side_effects=True, vmem_limit_bytes=32 * 2**20
+        ),
+        name="gather_weights",
+    )(*shards, small)
+
+
+def pack_rows(pieces, rows):
+    flat = jnp.concatenate([p.reshape(-1) for p in pieces])
+    return jnp.pad(flat, (0, rows * 128 - flat.shape[0])).reshape(rows, 128)
+
+
+def unpack_rows(packed, shapes):
+    flat = packed.reshape(-1)
+    out = []
+    start = 0
+    for shape in shapes:
+        size = 1
+        for extent in shape:
+            size *= extent
+        out.append(flat[start : start + size].reshape(shape))
+        start += size
+    return out
 
 
 def unit_blocks(unit):
@@ -95,7 +274,14 @@
     depth,
     rows_ref,
     cols_ref,
+    small_ref,
     out_ref,
+    small_out,
+    small_part,
+    small_in,
+    small_deep,
+    small_send,
+    small_recv,
     out_x,
     in_x,
     out_z,
@@ -129,24 +315,10 @@
 
     across = device(z, 1 - x, core)
     beside = device(z, x, 1 - core)
-    barrier = pltpu.get_barrier_semaphore()
-    for offset in range(1, depth):
-        pl.semaphore_signal(
-            barrier, inc=1, device_id=device(ahead(offset), x, core), device_id_type=MESH
-        )
-    pl.semaphore_signal(barrier, inc=1, device_id=across, device_id_type=MESH)
-    pl.semaphore_signal(barrier, inc=1, device_id=beside, device_id_type=MESH)
-    pl.semaphore_wait(barrier, depth + 1)
-
-    def copy_to(target, source, destination, send, recv):
-        return pltpu.make_async_remote_copy(
-            src_ref=source,
-            dst_ref=destination,
-            send_sem=send,
-            recv_sem=recv,
-            device_id=target,
-            device_id_type=MESH,
-        )
+    over = (index, 1 - group)
+    peers = [device(ahead(offset), x, core) for offset in range(1, depth)]
+    greet(peers + [across, beside, over])
+    copy_to = remote
 
     def product(unit, half):
         a, g = unit_blocks(unit)
@@ -250,6 +422,48 @@
 
     stages = (stage_send, stage_pair, stage_total, stage_half, stage_core, stage_end)
 
+    def small_copy(at, target, source):
+        return remote(
+            target, source, small_in.at[at], small_send.at[at], small_recv.at[at]
+        )
+
+    def small_start():
+        small_copy(0, over, small_ref.at[1 - group]).start()
+
+    def small_beside():
+        small_copy(0, over, small_ref.at[1 - group]).wait()
+        small_part[0] = small_ref[group] + small_in[0]
+        small_copy(1, beside, small_part.at[0]).start()
+
+    def small_across():
+        small_copy(1, beside, small_part.at[0]).wait()
+        small_part[1] = small_part[0] + small_in[1]
+        small_copy(2, across, small_part.at[1]).start()
+
+    def small_along(offset):
+        return remote(
+            device(ahead(offset), x, core),
+            small_part.at[2],
+            small_deep.at[offset - 1],
+            small_send.at[2 + offset],
+            small_recv.at[2 + offset],
+        )
+
+    def small_spread():
+        small_copy(2, across, small_part.at[1]).wait()
+        small_part[2] = small_part[1] + small_in[2]
+        for offset in range(1, depth):
+            small_along(offset).start()
+
+    def small_end():
+        total = small_part[2]
+        for offset in range(1, depth):
+            small_along(offset).wait()
+            total = total + small_deep[offset - 1]
+        small_out[...] = total
+
+    small_stages = (small_start, small_beside, small_across, small_spread, small_end)
+
     def body(step, carry):
         for late, stage in enumerate(stages):
             unit = step - late
@@ -258,20 +472,37 @@
             def run(stage=stage, unit=unit):
                 stage(unit)
 
+        for at, small_stage in enumerate(small_stages):
+
+            @pl.when(step == 2 * at)
+            def run_small(small_stage=small_stage):
+                small_stage()
+
         return carry
 
     lax.fori_loop(0, UNITS + len(stages) - 1, body, 0)
 
 
-def sum_grads(rows, columns, depth):
+def sum_grads(rows, columns, small, depth):
     piece = SIDE // depth
     dma = pltpu.SemaphoreType.DMA
     return pl.pallas_call(
         partial(sum_kernel, depth),
-        out_shape=jax.ShapeDtypeStruct((UNITS, SIDE, 2 * SIDE), jnp.bfloat16),
-        in_specs=[pl.BlockSpec(memory_space=pltpu.VMEM)] * 2,
-        out_specs=pl.BlockSpec(memory_space=pl.ANY),
+        out_shape=[
+            jax.ShapeDtypeStruct((UNITS, SIDE, 2 * SIDE), jnp.bfloat16),
+            jax.ShapeDtypeStruct(small.shape[1:], jnp.float32),
+        ],
+        in_specs=[pl.BlockSpec(memory_space=pltpu.VMEM)] * 3,
+        out_specs=[
+            pl.BlockSpec(memory_space=pl.ANY),
+            pl.BlockSpec(memory_space=pltpu.VMEM),
+        ],
         scratch_shapes=[
+            pltpu.VMEM((3,) + small.shape[1:], jnp.float32),
+            pltpu.VMEM((3,) + small.shape[1:], jnp.float32),
+            pltpu.VMEM((depth - 1,) + small.shape[1:], jnp.float32),
+            dma((2 + depth,)),
+            dma((2 + depth,)),
             pltpu.VMEM((UNITS, SIDE, PART), jnp.bfloat16),
             pltpu.VMEM((UNITS, SIDE, PART), jnp.bfloat16),
             pltpu.VMEM((UNITS, SIDE, PART), jnp.bfloat16),
@@ -293,7 +524,7 @@
             collective_id=1, has_side_effects=True, vmem_limit_bytes=48 * 2**20
         ),
         name="sum_grads",
-    )(rows, columns)
+    )(rows, columns, small)
 
 
 def swap(value, axis, stride):
@@ -325,11 +556,6 @@
 
 def stacked_blocks(units):
     return units.reshape(-1, units.shape[2]).astype(jnp.float32)
-
-
-def own_half(value):
-    half = value.shape[0] // 2
-    return lax.dynamic_slice_in_dim(value, lax.axis_index("fsdp") * half, half)
 
 
 def per_device(
@@ -350,33 +576,27 @@
     up_weight,
     down_weight,
 ):
+    vectors = (attention_gain, feedforward_gain, query_gain, key_gain, headgate_weight)
+    vector_shapes = [v.shape for v in vectors]
     (
         query_full,
         key_full,
         value_full,
-        headgate_full,
         out_full,
         gate_full,
         up_full,
         down_full,
-        gain_one,
-        gain_query,
-        gain_key,
-        gain_two,
-    ) = (
-        lax.all_gather(query_weight, "fsdp", axis=0, tiled=True),
-        lax.all_gather(key_weight, "fsdp", axis=0, tiled=True),
-        lax.all_gather(value_weight, "fsdp", axis=0, tiled=True),
-        lax.all_gather(headgate_weight, "fsdp", axis=0, tiled=True),
-        lax.all_gather(out_weight, "fsdp", axis=0, tiled=True),
-        lax.all_gather(gate_weight, "fsdp", axis=0, tiled=True),
-        lax.all_gather(up_weight, "fsdp", axis=0, tiled=True),
-        lax.all_gather(down_weight, "fsdp", axis=0, tiled=True),
-        lax.all_gather(attention_gain, "fsdp", axis=0, tiled=True),
-        lax.all_gather(query_gain, "fsdp", axis=0, tiled=True),
-        lax.all_gather(key_gain, "fsdp", axis=0, tiled=True),
-        lax.all_gather(feedforward_gain, "fsdp", axis=0, tiled=True),
-    )
+        vectors_full,
+    ) = gather_weights(
+        (query_weight, key_weight, value_weight, out_weight, gate_weight, up_weight, down_weight),
+        pack_rows(vectors, VECTOR_ROWS),
+    )
+    gain_one, gain_two, gain_query, gain_key, headgate_full = [
+        jnp.concatenate(halves, axis=0)
+        for halves in zip(
+            unpack_rows(vectors_full[0], vector_shapes), unpack_rows(vectors_full[1], vector_shapes)
+        )
+    ]
     gain_one = gain_one.astype(jnp.float32)
     gain_query = gain_query.astype(jnp.float32)
     gain_key = gain_key.astype(jnp.float32)
@@ -539,14 +759,17 @@
         [hidden, lowered_two, mixed_in, lowered],
         [upstream_low, gate_rows, up_rows, middle_low, query_low, key_low, value_low],
     )
-    units = sum_grads(rows, columns, lax.axis_size("ctx") // 4)
-    small = [gain_one_grad, query_gain_grad, key_gain_grad, gain_two_grad, headgate_weight_grad]
-    flat = lax.psum(jnp.concatenate([s.reshape(-1) for s in small]), ("ctx", "fsdp"))
-    totals = []
-    start = 0
-    for s in small:
-        totals.append(own_half(flat[start : start + s.size].reshape(s.shape)))
-        start += s.size
+    vector_grads = (
+        gain_one_grad,
+        gain_two_grad,
+        query_gain_grad,
+        key_gain_grad,
+        headgate_weight_grad,
+    )
+    split_grads = [g.reshape((2, -1)) for g in vector_grads]
+    small = jnp.stack([pack_rows([g[half] for g in split_grads], VECTOR_ROWS) for half in (0, 1)])
+    units, small_total = sum_grads(rows, columns, small, lax.axis_size("ctx") // 4)
+    totals = unpack_rows(small_total, vector_shapes)
     return (
         mixed,
         token_grad,
@@ -555,10 +778,10 @@
         beside_blocks(units[13:14]),
         beside_blocks(units[14:15]),
         totals[4],
+        totals[2],
+        totals[3],
+        stacked_blocks(units[9:11]),
         totals[1],
-        totals[2],
-        stacked_blocks(units[9:11]),
-        totals[3],
         beside_blocks(units[3:6]),
         beside_blocks(units[6:9]),
         stacked_blocks(units[0:3]),

time: 1440 us -> 1080 us (0.75)
  waiting for transfers between devices: 813 us -> 306 us
  Pallas kernels: 195 us -> 280 us
  local copies, waits for them, and re-layouts: 110 us -> 190 us
  other arithmetic: 97.7 us -> 125 us
  blocking collectives: 19.4 us -> 0 us
  matrix products: 169 us -> 153 us
    all_gather x7 -> x0, waiting for transfers between devices: 347 us -> none  [the longest x1 78.1 us: per_device(): lax.all_gather(gate_weight, 'fsdp', axis=0, tiled=True)]
    psum x1 -> x0, waiting for transfers between devices: 114 us -> none  [per_device(): lax.psum(jnp.concatenate([s.reshape(-1) for s in small]), ('ctx', 'fsdp'))]
    pallas_call x1 -> x2, Pallas kernels: 195 us -> 280 us  [the longest x1 199 us: sum_grads(): pl.pallas_call(partial(sum_kernel, depth), out_shape=[jax.ShapeDtypeStruc...]
    slice x16, local copies, waits for them, and re-layouts: 0.56 us -> 28.2 us  [cycle_step(): value_heads = pair_piece[1].reshape(count, KV_HEADS, HEAD_DIM)]
    all_gather x1, waiting for transfers between devices: 47.9 us -> 22.7 us  [per_device(): key_piece = lax.all_gather(keys, 'ctx', axis=0, tiled=True)]
    convert_element_type x16, other arithmetic: 17.8 us -> 33.3 us  [cycle_step(): from_behind(grad_piece.astype(jnp.bfloat16), 'ctx', 1)]
    ppermute x32, waiting for transfers between devices: 217 us -> 202 us  [from_behind(): return lax.ppermute(value, axis, pairs)]
    all_gather x3 -> x0, blocking collectives: 14.5 us -> none  [the longest x1 5.26 us: per_device(): lax.all_gather(attention_gain, 'fsdp', axis=0, tiled=True)]
  transfers between devices with their start and end apart: 46 -> 38, of which waited for: 44 -> 36; matrix products, arithmetic and copies ran while one was open for 13% -> 16% of each run, Pallas kernels for 0% -> 0%
where the time goes in v2:
time: 1080 us; the launch traced here: 1070 us
  waiting for transfers between devices  306 us (28%)
  Pallas kernels  280 us (26%)
  local copies, waits for them, and re-layouts  190 us (18%)
  matrix products  153 us (14%)
  other arithmetic  125 us (12%)
  between operations  15.5 us (1%)
    ppermute x32, waiting for transfers between devices, from_behind(): return lax.ppermute(value, axis, pairs)  202 us
    pallas_call x1, Pallas kernels, sum_grads(): pl.pallas_call(partial(sum_kernel, depth), out_shape=[jax.ShapeDtypeStruc...  199 us
    pallas_call x1, Pallas kernels, gather_weights(): pl.pallas_call(partial(gather_kernel, count), out_shape=[jax.ShapeDtypeSt...  81.6 us
    ppermute x4, waiting for transfers between devices, swap(): return lax.ppermute(value, axis, [(i, i ^ stride) for i in range(count)])  49 us
    dot_general x16, matrix products, cycle_step(): jnp.einsum('kgts,skd->tkgd', score_grad, key_heads, preferred_element_typ...  39.6 us
    convert_element_type x16, other arithmetic, cycle_step(): from_behind(grad_piece.astype(jnp.bfloat16), 'ctx', 1)  33.3 us
    all_gather x1, waiting for transfers between devices, per_device(): value_piece = lax.all_gather(values, 'ctx', axis=0, tiled=True)  32 us
    unnamed x206, local copies, waits for them, and re-layouts  30.8 us
  transfers between devices with their start and end apart: 38, of which 36 were waited for; matrix products, arithmetic and copies ran while one was open for 16% of the time, Pallas kernels for 0%

profile of v2, /device:TPU:0, one launch (start us, length us, event | category | flops | bytes accessed | tf_op | source)
XLA Modules:
  0.0 1073.8 jit_solution(10714560610692490514)
XLA Ops:
  22.3 81.6 %gather_weights.1 = (bf16[1024,2048]{1,0:T(8,128)(2,1)}, bf16[1024,1024]{1,0:T(8,128)(2,1)S(1)}, bf16[1024,1024]{1,0:T(8,128)(2,1)S(1)}, bf16[2048,1024]{1,0:T(8...) custom-call(bf16[512,2048]{1,0:T(8,128)(2,1)S(1)} %copy-done.6, ...), custom_call_target="tpu_custom_call" | custom-call | tf_op jit(solution)/shard_map/gather_weights/pallas_call | solution.py:223
  106.3 3.9 copy.202
  116.5 6.4 copy.205
  123.1 3.5 multiply_reduce_fusion.3
  144.1 22.7 %all-gather.3.cloned.1.call-done = bf16[2048,1024]{0,1:T(8,128)(2,1)} async-done(((bf16[128,1024]{0,1:T(8,128)(2,1)}), bf16[2048,1024]{0,1:T(8,128)(2,1)}) %all-gather.3.cloned.1.call-update) | async-done | bytes 4194320 | tf_op jit(solution)/shard_map/all_gather | solution.py:639
  166.8 10.5 fusion.11
  177.3 9.2 fusion.12
  186.6 32.0 %all-gather.5.cloned.1.call-done = bf16[2048,1024]{1,0:T(8,128)(2,1)} async-done(((bf16[128,1024]{1,0:T(8,128)(2,1)}), bf16[2048,1024]{1,0:T(8,128)(2,1)}) %all-gather.5.cloned.1.call-update) | async-done | bytes 4194320 | tf_op jit(solution)/shard_map/all_gather | solution.py:640
  218.6 6.4 copy.206
  225.1 10.2 fusion.35
  240.9 3.8 multiply_convert_fusion
  252.6 6.2 multiply_reduce_fusion.5
  265.1 432.4 %while.18 = (s32[]{:T(128)}, bf16[2,128,1024]{1,2,0:T(8,128)(2,1)}, f32[2,128,1024]{1,2,0:T(8,128)}, f32[128,8,2,128]{3,0,2,1:T(8,128)}, s32[128]{0:T(128)S(1)},...) while((s32[]{:T(128)}, bf16[2,128,1024]{1,2,0:T(8,128)(2,1)}, ...), condition=%wide.region_12.13_spmd.clone, body=%wide.region_11.12_spmd.clone.sunk | while | flops 339263488 | bytes 26530248 | solution.py:742
  276.9 9.6 collective-permute-done.1
  288.6 3.5 collective-permute-done
  304.4 9.1 collective-permute-done.1
  315.6 3.5 collective-permute-done
  331.5 9.1 collective-permute-done.1
  342.6 3.5 collective-permute-done
  358.5 9.1 collective-permute-done.1
  369.6 3.5 collective-permute-done
  385.5 9.1 collective-permute-done.1
  396.7 3.5 collective-permute-done
  412.5 9.1 collective-permute-done.1
  439.6 9.1 collective-permute-done.1
  466.6 9.1 collective-permute-done.1
  493.6 9.1 collective-permute-done.1
  520.6 9.1 collective-permute-done.1
  547.7 9.1 collective-permute-done.1
  558.8 3.5 collective-permute-done
  574.7 9.1 collective-permute-done.1
  601.7 9.1 collective-permute-done.1
  612.9 3.5 collective-permute-done
  628.7 9.1 collective-permute-done.1
  655.8 9.1 collective-permute-done.1
  666.9 3.5 collective-permute-done
  682.8 9.1 collective-permute-done.1
  747.0 44.3 %collective-permute-done.4 = bf16[128,12,2,512]{0,3,1,2:T(8,128)(2,1)} collective-permute-done((bf16[128,12,2,512]{0,3,1,2:T(8,128)(2,1)}, bf16[128,12,2,512]{0,3,1,2:T(8,128)(2,1)}, u32[]{:S(2)}, u32[]{:S(2)}) %collective-permute-start.4) | collective-permute-done | bytes 3145760 | tf_op jit(solution)/shard_map/ppermute | solution.py:532
  791.3 4.5 fusion.19
  796.4 4.7 collective-permute-done.2
  810.5 4.5 fusion.26
  815.0 6.8 pad_maximum_fusion.1.rows_ref
  824.8 4.8 copy.184
  829.6 5.5 pad_maximum_fusion.cols_ref
  835.1 198.7 %sum_grads.1 = (bf16[15,512,1024]{2,1,0:T(8,128)(2,1)}, f32[80,128]{1,0:T(8,128)S(1)}) custom-call(bf16[512,3584]{1,0:T(8,128)(2,1)S(1)} %copy-done, bf16[512,6144]{1,0:T(8,128)(2,1)} %pad_maximum_fusion.cols_ref, f32[2,80,128]{2,1,0:T(8,128)S(1)} %pad_maximum_fusion.5.small_ref), custom_call_target="tpu_custom_call" | custom-call | tf_op jit(solution)/shard_map/sum_grads/pallas_call | solution.py:489
  1034.4 8.1 slice_bitcast_fusion.2
  1049.2 4.1 bitcast_convert_fusion.1
  1053.3 3.7 bitcast_convert_fusion
  (640 shorter events, 397.4 us)
Async XLA Ops:
  7.2 159.6 %all-gather.3.cloned.1.call-start = ((), (), s32[]{:S(2)}) async-start(), calls=%async_computation | async-start | bytes 4456448 | tf_op jit(solution)/shard_map/all_gather | solution.py:639
  22.3 83.6 %copy-start.21 = (bf16[1,128,1024]{2,1,0:T(8,128)(2,1)S(1)}, bf16[1,128,1024]{2,1,0:T(8,128)(2,1)}, u32[]{:S(2)}) copy-start(bf16[1,128,1024]{2,1,0:T(8,128)(2,1)} %param.18) | copy-start | bytes 786436
  22.3 83.8 %copy-start.89 = (s32[1,2]{1,0:T(1,128)S(1)}, s32[1,2]{1,0:T(1,128)}, u32[]{:S(2)}) copy-start(s32[1,2]{1,0:T(1,128)} %param.21) | copy-start | bytes 28
  114.1 104.5 %all-gather.5.cloned.1.call-start = ((), (), s32[]{:S(2)}) async-start(), calls=%async_computation.1 | async-start | bytes 4456448 | tf_op jit(solution)/shard_map/all_gather | solution.py:640
  141.1 36.3 %copy-start.71 = (s32[128]{0:T(128)}, s32[128]{0:T(128)S(1)}, u32[]{:S(2)}) copy-start(s32[128]{0:T(128)S(1)} %fusion.66) | copy-start | bytes 1540
  236.2 22.6 %copy-start.14 = (f32[128,1024]{1,0:T(8,128)}, f32[128,1024]{1,0:T(8,128)S(1)}, u32[]{:S(2)}) copy-start(f32[128,1024]{1,0:T(8,128)S(1)} %get-tuple-element.501) | copy-start | bytes 1572868
  265.0 435.5 %copy-start.81 = (f32[128]{0:T(128)S(1)}, f32[128]{0:T(128)}, u32[]{:S(2)}) copy-start(f32[128]{0:T(128)} %copy-done.80) | copy-start | bytes 1540
  274.9 11.6 %collective-permute-start.1 = (bf16[2,128,1024]{1,2,0:T(8,128)(2,1)}, bf16[2,128,1024]{1,2,0:T(8,128)(2,1)}, u32[]{:S(2)}, u32[]{:S(2)}) collective-permute-start(bf16[2,128,1024]{1,2,0:T(8,128)(2,1)} %fusion.160), channel_id=1, source_target_pairs={{0,2},{2,4},{4,6},{6,8},{8,10},{10,12},{12,14},{14,16},{16,18},{18... | collective-permute-start | bytes 1572872 | tf_op jit(solution)/shard_map/while/body/eval_jaxpr/ppermute | solution.py:23
  275.1 17.0 %collective-permute-start = (bf16[2,128,1024]{1,2,0:T(8,128)(2,1)}, bf16[2,128,1024]{1,2,0:T(8,128)(2,1)}, u32[]{:S(2)}, u32[]{:S(2)}) collective-permute-start(bf16[2,128,1024]{1,2,0:T(8,128)(2,1)} %copy.242), channel_id=1, source_target_pairs={{0,2},{2,4},{4,6},{6,8},{8,10},{10,12},{12,14},{14,16},{16,18},{18... | collective-permute-start | bytes 1572872 | tf_op jit(solution)/shard_map/while/body/eval_jaxpr/ppermute | solution.py:23
  301.9 11.6 %collective-permute-start.1 = (bf16[2,128,1024]{1,2,0:T(8,128)(2,1)}, bf16[2,128,1024]{1,2,0:T(8,128)(2,1)}, u32[]{:S(2)}, u32[]{:S(2)}) collective-permute-start(bf16[2,128,1024]{1,2,0:T(8,128)(2,1)} %fusion.160), channel_id=1, source_target_pairs={{0,2},{2,4},{4,6},{6,8},{8,10},{10,12},{12,14},{14,16},{16,18},{18... | collective-permute-start | bytes 1572872 | tf_op jit(solution)/shard_map/while/body/eval_jaxpr/ppermute | solution.py:23
  301.9 17.2 %collective-permute-start = (bf16[2,128,1024]{1,2,0:T(8,128)(2,1)}, bf16[2,128,1024]{1,2,0:T(8,128)(2,1)}, u32[]{:S(2)}, u32[]{:S(2)}) collective-permute-start(bf16[2,128,1024]{1,2,0:T(8,128)(2,1)} %copy.242), channel_id=1, source_target_pairs={{0,2},{2,4},{4,6},{6,8},{8,10},{10,12},{12,14},{14,16},{16,18},{18... | collective-permute-start | bytes 1572872 | tf_op jit(solution)/shard_map/while/body/eval_jaxpr/ppermute | solution.py:23
  328.9 11.6 %collective-permute-start.1 = (bf16[2,128,1024]{1,2,0:T(8,128)(2,1)}, bf16[2,128,1024]{1,2,0:T(8,128)(2,1)}, u32[]{:S(2)}, u32[]{:S(2)}) collective-permute-start(bf16[2,128,1024]{1,2,0:T(8,128)(2,1)} %fusion.160), channel_id=1, source_target_pairs={{0,2},{2,4},{4,6},{6,8},{8,10},{10,12},{12,14},{14,16},{16,18},{18... | collective-permute-start | bytes 1572872 | tf_op jit(solution)/shard_map/while/body/eval_jaxpr/ppermute | solution.py:23
  328.9 17.2 %collective-permute-start = (bf16[2,128,1024]{1,2,0:T(8,128)(2,1)}, bf16[2,128,1024]{1,2,0:T(8,128)(2,1)}, u32[]{:S(2)}, u32[]{:S(2)}) collective-permute-start(bf16[2,128,1024]{1,2,0:T(8,128)(2,1)} %copy.242), channel_id=1, source_target_pairs={{0,2},{2,4},{4,6},{6,8},{8,10},{10,12},{12,14},{14,16},{16,18},{18... | collective-permute-start | bytes 1572872 | tf_op jit(solution)/shard_map/while/body/eval_jaxpr/ppermute | solution.py:23
  355.9 11.6 %collective-permute-start.1 = (bf16[2,128,1024]{1,2,0:T(8,128)(2,1)}, bf16[2,128,1024]{1,2,0:T(8,128)(2,1)}, u32[]{:S(2)}, u32[]{:S(2)}) collective-permute-start(bf16[2,128,1024]{1,2,0:T(8,128)(2,1)} %fusion.160), channel_id=1, source_target_pairs={{0,2},{2,4},{4,6},{6,8},{8,10},{10,12},{12,14},{14,16},{16,18},{18... | collective-permute-start | bytes 1572872 | tf_op jit(solution)/shard_map/while/body/eval_jaxpr/ppermute | solution.py:23
  355.9 17.2 %collective-permute-start = (bf16[2,128,1024]{1,2,0:T(8,128)(2,1)}, bf16[2,128,1024]{1,2,0:T(8,128)(2,1)}, u32[]{:S(2)}, u32[]{:S(2)}) collective-permute-start(bf16[2,128,1024]{1,2,0:T(8,128)(2,1)} %copy.242), channel_id=1, source_target_pairs={{0,2},{2,4},{4,6},{6,8},{8,10},{10,12},{12,14},{14,16},{16,18},{18... | collective-permute-start | bytes 1572872 | tf_op jit(solution)/shard_map/while/body/eval_jaxpr/ppermute | solution.py:23
  383.0 11.6 %collective-permute-start.1 = (bf16[2,128,1024]{1,2,0:T(8,128)(2,1)}, bf16[2,128,1024]{1,2,0:T(8,128)(2,1)}, u32[]{:S(2)}, u32[]{:S(2)}) collective-permute-start(bf16[2,128,1024]{1,2,0:T(8,128)(2,1)} %fusion.160), channel_id=1, source_target_pairs={{0,2},{2,4},{4,6},{6,8},{8,10},{10,12},{12,14},{14,16},{16,18},{18... | collective-permute-start | bytes 1572872 | tf_op jit(solution)/shard_map/while/body/eval_jaxpr/ppermute | solution.py:23
  383.0 17.2 %collective-permute-start = (bf16[2,128,1024]{1,2,0:T(8,128)(2,1)}, bf16[2,128,1024]{1,2,0:T(8,128)(2,1)}, u32[]{:S(2)}, u32[]{:S(2)}) collective-permute-start(bf16[2,128,1024]{1,2,0:T(8,128)(2,1)} %copy.242), channel_id=1, source_target_pairs={{0,2},{2,4},{4,6},{6,8},{8,10},{10,12},{12,14},{14,16},{16,18},{18... | collective-permute-start | bytes 1572872 | tf_op jit(solution)/shard_map/while/body/eval_jaxpr/ppermute | solution.py:23
  410.0 11.6 %collective-permute-start.1 = (bf16[2,128,1024]{1,2,0:T(8,128)(2,1)}, bf16[2,128,1024]{1,2,0:T(8,128)(2,1)}, u32[]{:S(2)}, u32[]{:S(2)}) collective-permute-start(bf16[2,128,1024]{1,2,0:T(8,128)(2,1)} %fusion.160), channel_id=1, source_target_pairs={{0,2},{2,4},{4,6},{6,8},{8,10},{10,12},{12,14},{14,16},{16,18},{18... | collective-permute-start | bytes 1572872 | tf_op jit(solution)/shard_map/while/body/eval_jaxpr/ppermute | solution.py:23
  410.0 17.2 %collective-permute-start = (bf16[2,128,1024]{1,2,0:T(8,128)(2,1)}, bf16[2,128,1024]{1,2,0:T(8,128)(2,1)}, u32[]{:S(2)}, u32[]{:S(2)}) collective-permute-start(bf16[2,128,1024]{1,2,0:T(8,128)(2,1)} %copy.242), channel_id=1, source_target_pairs={{0,2},{2,4},{4,6},{6,8},{8,10},{10,12},{12,14},{14,16},{16,18},{18... | collective-permute-start | bytes 1572872 | tf_op jit(solution)/shard_map/while/body/eval_jaxpr/ppermute | solution.py:23
  437.0 11.6 %collective-permute-start.1 = (bf16[2,128,1024]{1,2,0:T(8,128)(2,1)}, bf16[2,128,1024]{1,2,0:T(8,128)(2,1)}, u32[]{:S(2)}, u32[]{:S(2)}) collective-permute-start(bf16[2,128,1024]{1,2,0:T(8,128)(2,1)} %fusion.160), channel_id=1, source_target_pairs={{0,2},{2,4},{4,6},{6,8},{8,10},{10,12},{12,14},{14,16},{16,18},{18... | collective-permute-start | bytes 1572872 | tf_op jit(solution)/shard_map/while/body/eval_jaxpr/ppermute | solution.py:23
  437.0 17.2 %collective-permute-start = (bf16[2,128,1024]{1,2,0:T(8,128)(2,1)}, bf16[2,128,1024]{1,2,0:T(8,128)(2,1)}, u32[]{:S(2)}, u32[]{:S(2)}) collective-permute-start(bf16[2,128,1024]{1,2,0:T(8,128)(2,1)} %copy.242), channel_id=1, source_target_pairs={{0,2},{2,4},{4,6},{6,8},{8,10},{10,12},{12,14},{14,16},{16,18},{18... | collective-permute-start | bytes 1572872 | tf_op jit(solution)/shard_map/while/body/eval_jaxpr/ppermute | solution.py:23
  464.0 11.6 %collective-permute-start.1 = (bf16[2,128,1024]{1,2,0:T(8,128)(2,1)}, bf16[2,128,1024]{1,2,0:T(8,128)(2,1)}, u32[]{:S(2)}, u32[]{:S(2)}) collective-permute-start(bf16[2,128,1024]{1,2,0:T(8,128)(2,1)} %fusion.160), channel_id=1, source_target_pairs={{0,2},{2,4},{4,6},{6,8},{8,10},{10,12},{12,14},{14,16},{16,18},{18... | collective-permute-start | bytes 1572872 | tf_op jit(solution)/shard_map/while/body/eval_jaxpr/ppermute | solution.py:23
  464.0 17.2 %collective-permute-start = (bf16[2,128,1024]{1,2,0:T(8,128)(2,1)}, bf16[2,128,1024]{1,2,0:T(8,128)(2,1)}, u32[]{:S(2)}, u32[]{:S(2)}) collective-permute-start(bf16[2,128,1024]{1,2,0:T(8,128)(2,1)} %copy.242), channel_id=1, source_target_pairs={{0,2},{2,4},{4,6},{6,8},{8,10},{10,12},{12,14},{14,16},{16,18},{18... | collective-permute-start | bytes 1572872 | tf_op jit(solution)/shard_map/while/body/eval_jaxpr/ppermute | solution.py:23
  491.1 11.6 %collective-permute-start.1 = (bf16[2,128,1024]{1,2,0:T(8,128)(2,1)}, bf16[2,128,1024]{1,2,0:T(8,128)(2,1)}, u32[]{:S(2)}, u32[]{:S(2)}) collective-permute-start(bf16[2,128,1024]{1,2,0:T(8,128)(2,1)} %fusion.160), channel_id=1, source_target_pairs={{0,2},{2,4},{4,6},{6,8},{8,10},{10,12},{12,14},{14,16},{16,18},{18... | collective-permute-start | bytes 1572872 | tf_op jit(solution)/shard_map/while/body/eval_jaxpr/ppermute | solution.py:23
  491.1 17.2 %collective-permute-start = (bf16[2,128,1024]{1,2,0:T(8,128)(2,1)}, bf16[2,128,1024]{1,2,0:T(8,128)(2,1)}, u32[]{:S(2)}, u32[]{:S(2)}) collective-permute-start(bf16[2,128,1024]{1,2,0:T(8,128)(2,1)} %copy.242), channel_id=1, source_target_pairs={{0,2},{2,4},{4,6},{6,8},{8,10},{10,12},{12,14},{14,16},{16,18},{18... | collective-permute-start | bytes 1572872 | tf_op jit(solution)/shard_map/while/body/eval_jaxpr/ppermute | solution.py:23
  518.1 11.6 %collective-permute-start.1 = (bf16[2,128,1024]{1,2,0:T(8,128)(2,1)}, bf16[2,128,1024]{1,2,0:T(8,128)(2,1)}, u32[]{:S(2)}, u32[]{:S(2)}) collective-permute-start(bf16[2,128,1024]{1,2,0:T(8,128)(2,1)} %fusion.160), channel_id=1, source_target_pairs={{0,2},{2,4},{4,6},{6,8},{8,10},{10,12},{12,14},{14,16},{16,18},{18... | collective-permute-start | bytes 1572872 | tf_op jit(solution)/shard_map/while/body/eval_jaxpr/ppermute | solution.py:23
  518.1 17.2 %collective-permute-start = (bf16[2,128,1024]{1,2,0:T(8,128)(2,1)}, bf16[2,128,1024]{1,2,0:T(8,128)(2,1)}, u32[]{:S(2)}, u32[]{:S(2)}) collective-permute-start(bf16[2,128,1024]{1,2,0:T(8,128)(2,1)} %copy.242), channel_id=1, source_target_pairs={{0,2},{2,4},{4,6},{6,8},{8,10},{10,12},{12,14},{14,16},{16,18},{18... | collective-permute-start | bytes 1572872 | tf_op jit(solution)/shard_map/while/body/eval_jaxpr/ppermute | solution.py:23
  545.1 11.6 %collective-permute-start.1 = (bf16[2,128,1024]{1,2,0:T(8,128)(2,1)}, bf16[2,128,1024]{1,2,0:T(8,128)(2,1)}, u32[]{:S(2)}, u32[]{:S(2)}) collective-permute-start(bf16[2,128,1024]{1,2,0:T(8,128)(2,1)} %fusion.160), channel_id=1, source_target_pairs={{0,2},{2,4},{4,6},{6,8},{8,10},{10,12},{12,14},{14,16},{16,18},{18... | collective-permute-start | bytes 1572872 | tf_op jit(solution)/shard_map/while/body/eval_jaxpr/ppermute | solution.py:23
  545.1 17.2 %collective-permute-start = (bf16[2,128,1024]{1,2,0:T(8,128)(2,1)}, bf16[2,128,1024]{1,2,0:T(8,128)(2,1)}, u32[]{:S(2)}, u32[]{:S(2)}) collective-permute-start(bf16[2,128,1024]{1,2,0:T(8,128)(2,1)} %copy.242), channel_id=1, source_target_pairs={{0,2},{2,4},{4,6},{6,8},{8,10},{10,12},{12,14},{14,16},{16,18},{18... | collective-permute-start | bytes 1572872 | tf_op jit(solution)/shard_map/while/body/eval_jaxpr/ppermute | solution.py:23
  572.1 11.6 %collective-permute-start.1 = (bf16[2,128,1024]{1,2,0:T(8,128)(2,1)}, bf16[2,128,1024]{1,2,0:T(8,128)(2,1)}, u32[]{:S(2)}, u32[]{:S(2)}) collective-permute-start(bf16[2,128,1024]{1,2,0:T(8,128)(2,1)} %fusion.160), channel_id=1, source_target_pairs={{0,2},{2,4},{4,6},{6,8},{8,10},{10,12},{12,14},{14,16},{16,18},{18... | collective-permute-start | bytes 1572872 | tf_op jit(solution)/shard_map/while/body/eval_jaxpr/ppermute | solution.py:23
  572.1 17.2 %collective-permute-start = (bf16[2,128,1024]{1,2,0:T(8,128)(2,1)}, bf16[2,128,1024]{1,2,0:T(8,128)(2,1)}, u32[]{:S(2)}, u32[]{:S(2)}) collective-permute-start(bf16[2,128,1024]{1,2,0:T(8,128)(2,1)} %copy.242), channel_id=1, source_target_pairs={{0,2},{2,4},{4,6},{6,8},{8,10},{10,12},{12,14},{14,16},{16,18},{18... | collective-permute-start | bytes 1572872 | tf_op jit(solution)/shard_map/while/body/eval_jaxpr/ppermute | solution.py:23
  599.2 11.6 %collective-permute-start.1 = (bf16[2,128,1024]{1,2,0:T(8,128)(2,1)}, bf16[2,128,1024]{1,2,0:T(8,128)(2,1)}, u32[]{:S(2)}, u32[]{:S(2)}) collective-permute-start(bf16[2,128,1024]{1,2,0:T(8,128)(2,1)} %fusion.160), channel_id=1, source_target_pairs={{0,2},{2,4},{4,6},{6,8},{8,10},{10,12},{12,14},{14,16},{16,18},{18... | collective-permute-start | bytes 1572872 | tf_op jit(solution)/shard_map/while/body/eval_jaxpr/ppermute | solution.py:23
  599.2 17.2 %collective-permute-start = (bf16[2,128,1024]{1,2,0:T(8,128)(2,1)}, bf16[2,128,1024]{1,2,0:T(8,128)(2,1)}, u32[]{:S(2)}, u32[]{:S(2)}) collective-permute-start(bf16[2,128,1024]{1,2,0:T(8,128)(2,1)} %copy.242), channel_id=1, source_target_pairs={{0,2},{2,4},{4,6},{6,8},{8,10},{10,12},{12,14},{14,16},{16,18},{18... | collective-permute-start | bytes 1572872 | tf_op jit(solution)/shard_map/while/body/eval_jaxpr/ppermute | solution.py:23
  626.2 11.6 %collective-permute-start.1 = (bf16[2,128,1024]{1,2,0:T(8,128)(2,1)}, bf16[2,128,1024]{1,2,0:T(8,128)(2,1)}, u32[]{:S(2)}, u32[]{:S(2)}) collective-permute-start(bf16[2,128,1024]{1,2,0:T(8,128)(2,1)} %fusion.160), channel_id=1, source_target_pairs={{0,2},{2,4},{4,6},{6,8},{8,10},{10,12},{12,14},{14,16},{16,18},{18... | collective-permute-start | bytes 1572872 | tf_op jit(solution)/shard_map/while/body/eval_jaxpr/ppermute | solution.py:23
  626.2 17.2 %collective-permute-start = (bf16[2,128,1024]{1,2,0:T(8,128)(2,1)}, bf16[2,128,1024]{1,2,0:T(8,128)(2,1)}, u32[]{:S(2)}, u32[]{:S(2)}) collective-permute-start(bf16[2,128,1024]{1,2,0:T(8,128)(2,1)} %copy.242), channel_id=1, source_target_pairs={{0,2},{2,4},{4,6},{6,8},{8,10},{10,12},{12,14},{14,16},{16,18},{18... | collective-permute-start | bytes 1572872 | tf_op jit(solution)/shard_map/while/body/eval_jaxpr/ppermute | solution.py:23
  653.2 11.6 %collective-permute-start.1 = (bf16[2,128,1024]{1,2,0:T(8,128)(2,1)}, bf16[2,128,1024]{1,2,0:T(8,128)(2,1)}, u32[]{:S(2)}, u32[]{:S(2)}) collective-permute-start(bf16[2,128,1024]{1,2,0:T(8,128)(2,1)} %fusion.160), channel_id=1, source_target_pairs={{0,2},{2,4},{4,6},{6,8},{8,10},{10,12},{12,14},{14,16},{16,18},{18... | collective-permute-start | bytes 1572872 | tf_op jit(solution)/shard_map/while/body/eval_jaxpr/ppermute | solution.py:23
  653.2 17.2 %collective-permute-start = (bf16[2,128,1024]{1,2,0:T(8,128)(2,1)}, bf16[2,128,1024]{1,2,0:T(8,128)(2,1)}, u32[]{:S(2)}, u32[]{:S(2)}) collective-permute-start(bf16[2,128,1024]{1,2,0:T(8,128)(2,1)} %copy.242), channel_id=1, source_target_pairs={{0,2},{2,4},{4,6},{6,8},{8,10},{10,12},{12,14},{14,16},{16,18},{18... | collective-permute-start | bytes 1572872 | tf_op jit(solution)/shard_map/while/body/eval_jaxpr/ppermute | solution.py:23
  680.2 11.6 %collective-permute-start.1 = (bf16[2,128,1024]{1,2,0:T(8,128)(2,1)}, bf16[2,128,1024]{1,2,0:T(8,128)(2,1)}, u32[]{:S(2)}, u32[]{:S(2)}) collective-permute-start(bf16[2,128,1024]{1,2,0:T(8,128)(2,1)} %fusion.160), channel_id=1, source_target_pairs={{0,2},{2,4},{4,6},{6,8},{8,10},{10,12},{12,14},{14,16},{16,18},{18... | collective-permute-start | bytes 1572872 | tf_op jit(solution)/shard_map/while/body/eval_jaxpr/ppermute | solution.py:23
  680.2 17.2 %collective-permute-start = (bf16[2,128,1024]{1,2,0:T(8,128)(2,1)}, bf16[2,128,1024]{1,2,0:T(8,128)(2,1)}, u32[]{:S(2)}, u32[]{:S(2)}) collective-permute-start(bf16[2,128,1024]{1,2,0:T(8,128)(2,1)} %copy.242), channel_id=1, source_target_pairs={{0,2},{2,4},{4,6},{6,8},{8,10},{10,12},{12,14},{14,16},{16,18},{18... | collective-permute-start | bytes 1572872 | tf_op jit(solution)/shard_map/while/body/eval_jaxpr/ppermute | solution.py:23
  724.0 67.3 %collective-permute-start.4 = (bf16[128,12,2,512]{0,3,1,2:T(8,128)(2,1)}, bf16[128,12,2,512]{0,3,1,2:T(8,128)(2,1)}, u32[]{:S(2)}, u32[]{:S(2)}) collective-permute-start(bf16[128,12,2,512]{0,3,1,2:T(8,128)(2,1)} %constant_dynamic-update-slice_fusion), channel_id=1, source_target_pairs={{0,1},{1,0},{2,3},{3,2},{4,5},{5,4},{6,7},{7,6},{8,9},{9,8},{10,11... | collective-permute-start | bytes 9437192 | tf_op jit(solution)/shard_map/ppermute | solution.py:532
  741.4 59.7 %collective-permute-start.2 = (bf16[128,3584]{1,0:T(8,128)(2,1)}, bf16[128,3584]{1,0:T(8,128)(2,1)}, u32[]{:S(2)}, u32[]{:S(2)}) collective-permute-start(bf16[128,3584]{1,0:T(8,128)(2,1)} %pad_maximum_fusion.3), channel_id=1, source_target_pairs={{0,1},{1,0},{2,3},{3,2},{4,5},{5,4},{6,7},{7,6},{8,9},{9,8},{10,11... | collective-permute-start | bytes 2752520 | tf_op jit(solution)/shard_map/ppermute | solution.py:532
  743.7 47.5 %copy-start.43 = (bf16[128,12,2,512]{0,3,1,2:T(8,128)(2,1)S(1)}, bf16[128,12,2,512]{0,3,1,2:T(8,128)(2,1)}, u32[]{:S(2)}) copy-start(bf16[128,12,2,512]{0,3,1,2:T(8,128)(2,1)} %constant_dynamic-update-slice_fusion) | copy-start | bytes 9437188
  747.0 49.1 %copy-start.56 = (bf16[128,1,1024]{0,2,1:T(8,128)(2,1)S(1)}, bf16[128,1,1024]{0,2,1:T(8,128)(2,1)}, u32[]{:S(2)}) copy-start(bf16[128,1,1024]{0,2,1:T(8,128)(2,1)} %get-tuple-element.466) | copy-start | bytes 786436
  747.0 49.3 %copy-start.57 = (bf16[128,1,512]{2,1,0:T(2,128)(2,1)S(1)}, bf16[128,1,512]{2,1,0:T(2,128)(2,1)}, u32[]{:S(2)}) copy-start(bf16[128,1,512]{2,1,0:T(2,128)(2,1)} %get-tuple-element.468) | copy-start | bytes 393220
  747.0 49.3 %copy-start.45 = (bf16[128,1,1536]{2,1,0:T(2,128)(2,1)S(1)}, bf16[128,1,1536]{2,1,0:T(2,128)(2,1)}, u32[]{:S(2)}) copy-start(bf16[128,1,1536]{2,1,0:T(2,128)(2,1)} %get-tuple-element.460) | copy-start | bytes 1179652
  747.0 54.1 %copy-start.54 = (bf16[128,512]{1,0:T(8,128)(2,1)S(1)}, bf16[128,512]{1,0:T(8,128)(2,1)}, u32[]{:S(2)}) copy-start(bf16[128,512]{1,0:T(8,128)(2,1)} %get-tuple-element.470) | copy-start | bytes 393220
  795.7 29.1 %collective-permute-start.5 = (bf16[256,12,512]{0,2,1:T(8,128)(2,1)}, bf16[256,12,512]{0,2,1:T(8,128)(2,1)}, u32[]{:S(2)}, u32[]{:S(2)}) collective-permute-start(bf16[256,12,512]{0,2,1:T(8,128)(2,1)} %get-tuple-element.452), channel_id=1, source_target_pairs={{0,2},{2,0},{4,6},{6,4},{8,10},{10,8},{12,14},{14,12},{16,18},{18,... | collective-permute-start | bytes 9437192 | tf_op jit(solution)/shard_map/ppermute | solution.py:532
  803.7 11.3 %collective-permute-start.3 = (bf16[256,3584]{1,0:T(8,128)(2,1)}, bf16[256,3584]{1,0:T(8,128)(2,1)}, u32[]{:S(2)}, u32[]{:S(2)}) collective-permute-start(bf16[256,3584]{1,0:T(8,128)(2,1)} %pad_maximum_fusion.2), channel_id=1, source_target_pairs={{0,2},{2,0},{4,6},{6,4},{8,10},{10,8},{12,14},{14,12},{16,18},{18,... | collective-permute-start | bytes 5505032 | tf_op jit(solution)/shard_map/ppermute | solution.py:532
  (117 other events, 640.5 us)
Sparse Core Ops, SparseCore 0:
  114.3 52.5 all-gather.2
  169.5 49.0 all-gather.4

commit v3 on v2

--- a/solution.py
+++ b/solution.py
@@ -527,6 +527,374 @@
     )(rows, columns, small)
 
 
+def attend_kernel(
+    depth,
+    q_ref,
+    kv_ref,
+    q_pos,
+    q_begin,
+    k_pos,
+    out_ref,
+    log_ref,
+    kv_all,
+    stacked,
+    summed,
+    sums,
+    bias,
+    send_z,
+    recv_z,
+    send_x,
+    recv_x,
+    send_core,
+    recv_core,
+):
+    index = lax.axis_index("ctx")
+    group = lax.axis_index("fsdp")
+    z, x, core = place_of(index)
+    count = q_ref.shape[0]
+    wide = 4 * count
+    heads = q_ref.shape[1] // HEAD_DIM // 2
+
+    def device(at_z, at_x, at_core):
+        return ((at_z * 2 + at_x) * 2 + at_core, group)
+
+    across = device(z, 1 - x, core)
+    beside = device(z, x, 1 - core)
+    ahead = [lax.rem(z + offset, depth) for offset in range(depth)]
+    behind = [lax.rem(z + depth - offset, depth) for offset in range(depth)]
+    greet([device(ahead[offset], x, core) for offset in range(1, depth)] + [across, beside])
+
+    def rows(at_z, at_x, at_core):
+        first = ((at_z * 2 + at_x) * 2 + at_core) * count
+        return kv_all.at[pl.ds(pl.multiple_of(first, count), count)]
+
+    def z_copy(offset, at_z):
+        return remote(
+            device(ahead[offset], x, core),
+            kv_ref,
+            rows(at_z, x, core),
+            send_z.at[offset - 1],
+            recv_z.at[offset - 1],
+        )
+
+    def x_copy(offset, at_x):
+        part = rows(behind[offset], at_x, core)
+        return remote(across, part, part, send_x.at[offset], recv_x.at[offset])
+
+    def core_copy(offset, which, at_core):
+        part = rows(behind[offset], x + which - 2 * x * which, at_core)
+        return remote(
+            beside, part, part, send_core.at[offset, which], recv_core.at[offset, which]
+        )
+
+    for offset in range(1, depth):
+        z_copy(offset, z).start()
+    rows(z, x, core)[...] = kv_ref[...]
+    for head in range(heads):
+        for turn in range(2):
+            at = (2 * head + turn) * HEAD_DIM
+            stacked[head, turn * count : (turn + 1) * count] = q_ref[:, at : at + HEAD_DIM]
+    summed[...] = jnp.zeros_like(summed)
+    sums[...] = jnp.zeros_like(sums)
+
+    def stage_far(offset):
+        if offset:
+            z_copy(offset, behind[offset]).wait_recv()
+        x_copy(offset, x).start()
+        core_copy(offset, 0, core).start()
+
+    def stage_across(offset):
+        x_copy(offset, 1 - x).wait_recv()
+        core_copy(offset, 1, core).start()
+
+    def stage_attend(offset):
+        core_copy(offset, 0, 1 - core).wait_recv()
+        core_copy(offset, 1, 1 - core).wait_recv()
+        first = pl.multiple_of(behind[offset] * wide, wide)
+        place = k_pos[:, pl.ds(first, wide)]
+        allowed = (place >= q_begin[...]) & (place <= q_pos[...])
+        low = jnp.where(allowed, 0.0, NEG)
+        bias[:count] = low
+        bias[count:] = low
+
+        def one(head, carry):
+            at = pl.multiple_of(head * HEAD_DIM, HEAD_DIM)
+            keys = kv_all[pl.ds(first, wide), pl.ds(at, HEAD_DIM)]
+            at_v = pl.multiple_of((heads + head) * HEAD_DIM, HEAD_DIM)
+            values = kv_all[pl.ds(first, wide), pl.ds(at_v, HEAD_DIM)]
+            scores = lax.dot_general(
+                stacked[head], keys, (((1,), (1,)), ((), ())), preferred_element_type=jnp.float32
+            )
+            weights = jnp.exp(scores + bias[...])
+            part = weights[:, :HEAD_DIM]
+            for at_k in range(HEAD_DIM, wide, HEAD_DIM):
+                part = part + weights[:, at_k : at_k + HEAD_DIM]
+            sums[head] = sums[head] + part
+            summed[head] = summed[head] + jnp.dot(
+                weights.astype(jnp.bfloat16), values, preferred_element_type=jnp.float32
+            )
+            return carry
+
+        lax.fori_loop(0, heads, one, 0)
+
+    stages = (stage_far, stage_across, stage_attend)
+    for step in range(depth + len(stages) - 1):
+        for late, stage in enumerate(stages):
+            if 0 <= step - late < depth:
+                stage(step - late)
+    for head in range(heads):
+        total = jnp.sum(sums[head], axis=1, keepdims=True)
+        result = summed[head] / total
+        for turn in range(2):
+            at = (2 * head + turn) * HEAD_DIM
+            out_ref[:, at : at + HEAD_DIM] = result[turn * count : (turn + 1) * count]
+        across_rows = jnp.sum(sums[head].T, axis=0, keepdims=True)
+        log_ref[head : head + 1, :] = jnp.log(across_rows)
+    for offset in range(depth):
+        if offset:
+            z_copy(offset, z).wait_send()
+        x_copy(offset, x).wait_send()
+        core_copy(offset, 0, core).wait_send()
+        core_copy(offset, 1, core).wait_send()
+
+
+def attend(queries, key_values, q_pos, q_begin, k_pos):
+    depth = lax.axis_size("ctx") // 4
+    count = queries.shape[0]
+    heads = queries.shape[1] // HEAD_DIM // 2
+    dma = pltpu.SemaphoreType.DMA
+    vmem = pl.BlockSpec(memory_space=pltpu.VMEM)
+    return pl.pallas_call(
+        partial(attend_kernel, depth),
+        out_shape=[
+            jax.ShapeDtypeStruct(queries.shape, jnp.float32),
+            jax.ShapeDtypeStruct((heads, 2 * count), jnp.float32),
+            jax.ShapeDtypeStruct((4 * depth * count, key_values.shape[1]), jnp.bfloat16),
+        ],
+        in_specs=[vmem] * 5,
+        out_specs=[vmem] * 3,
+        scratch_shapes=[
+            pltpu.VMEM((heads, 2 * count, HEAD_DIM), jnp.bfloat16),
+            pltpu.VMEM((heads, 2 * count, HEAD_DIM), jnp.float32),
+            pltpu.VMEM((heads, 2 * count, HEAD_DIM), jnp.float32),
+            pltpu.VMEM((2 * count, 4 * count), jnp.float32),
+            dma((depth - 1,)),
+            dma((depth - 1,)),
+            dma((depth,)),
+            dma((depth,)),
+            dma((depth, 2)),
+            dma((depth, 2)),
+        ],
+        compiler_params=pltpu.CompilerParams(
+            collective_id=3, has_side_effects=True, vmem_limit_bytes=40 * 2**20
+        ),
+        name="attend",
+    )(queries, key_values, q_pos, q_begin, k_pos)
+
+
+def attend_back_kernel(
+    depth,
+    q_ref,
+    grad_ref,
+    out_ref,
+    log_ref,
+    kv_all,
+    q_pos,
+    q_begin,
+    k_pos,
+    q_grad,
+    kv_grad,
+    stacked,
+    grads,
+    delta,
+    summed,
+    bias,
+    part,
+    in_core,
+    kept,
+    out_x,
+    in_x,
+    out_z,
+    in_z,
+    send_core,
+    recv_core,
+    send_x,
+    recv_x,
+    send_z,
+    recv_z,
+):
+    index = lax.axis_index("ctx")
+    group = lax.axis_index("fsdp")
+    z, x, core = place_of(index)
+    count = q_ref.shape[0]
+    wide = 4 * count
+    heads = q_ref.shape[1] // HEAD_DIM // 2
+
+    def device(at_z, at_x, at_core):
+        return ((at_z * 2 + at_x) * 2 + at_core, group)
+
+    across = device(z, 1 - x, core)
+    beside = device(z, x, 1 - core)
+    ahead = [lax.rem(z + offset, depth) for offset in range(depth)]
+    greet([device(ahead[offset], x, core) for offset in range(1, depth)] + [across, beside])
+
+    def core_copy(offset):
+        return remote(
+            beside,
+            part.at[offset, 1 - core],
+            in_core.at[offset],
+            send_core.at[offset],
+            recv_core.at[offset],
+        )
+
+    def x_copy(offset):
+        return remote(
+            across, out_x.at[offset], in_x.at[offset], send_x.at[offset], recv_x.at[offset]
+        )
+
+    def z_copy(offset):
+        return remote(
+            device(ahead[offset], x, core),
+            out_z.at[offset],
+            in_z.at[offset - 1],
+            send_z.at[offset - 1],
+            recv_z.at[offset - 1],
+        )
+
+    for head in range(heads):
+        for turn in range(2):
+            at = (2 * head + turn) * HEAD_DIM
+            inside = slice(turn * count, (turn + 1) * count)
+            stacked[head, inside] = q_ref[:, at : at + HEAD_DIM]
+            grads[head, inside] = grad_ref[:, at : at + HEAD_DIM]
+            product = grad_ref[:, at : at + HEAD_DIM].astype(jnp.float32) * out_ref[
+                :, at : at + HEAD_DIM
+            ]
+            delta[head : head + 1, inside] = jnp.sum(product.T, axis=0, keepdims=True)
+    summed[...] = jnp.zeros_like(summed)
+
+    def stage_pairs(offset):
+        first = pl.multiple_of(ahead[offset] * wide, wide)
+        place = k_pos[pl.ds(first, wide), :]
+        allowed = (place >= q_begin[...]) & (place <= q_pos[...])
+        bias[...] = jnp.where(allowed, 0.0, NEG)
+
+        def one(head, carry):
+            at = pl.multiple_of(head * HEAD_DIM, HEAD_DIM)
+            at_v = pl.multiple_of((heads + head) * HEAD_DIM, HEAD_DIM)
+            keys = kv_all[pl.ds(first, wide), pl.ds(at, HEAD_DIM)]
+            values = kv_all[pl.ds(first, wide), pl.ds(at_v, HEAD_DIM)]
+            scores = lax.dot_general(
+                keys, stacked[head], (((1,), (1,)), ((), ())), preferred_element_type=jnp.float32
+            )
+            weights = jnp.exp(scores + bias[...] - log_ref[pl.ds(head, 1), :])
+            weight_grad = lax.dot_general(
+                values, grads[head], (((1,), (1,)), ((), ())), preferred_element_type=jnp.float32
+            )
+            score_grad = (weights * (weight_grad - delta[pl.ds(head, 1), :])).astype(jnp.bfloat16)
+            key_term = jnp.dot(
+                score_grad, stacked[head], preferred_element_type=jnp.float32
+            ).astype(jnp.bfloat16)
+            value_term = jnp.dot(
+                weights.astype(jnp.bfloat16), grads[head], preferred_element_type=jnp.float32
+            ).astype(jnp.bfloat16)
+            for at_x in range(2):
+                for at_core in range(2):
+                    inside = slice((at_x * 2 + at_core) * count, (at_x * 2 + at_core + 1) * count)
+                    part[offset, at_core, at_x, :, pl.ds(at, HEAD_DIM)] = key_term[inside]
+                    part[offset, at_core, at_x, :, pl.ds(at_v, HEAD_DIM)] = value_term[inside]
+            summed[head] = summed[head] + lax.dot_general(
+                score_grad, keys, (((0,), (0,)), ((), ())), preferred_element_type=jnp.float32
+            )
+            return carry
+
+        lax.fori_loop(0, heads, one, 0)
+        core_copy(offset).start()
+
+    def stage_core(offset):
+        core_copy(offset).wait_recv()
+        out_x[offset] = (
+            part[offset, core, 1 - x].astype(jnp.float32)
+            + in_core[offset, 1 - x].astype(jnp.float32)
+        ).astype(jnp.bfloat16)
+        x_copy(offset).start()
+        kept[offset] = part[offset, core, x].astype(jnp.float32) + in_core[offset, x].astype(
+            jnp.float32
+        )
+
+    def stage_across(offset):
+        x_copy(offset).wait_recv()
+        total = kept[offset] + in_x[offset].astype(jnp.float32)
+        if offset:
+            out_z[offset] = total.astype(jnp.bfloat16)
+            z_copy(offset).start()
+        else:
+            kept[0] = total
+
+    order = tuple(range(1, depth)) + (0,)
+    stages = (stage_pairs, stage_core, stage_across)
+    for step in range(depth + len(stages) - 1):
+        for late, stage in enumerate(stages):
+            if 0 <= step - late < depth:
+                stage(order[step - late])
+    for head in range(heads):
+        for turn in range(2):
+            at = (2 * head + turn) * HEAD_DIM
+            q_grad[:, at : at + HEAD_DIM] = summed[head, turn * count : (turn + 1) * count]
+    total = kept[0]
+    for offset in range(1, depth):
+        z_copy(offset).wait_recv()
+        total = total + in_z[offset - 1].astype(jnp.float32)
+    kv_grad[...] = total
+    for offset in range(depth):
+        core_copy(offset).wait_send()
+        x_copy(offset).wait_send()
+        if offset:
+            z_copy(offset).wait_send()
+
+
+def attend_back(queries, grads, outs, logs, kv_all, q_pos, q_begin, k_pos):
+    depth = lax.axis_size("ctx") // 4
+    count = queries.shape[0]
+    heads = queries.shape[1] // HEAD_DIM // 2
+    width = kv_all.shape[1]
+    dma = pltpu.SemaphoreType.DMA
+    vmem = pl.BlockSpec(memory_space=pltpu.VMEM)
+    return pl.pallas_call(
+        partial(attend_back_kernel, depth),
+        out_shape=[
+            jax.ShapeDtypeStruct(queries.shape, jnp.float32),
+            jax.ShapeDtypeStruct((count, width), jnp.float32),
+        ],
+        in_specs=[vmem] * 8,
+        out_specs=[vmem] * 2,
+        scratch_shapes=[
+            pltpu.VMEM((heads, 2 * count, HEAD_DIM), jnp.bfloat16),
+            pltpu.VMEM((heads, 2 * count, HEAD_DIM), jnp.bfloat16),
+            pltpu.VMEM((heads, 2 * count), jnp.float32),
+            pltpu.VMEM((heads, 2 * count, HEAD_DIM), jnp.float32),
+            pltpu.VMEM((4 * count, 2 * count), jnp.float32),
+            pltpu.VMEM((depth, 2, 2, count, width), jnp.bfloat16),
+            pltpu.VMEM((depth, 2, count, width), jnp.bfloat16),
+            pltpu.VMEM((depth, count, width), jnp.float32),
+            pltpu.VMEM((depth, count, width), jnp.bfloat16),
+            pltpu.VMEM((depth, count, width), jnp.bfloat16),
+            pltpu.VMEM((depth, count, width), jnp.bfloat16),
+            pltpu.VMEM((depth - 1, count, width), jnp.bfloat16),
+            dma((depth,)),
+            dma((depth,)),
+            dma((depth,)),
+            dma((depth,)),
+            dma((depth - 1,)),
+            dma((depth - 1,)),
+        ],
+        compiler_params=pltpu.CompilerParams(
+            collective_id=4, has_side_effects=True, vmem_limit_bytes=56 * 2**20
+        ),
+        name="attend_back",
+    )(queries, grads, outs, logs, kv_all, q_pos, q_begin, k_pos)
+
+
 def swap(value, axis, stride):
     count = lax.axis_size(axis)
     return lax.ppermute(value, axis, [(i, i ^ stride) for i in range(count)])
@@ -636,32 +1004,44 @@
     queries = query_val.astype(jnp.bfloat16).reshape(count, KV_HEADS, groups, HEAD_DIM)
     keys = key_val.astype(jnp.bfloat16).reshape(count, KV_HEADS * HEAD_DIM)
     values = value_raw.astype(jnp.bfloat16)
-    key_piece = lax.all_gather(keys, "ctx", axis=0, tiled=True)
-    value_piece = lax.all_gather(values, "ctx", axis=0, tiled=True)
-    size = key_piece.shape[0]
-    key_pos, key_seg = slices(jnp.int32(0), size)
-    allowed = allowed_pairs(my_pos, my_seg, key_pos, key_seg)
-    top = jnp.full((KV_HEADS, groups, count), NEG, jnp.float32)
-    scores = jnp.einsum(
-        "tkgd,skd->kgts",
-        queries,
-        key_piece.reshape(size, KV_HEADS, HEAD_DIM),
-        preferred_element_type=jnp.float32,
-    )
-    scores = jnp.where(allowed, scores, NEG)
-    new_top = jnp.maximum(top, jnp.max(scores, axis=-1))
-    weights = jnp.where(allowed, jnp.exp(scores - new_top[..., None]), 0.0)
-    total = jnp.sum(weights, axis=-1)
-    summed = jnp.einsum(
-        "kgts,skd->kgtd",
-        weights.astype(jnp.bfloat16),
-        value_piece.reshape(size, KV_HEADS, HEAD_DIM),
-        preferred_element_type=jnp.float32,
-    )
-    top, total, summed = (new_top, total, summed)
-    attended = summed / total[..., None]
-    log_total = top + jnp.log(total)
-    heads_out = attended.transpose(2, 0, 1, 3).reshape(count, HEADS, HEAD_DIM)
+    near = lax.axis_size("ctx") <= 16
+    if near:
+        q_pos, q_begin = (my_pos, my_pos - my_rel)
+        heads_flat, log_total, kv_all = attend(
+            queries.reshape(count, -1),
+            jnp.concatenate([keys, values], axis=1),
+            q_pos[:, None],
+            q_begin[:, None],
+            place_all[None, :],
+        )
+        heads_out = heads_flat.reshape(count, HEADS, HEAD_DIM)
+    else:
+        key_piece = lax.all_gather(keys, "ctx", axis=0, tiled=True)
+        value_piece = lax.all_gather(values, "ctx", axis=0, tiled=True)
+        size = key_piece.shape[0]
+        key_pos, key_seg = slices(jnp.int32(0), size)
+        allowed = allowed_pairs(my_pos, my_seg, key_pos, key_seg)
+        top = jnp.full((KV_HEADS, groups, count), NEG, jnp.float32)
+        scores = jnp.einsum(
+            "tkgd,skd->kgts",
+            queries,
+            key_piece.reshape(size, KV_HEADS, HEAD_DIM),
+            preferred_element_type=jnp.float32,
+        )
+        scores = jnp.where(allowed, scores, NEG)
+        new_top = jnp.maximum(top, jnp.max(scores, axis=-1))
+        weights = jnp.where(allowed, jnp.exp(scores - new_top[..., None]), 0.0)
+        total = jnp.sum(weights, axis=-1)
+        summed = jnp.einsum(
+            "kgts,skd->kgtd",
+            weights.astype(jnp.bfloat16),
+            value_piece.reshape(size, KV_HEADS, HEAD_DIM),
+            preferred_element_type=jnp.float32,
+        )
+        top, total, summed = (new_top, total, summed)
+        attended = summed / total[..., None]
+        log_total = top + jnp.log(total)
+        heads_out = attended.transpose(2, 0, 1, 3).reshape(count, HEADS, HEAD_DIM)
     mixed_in = (
         (heads_out * head_gate[:, :, None]).reshape(count, HEADS * HEAD_DIM).astype(jnp.bfloat16)
     )
@@ -700,48 +1080,62 @@
     headgate_weight_grad = jnp.einsum(
         "td,th->dh", lowered, logit_grad, preferred_element_type=jnp.float32
     )
-    out_grad = heads_grad.reshape(count, KV_HEADS, groups, HEAD_DIM)
-    delta = jnp.sum(
-        out_grad.astype(jnp.float32) * heads_out.reshape(count, KV_HEADS, groups, HEAD_DIM), axis=-1
-    ).transpose(1, 2, 0)
-    cycle_size = lax.axis_size("ctx")
-    my_index = lax.axis_index("ctx")
-
-    def cycle_step(step, carry):
-        pair_piece, grad_piece, query_sum = carry
-        anchor = lax.rem(my_index - step + cycle_size, cycle_size)
-        key_pos, key_seg = slices(anchor * count, count)
-        allowed = allowed_pairs(my_pos, my_seg, key_pos, key_seg)
-        key_heads = pair_piece[0].reshape(count, KV_HEADS, HEAD_DIM)
-        value_heads = pair_piece[1].reshape(count, KV_HEADS, HEAD_DIM)
-        score_grad, weights = pair_terms(
-            queries, out_grad, log_total, delta, key_heads, value_heads, allowed
-        )
-        key_term = jnp.einsum(
-            "kgts,tkgd->skd", score_grad, queries, preferred_element_type=jnp.float32
-        ).reshape(count, KV_HEADS * HEAD_DIM)
-        value_term = jnp.einsum(
-            "kgts,tkgd->skd", weights, out_grad, preferred_element_type=jnp.float32
-        ).reshape(count, KV_HEADS * HEAD_DIM)
-        query_sum, grad_piece = (
-            query_sum
-            + jnp.einsum(
-                "kgts,skd->tkgd", score_grad, key_heads, preferred_element_type=jnp.float32
-            ),
-            grad_piece + jnp.stack([key_term, value_term]),
-        )
-        pair_piece = from_behind(pair_piece, "ctx", 1)
-        grad_piece = from_behind(grad_piece.astype(jnp.bfloat16), "ctx", 1).astype(grad_piece.dtype)
-        return (pair_piece, grad_piece, query_sum)
-
-    cycle_start = (
-        jnp.stack([keys, values]),
-        jnp.zeros((2, count, KV_HEADS * HEAD_DIM), jnp.float32),
-        jnp.zeros((count, KV_HEADS, groups, HEAD_DIM), jnp.float32),
-    )
-    last_pair, home_grads, query_grad = lax.fori_loop(0, cycle_size, cycle_step, cycle_start)
-    key_grad = home_grads[0].reshape(count, KV_HEADS, HEAD_DIM)
-    value_grad = home_grads[1].reshape(count, KV_HEADS, HEAD_DIM)
+    if near:
+        query_grad, kv_grad = attend_back(
+            queries.reshape(count, -1),
+            heads_grad.reshape(count, -1),
+            heads_flat,
+            log_total,
+            kv_all,
+            jnp.tile(q_pos, 2)[None, :],
+            jnp.tile(q_begin, 2)[None, :],
+            place_all[:, None],
+        )
+        key_grad = kv_grad[:, : KV_HEADS * HEAD_DIM].reshape(count, KV_HEADS, HEAD_DIM)
+        value_grad = kv_grad[:, KV_HEADS * HEAD_DIM :].reshape(count, KV_HEADS, HEAD_DIM)
+    else:
+        out_grad = heads_grad.reshape(count, KV_HEADS, groups, HEAD_DIM)
+        delta = jnp.sum(
+            out_grad.astype(jnp.float32) * heads_out.reshape(count, KV_HEADS, groups, HEAD_DIM), axis=-1
+        ).transpose(1, 2, 0)
+        cycle_size = lax.axis_size("ctx")
+        my_index = lax.axis_index("ctx")
+
+        def cycle_step(step, carry):
+            pair_piece, grad_piece, query_sum = carry
+            anchor = lax.rem(my_index - step + cycle_size, cycle_size)
+            key_pos, key_seg = slices(anchor * count, count)
+            allowed = allowed_pairs(my_pos, my_seg, key_pos, key_seg)
+            key_heads = pair_piece[0].reshape(count, KV_HEADS, HEAD_DIM)
+            value_heads = pair_piece[1].reshape(count, KV_HEADS, HEAD_DIM)
+            score_grad, weights = pair_terms(
+                queries, out_grad, log_total, delta, key_heads, value_heads, allowed
+            )
+            key_term = jnp.einsum(
+                "kgts,tkgd->skd", score_grad, queries, preferred_element_type=jnp.float32
+            ).reshape(count, KV_HEADS * HEAD_DIM)
+            value_term = jnp.einsum(
+                "kgts,tkgd->skd", weights, out_grad, preferred_element_type=jnp.float32
+            ).reshape(count, KV_HEADS * HEAD_DIM)
+            query_sum, grad_piece = (
+                query_sum
+                + jnp.einsum(
+                    "kgts,skd->tkgd", score_grad, key_heads, preferred_element_type=jnp.float32
+                ),
+                grad_piece + jnp.stack([key_term, value_term]),
+            )
+            pair_piece = from_behind(pair_piece, "ctx", 1)
+            grad_piece = from_behind(grad_piece.astype(jnp.bfloat16), "ctx", 1).astype(grad_piece.dtype)
+            return (pair_piece, grad_piece, query_sum)
+
+        cycle_start = (
+            jnp.stack([keys, values]),
+            jnp.zeros((2, count, KV_HEADS * HEAD_DIM), jnp.float32),
+            jnp.zeros((count, KV_HEADS, groups, HEAD_DIM), jnp.float32),
+        )
+        last_pair, home_grads, query_grad = lax.fori_loop(0, cycle_size, cycle_step, cycle_start)
+        key_grad = home_grads[0].reshape(count, KV_HEADS, HEAD_DIM)
+        value_grad = home_grads[1].reshape(count, KV_HEADS, HEAD_DIM)
     query_raw_grad, query_gain_grad = query_back(query_grad.reshape(count, HEADS, HEAD_DIM))
     key_raw_grad, key_gain_grad = key_back(key_grad)
     query_low = query_raw_grad.astype(jnp.bfloat16).reshape(count, -1)

time: 1080 us -> 736 us (0.68)
  waiting for transfers between devices: 306 us -> 55.7 us
  Pallas kernels: 280 us -> 437 us
  matrix products: 153 us -> 51.1 us
  local copies, waits for them, and re-layouts: 190 us -> 113 us
  other arithmetic: 125 us -> 64.3 us
  between operations: 15.5 us -> 2.42 us
    ppermute x32 -> x0, waiting for transfers between devices: 202 us -> none  [from_behind(): return lax.ppermute(value, axis, pairs)]
    pallas_call x0 -> x2, Pallas kernels: none -> 156 us  [the longest x1 85.1 us: attend_back(): pl.pallas_call(partial(attend_back_kernel, depth), out_shape=[jax.ShapeDt...]
    dot_general x82 -> x0, matrix products: 117 us -> none  [the longest x16 39.6 us: cycle_step(): jnp.einsum('kgts,skd->tkgd', score_grad, key_heads, preferred_element_typ...]
    all_gather x2 -> x0, waiting for transfers between devices: 54.7 us -> none  [the longest x1 32 us: per_device(): value_piece = lax.all_gather(values, 'ctx', axis=0, tiled=True)]
    convert_element_type x35 -> x0, other arithmetic: 48.7 us -> none  [the longest x16 33.3 us: cycle_step(): from_behind(grad_piece.astype(jnp.bfloat16), 'ctx', 1)]
    while x80 -> x0, local copies, waits for them, and re-layouts: 30.1 us -> none
    slice x18 -> x2, local copies, waits for them, and re-layouts: 31.2 us -> 2.9 us  [the longest x1 1.77 us: per_device(): kv_grad[:, KV_HEADS * HEAD_DIM:].reshape(count, KV_HEADS, HEAD_DIM)]
    dynamic_slice x34 -> x0, local copies, waits for them, and re-layouts: 26.4 us -> none  [the longest x16 12.8 us: slices(): lax.dynamic_slice_in_dim(place_all, start, size)]
  transfers between devices with their start and end apart: 38 -> 4, of which waited for: 36 -> 2; matrix products, arithmetic and copies ran while one was open for 16% -> 7% of each run, Pallas kernels for 0% -> 0%
where the time goes in v3:
time: 736 us; the launch traced here: 726 us
  Pallas kernels  437 us (59%)
  local copies, waits for them, and re-layouts  113 us (15%)
  other arithmetic  64.3 us (9%)
  waiting for transfers between devices  55.7 us (8%)
  matrix products  51.1 us (7%)
    pallas_call x1, Pallas kernels, sum_grads(): pl.pallas_call(partial(sum_kernel, depth), out_shape=[jax.ShapeDtypeStruc...  200 us
    pallas_call x1, Pallas kernels, attend_back(): pl.pallas_call(partial(attend_back_kernel, depth), out_shape=[jax.ShapeDt...  85.1 us
    pallas_call x1, Pallas kernels, gather_weights(): pl.pallas_call(partial(gather_kernel, count), out_shape=[jax.ShapeDtypeSt...  81.6 us
    pallas_call x1, Pallas kernels, attend(): pl.pallas_call(partial(attend_kernel, depth), out_shape=[jax.ShapeDtypeSt...  70.5 us
    ppermute x4, waiting for transfers between devices, swap(): return lax.ppermute(value, axis, [(i, i ^ stride) for i in range(count)])  55.7 us
    unnamed x239, local copies, waits for them, and re-layouts  35.3 us
    reshape x6, local copies, waits for them, and re-layouts, gather_tokens(): b.reshape(count, -1, 2, SIDE)  15.6 us
  transfers between devices with their start and end apart: 4, of which 2 were waited for; matrix products, arithmetic and copies ran while one was open for 7% of the time, Pallas kernels for 0%

profile of v3, /device:TPU:0, one launch (start us, length us, event | category | flops | bytes accessed | tf_op | source)
XLA Modules:
  0.0 725.8 jit_solution(475760803458768086)
XLA Ops:
  1.6 2.8 concatenate.100
  4.4 1.9 copy-done.5
  6.3 1.9 copy-done.6
  15.7 81.6 %gather_weights.1 = (bf16[1024,2048]{1,0:T(8,128)(2,1)}, bf16[1024,1024]{1,0:T(8,128)(2,1)S(1)}, bf16[1024,1024]{1,0:T(8,128)(2,1)S(1)}, bf16[2048,1024]{1,0:T(8...) custom-call(bf16[512,2048]{1,0:T(8,128)(2,1)S(1)} %copy-done.8, ...), custom_call_target="tpu_custom_call" | custom-call | tf_op jit(solution)/shard_map/gather_weights/pallas_call | solution.py:223
  100.4 6.4 copy.163
  107.5 3.6 multiply_reduce_fusion.2
  115.5 2.1 copy.164.q_ref
  118.8 4.0 copy.165
  122.7 2.4 multiply_reduce_fusion.8
  132.2 70.5 %attend.1 = (f32[128,2048]{1,0:T(8,128)S(1)}, f32[8,256]{1,0:T(8,128)S(1)}, bf16[2048,2048]{1,0:T(8,128)(2,1)S(1)}) custom-call(bf16[128,2048]{1,0:T(8,128)(2,1)S(1)} %copy-done.4, bf16[128,2048]{1,0:T(8,128)(2,1)S(1)} %pad_maximum_fusion.4.kv_ref, s32[128,1]{1,0:T(8,128)S(1)} %copy.131.q_pos, s32[128,1]{1,0:T(8,128)S(1)} %copy.132.q_begin, ...), custom_call_target="tpu_custom_call" | custom-call | tf_op jit(solution)/shard_map/attend/pallas_call | solution.py:667
  202.7 3.3 copy-done.2
  209.5 5.1 fusion.60
  214.7 2.1 fusion.61
  218.6 7.4 %multiply_convert_fusion = (bf16[128,3072]{1,0:T(8,128)(2,1)}, bf16[128,3072]{1,0:T(8,128)(2,1)S(1)}, bf16[128,3072]{1,0:T(8,128)(2,1)}) fusion(f32[128,3072]{1,0:T(8,128)} %fusion.60, f32[128,3072]{1,0:T(8,128)} %fusion.61, bf16[3072,1024]{1,0:T(8,128)(2,1)} %get-tuple-element.37, bf16[1,128,1024]{2,1,0:T(8,128)(2,1)} %param.17), kind=kOutput, calls=%fused_computation.17 | convolution fusion | flops 811204608 | bytes 12058624 | tf_op jit(solution)/shard_map/td,fd->tf/dot_general | solution.py:1059
  226.9 5.8 fusion.62
  232.6 3.2 reshape.453
  235.9 3.4 reshape.454
  239.3 6.3 multiply_reduce_fusion.4
  247.2 3.0 multiply_bitcast_fusion
  254.5 85.1 %attend_back.1 = (f32[128,2048]{1,0:T(8,128)}, f32[128,2048]{1,0:T(8,128)}) custom-call(bf16[128,2048]{1,0:T(8,128)(2,1)} %copy.164.q_ref, bf16[128,2048]{1,0:T(8,128)(2,1)} %get-tuple-element.130.grad_ref, f32[128,2048]{1,0:T(8,128)} %copy-done.1, f32[8,256]{1,0:T(8,128)} %copy-done.13, bf16[2048,2048]{1,0:T(8,128)(2,1)} %copy-done.2, s32[1,256]{1,0:T(1,128)} %bitcast.250, ...), custom_call_target="tpu_custom_call" | custom-call | tf_op jit(solution)/shard_map/attend_back/pallas_call | solution.py:863
  347.4 2.5 copy.169
  354.2 3.0 copy.151
  357.2 3.3 copy.152
  361.4 2.2 constant_dynamic-update-slice_fusion.4
  363.6 2.2 constant_dynamic-update-slice_fusion.3
  373.2 1.9 constant_dynamic-slice_fusion.3
  377.8 2.6 reshape.450
  380.4 2.5 constant_dynamic-slice_fusion.5
  388.6 2.6 fusion.63
  396.4 44.7 %collective-permute-done.2 = bf16[128,12,2,512]{0,3,1,2:T(8,128)(2,1)} collective-permute-done((bf16[128,12,2,512]{0,3,1,2:T(8,128)(2,1)}, bf16[128,12,2,512]{0,3,1,2:T(8,128)(2,1)}, u32[]{:S(2)}, u32[]{:S(2)}) %collective-permute-start.2) | collective-permute-done | bytes 3145760 | tf_op jit(solution)/shard_map/ppermute | solution.py:900
  441.2 5.2 fusion.2
  447.0 11.0 %collective-permute-done = bf16[128,3584]{1,0:T(8,128)(2,1)} collective-permute-done((bf16[128,3584]{1,0:T(8,128)(2,1)}, bf16[128,3584]{1,0:T(8,128)(2,1)}, u32[]{:S(2)}, u32[]{:S(2)}) %collective-permute-start) | collective-permute-done | bytes 917536 | tf_op jit(solution)/shard_map/ppermute | solution.py:900
  457.9 2.6 pad_maximum_fusion.2
  464.7 2.1 fusion.29
  466.8 4.5 fusion.6
  471.3 7.7 %pad_maximum_fusion.1.rows_ref = bf16[512,3584]{1,0:T(8,128)(2,1)} fusion(bf16[256,3584]{1,0:T(8,128)(2,1)} %collective-permute-done.1, bf16[128,3584]{1,0:T(8,128)(2,1)} %collective-permute-done, bf16[128,512]{1,0:T(8,128)(2,1)S(1)} %copy-done.60, bf16[128,1024]{1,0:T(8,128)(2,1)S(1)} %bitcast.231, bf16[128,512]{1,0:T(8,128)(2,1)S(1)} %bitcast.238, ...), kind=kLoop, calls=%fused_computation.6 | loop fusion | flops 22020096 | bytes 7340032 | tf_op jit(solution)/shard_map/concatenate | solution.py:916
  479.0 3.0 copy.157
  482.0 4.8 copy.158
  486.8 5.5 pad_maximum_fusion.cols_ref
  492.3 200.0 %sum_grads.1 = (bf16[15,512,1024]{2,1,0:T(8,128)(2,1)}, f32[80,128]{1,0:T(8,128)S(1)}) custom-call(bf16[512,3584]{1,0:T(8,128)(2,1)S(1)} %copy-done, bf16[512,6144]{1,0:T(8,128)(2,1)} %pad_maximum_fusion.cols_ref, f32[2,80,128]{2,1,0:T(8,128)S(1)} %pad_maximum_fusion.6.small_ref), custom_call_target="tpu_custom_call" | custom-call | tf_op jit(solution)/shard_map/sum_grads/pallas_call | solution.py:489
  692.9 8.1 %slice_bitcast_fusion.2 = (bf16[512,1024]{1,0:T(8,128)(2,1)}, bf16[512,1024]{1,0:T(8,128)(2,1)}, bf16[512,1024]{1,0:T(8,128)(2,1)}, bf16[512,1024]{1,0:T(8,128)(...) fusion(bf16[15,512,1024]{2,1,0:T(8,128)(2,1)} %get-tuple-element.43), kind=kLoop, calls=%fused_computation.46 | loop fusion | flops 1048576 | bytes 23068672 | tf_op jit(solution)/shard_map/squeeze | solution.py:922
  701.0 3.1 slice.213
  704.1 2.2 slice.222
  707.7 4.1 bitcast_convert_fusion.1
  711.8 3.7 bitcast_convert_fusion
  715.5 2.5 maximum_convert_fusion.2
  718.3 3.5 maximum_convert_fusion
  721.8 3.5 maximum_convert_fusion.1
  (341 shorter events, 76.8 us)
Async XLA Ops:
  100.4 6.4 copy-start.17
  107.0 15.7 %copy-start.87 = (f32[128]{0:T(128)}, f32[128]{0:T(128)S(1)}, u32[]{:S(2)}) copy-start(f32[128]{0:T(128)S(1)} %fusion.39) | copy-start | bytes 1540
  111.1 6.5 copy-start.21
  111.1 6.5 copy-start.74
  111.1 6.4 copy-start.72
  114.2 11.2 %copy-start.67 = (f32[128,64]{0,1:T(8,128)}, f32[128,64]{0,1:T(8,128)S(1)}, u32[]{:S(2)}) copy-start(f32[128,64]{0,1:T(8,128)S(1)} %get-tuple-element.164) | copy-start | bytes 98308
  114.2 11.2 %copy-start.69 = (f32[128,64]{0,1:T(8,128)}, f32[128,64]{0,1:T(8,128)S(1)}, u32[]{:S(2)}) copy-start(f32[128,64]{0,1:T(8,128)S(1)} %get-tuple-element.165) | copy-start | bytes 98308
  118.8 6.4 copy-start.106
  118.8 6.4 copy-start.107
  132.2 75.6 %copy-start.19 = (bf16[2048,1024]{1,0:T(8,128)(2,1)S(1)}, bf16[2048,1024]{1,0:T(8,128)(2,1)}, u32[]{:S(2)}) copy-start(bf16[2048,1024]{1,0:T(8,128)(2,1)} %get-tuple-element.34) | copy-start | bytes 12582916
  206.0 39.9 %copy-start.1 = (f32[128,2048]{1,0:T(8,128)}, f32[128,2048]{1,0:T(8,128)S(1)}, u32[]{:S(2)}) copy-start(f32[128,2048]{1,0:T(8,128)S(1)} %get-tuple-element.33.out_ref) | copy-start | bytes 3145732
  208.6 37.1 %copy-start.92 = (f32[128]{0:T(128)}, f32[128]{0:T(128)S(1)}, u32[]{:S(2)}) copy-start(f32[128]{0:T(128)S(1)} %fusion.40) | copy-start | bytes 1540
  239.3 6.4 copy-start.15
  239.3 6.4 copy-start.53
  239.3 7.8 %copy-start.20 = (bf16[2048,1024]{1,0:T(8,128)(2,1)S(1)}, bf16[2048,1024]{1,0:T(8,128)(2,1)}, u32[]{:S(2)}) copy-start(bf16[2048,1024]{1,0:T(8,128)(2,1)} %get-tuple-element.34) | copy-start | bytes 12582916
  239.3 7.8 %copy-start.26 = (f32[128,16,128]{2,1,0:T(8,128)S(1)}, f32[128,16,128]{2,1,0:T(8,128)}, u32[]{:S(2)}) copy-start(f32[128,16,128]{2,1,0:T(8,128)} %copy-done.25) | copy-start | bytes 3145732
  247.2 6.2 copy-start.105
  247.2 6.7 copy-start.99
  254.5 89.1 %copy-start.68 = (f32[128,64]{0,1:T(8,128)S(1)}, f32[128,64]{0,1:T(8,128)}, u32[]{:S(2)}) copy-start(f32[128,64]{0,1:T(8,128)} %copy-done.67) | copy-start | bytes 98308
  254.5 89.1 %copy-start.70 = (f32[128,64]{0,1:T(8,128)S(1)}, f32[128,64]{0,1:T(8,128)}, u32[]{:S(2)}) copy-start(f32[128,64]{0,1:T(8,128)} %copy-done.69) | copy-start | bytes 98308
  353.4 7.1 copy-start.65
  357.2 10.3 %copy-start.31 = (bf16[128,16,128]{0,2,1:T(8,128)(2,1)S(1)}, bf16[128,16,128]{0,2,1:T(8,128)(2,1)}, u32[]{:S(2)}) copy-start(bf16[128,16,128]{0,2,1:T(8,128)(2,1)} %fusion.10) | copy-start | bytes 1572868
  357.2 11.1 %copy-start.52 = (bf16[128,8,128]{0,2,1:T(8,128)(2,1)S(1)}, bf16[128,8,128]{0,2,1:T(8,128)(2,1)}, u32[]{:S(2)}) copy-start(bf16[128,8,128]{0,2,1:T(8,128)(2,1)} %fusion.15) | copy-start | bytes 786436
  361.4 7.7 %copy-start.66 = (bf16[128,1024]{0,1:T(8,128)(2,1)S(1)}, bf16[128,1024]{0,1:T(8,128)(2,1)}, u32[]{:S(2)}) copy-start(bf16[128,1024]{0,1:T(8,128)(2,1)} %copy.168) | copy-start | bytes 786436
  363.6 9.4 %copy-start.30 = (bf16[128,1024]{1,0:T(8,128)(2,1)S(1)}, bf16[128,1024]{1,0:T(8,128)(2,1)}, u32[]{:S(2)}) copy-start(bf16[128,1024]{1,0:T(8,128)(2,1)} %copy-done.29) | copy-start | bytes 786436
  363.6 9.6 %copy-start.97 = (bf16[1,1,4,128]{3,2,1,0:T(4,128)(2,1)S(1)}, bf16[1,1,4,128]{3,2,1,0:T(4,128)(2,1)}, u32[]{:S(2)}) copy-start(bf16[1,1,4,128]{3,2,1,0:T(4,128)(2,1)} %get-tuple-element.149) | copy-start | bytes 3076
  363.6 9.6 %copy-start.98 = (bf16[1,1,4,128]{3,2,1,0:T(4,128)(2,1)S(1)}, bf16[1,1,4,128]{3,2,1,0:T(4,128)(2,1)}, u32[]{:S(2)}) copy-start(bf16[1,1,4,128]{3,2,1,0:T(4,128)(2,1)} %get-tuple-element.150) | copy-start | bytes 3076
  369.8 71.4 %collective-permute-start.2 = (bf16[128,12,2,512]{0,3,1,2:T(8,128)(2,1)}, bf16[128,12,2,512]{0,3,1,2:T(8,128)(2,1)}, u32[]{:S(2)}, u32[]{:S(2)}) collective-permute-start(bf16[128,12,2,512]{0,3,1,2:T(8,128)(2,1)} %constant_dynamic-update-slice_fusion), channel_id=1, source_target_pairs={{0,1},{1,0},{2,3},{3,2},{4,5},{5,4},{6,7},{7,6},{8,9},{9,8},{10,11... | collective-permute-start | bytes 9437192 | tf_op jit(solution)/shard_map/ppermute | solution.py:900
  383.3 74.7 %copy-start.59 = (bf16[128,512]{1,0:T(8,128)(2,1)}, bf16[128,512]{1,0:T(8,128)(2,1)S(1)}, u32[]{:S(2)}) copy-start(bf16[128,512]{1,0:T(8,128)(2,1)S(1)} %get-tuple-element.141) | copy-start | bytes 393220
  384.3 73.6 %collective-permute-start = (bf16[128,3584]{1,0:T(8,128)(2,1)}, bf16[128,3584]{1,0:T(8,128)(2,1)}, u32[]{:S(2)}, u32[]{:S(2)}) collective-permute-start(bf16[128,3584]{1,0:T(8,128)(2,1)} %pad_maximum_fusion.3), channel_id=1, source_target_pairs={{0,1},{1,0},{2,3},{3,2},{4,5},{5,4},{6,7},{7,6},{8,9},{9,8},{10,11... | collective-permute-start | bytes 2752520 | tf_op jit(solution)/shard_map/ppermute | solution.py:900
  387.0 6.1 copy-start.32
  396.4 50.2 %copy-start.56 = (bf16[128,1,1024]{2,1,0:T(2,128)(2,1)S(1)}, bf16[128,1,1024]{2,1,0:T(2,128)(2,1)}, u32[]{:S(2)}) copy-start(bf16[128,1,1024]{2,1,0:T(2,128)(2,1)} %get-tuple-element.137) | copy-start | bytes 786436
  396.4 50.3 %copy-start.62 = (bf16[128,1,512]{2,1,0:T(2,128)(2,1)S(1)}, bf16[128,1,512]{2,1,0:T(2,128)(2,1)}, u32[]{:S(2)}) copy-start(bf16[128,1,512]{2,1,0:T(2,128)(2,1)} %get-tuple-element.139) | copy-start | bytes 393220
  396.4 50.4 %copy-start.47 = (bf16[128,1,1536]{2,1,0:T(2,128)(2,1)S(1)}, bf16[128,1,1536]{2,1,0:T(2,128)(2,1)}, u32[]{:S(2)}) copy-start(bf16[128,1,1536]{2,1,0:T(2,128)(2,1)} %get-tuple-element.131) | copy-start | bytes 1179652
  446.3 35.7 %collective-permute-start.3 = (bf16[256,12,512]{0,2,1:T(8,128)(2,1)}, bf16[256,12,512]{0,2,1:T(8,128)(2,1)}, u32[]{:S(2)}, u32[]{:S(2)}) collective-permute-start(bf16[256,12,512]{0,2,1:T(8,128)(2,1)} %get-tuple-element.121), channel_id=1, source_target_pairs={{0,2},{2,0},{4,6},{6,4},{8,10},{10,8},{12,14},{14,12},{16,18},{18,... | collective-permute-start | bytes 9437192 | tf_op jit(solution)/shard_map/ppermute | solution.py:900
  446.7 13.9 %copy-start.91 = (f32[1024]{0:T(1024)S(1)}, f32[1024]{0:T(1024)}, u32[]{:S(2)}) copy-start(f32[1024]{0:T(1024)} %get-tuple-element.104) | copy-start | bytes 12292
  446.7 13.9 %copy-start.108 = (f32[128]{0:T(128)S(1)}, f32[128]{0:T(128)}, u32[]{:S(2)}) copy-start(f32[128]{0:T(128)} %get-tuple-element.100) | copy-start | bytes 1540
  446.7 14.0 %copy-start.101 = (f32[128]{0:T(128)S(1)}, f32[128]{0:T(128)}, u32[]{:S(2)}) copy-start(f32[128]{0:T(128)} %get-tuple-element.102) | copy-start | bytes 1540
  446.8 14.9 %copy-start.49 = (bf16[128,1,1024]{2,0,1:T(8,128)(2,1)}, bf16[128,1,1024]{2,0,1:T(8,128)(2,1)S(1)}, u32[]{:S(2)}) copy-start(bf16[128,1,1024]{2,0,1:T(8,128)(2,1)S(1)} %copy.200) | copy-start | bytes 786436
  446.8 17.0 %copy-start.57 = (bf16[128,1,512]{2,0,1:T(8,128)(2,1)}, bf16[128,1,512]{2,0,1:T(8,128)(2,1)S(1)}, u32[]{:S(2)}) copy-start(bf16[128,1,512]{2,0,1:T(8,128)(2,1)S(1)} %copy.202) | copy-start | bytes 393220
  446.8 17.8 %copy-start.16 = (f32[128,1024]{1,0:T(8,128)S(1)}, f32[128,1024]{1,0:T(8,128)}, u32[]{:S(2)}) copy-start(f32[128,1024]{1,0:T(8,128)} %copy-done.14) | copy-start | bytes 1572868
  446.9 17.8 %copy-start.35 = (f32[128,1024]{1,0:T(8,128)S(1)}, f32[128,1024]{1,0:T(8,128)}, u32[]{:S(2)}) copy-start(f32[128,1024]{1,0:T(8,128)} %copy-done.34) | copy-start | bytes 1572868
  446.9 17.8 %copy-start.54 = (bf16[1,128,1024]{2,1,0:T(8,128)(2,1)S(1)}, bf16[1,128,1024]{2,1,0:T(8,128)(2,1)}, u32[]{:S(2)}) copy-start(bf16[1,128,1024]{2,1,0:T(8,128)(2,1)} %param.17) | copy-start | bytes 786436
  446.9 17.8 %copy-start.90 = (f32[128]{0:T(128)S(1)}, f32[128]{0:T(128)}, u32[]{:S(2)}) copy-start(f32[128]{0:T(128)} %copy-done.87) | copy-start | bytes 1540
  446.9 19.8 %copy-start.45 = (bf16[128,1,1536]{2,0,1:T(8,128)(2,1)}, bf16[128,1,1536]{2,0,1:T(8,128)(2,1)S(1)}, u32[]{:S(2)}) copy-start(bf16[128,1,1536]{2,0,1:T(8,128)(2,1)S(1)} %copy.198) | copy-start | bytes 1179652
  457.9 8.8 %copy-start.48 = (bf16[128,3072]{1,0:T(8,128)(2,1)S(1)}, bf16[128,3072]{1,0:T(8,128)(2,1)}, u32[]{:S(2)}) copy-start(bf16[128,3072]{1,0:T(8,128)(2,1)} %get-tuple-element.124) | copy-start | bytes 2359300
  460.5 10.8 %collective-permute-start.1 = (bf16[256,3584]{1,0:T(8,128)(2,1)}, bf16[256,3584]{1,0:T(8,128)(2,1)}, u32[]{:S(2)}, u32[]{:S(2)}) collective-permute-start(bf16[256,3584]{1,0:T(8,128)(2,1)} %pad_maximum_fusion.2), channel_id=1, source_target_pairs={{0,2},{2,0},{4,6},{6,4},{8,10},{10,8},{12,14},{14,12},{16,18},{18,... | collective-permute-start | bytes 5505032 | tf_op jit(solution)/shard_map/ppermute | solution.py:900
  471.3 7.7 %copy-start.23 = (bf16[256,12,1,512]{0,3,1,2:T(8,128)(2,1)S(1)}, bf16[256,12,1,512]{0,3,1,2:T(8,128)(2,1)}, u32[]{:S(2)}) copy-start(bf16[256,12,1,512]{0,3,1,2:T(8,128)(2,1)} %get-tuple-element.120) | copy-start | bytes 9437188
  (67 other events, 203.9 us)

commit v4 on v3

--- a/solution.py
+++ b/solution.py
@@ -1,4 +1,5 @@
 from functools import partial
+from types import SimpleNamespace
 
 import jax
 import jax.numpy as jnp
@@ -233,7 +234,7 @@
         scratch_shapes=[pltpu.VMEM(s.shape, jnp.bfloat16) for s in shards]
         + [dma((count, 2)), dma((count, 8)), dma((count, 8)), dma((2,))],
         compiler_params=pltpu.CompilerParams(
-            collective_id=2, has_side_effects=True, vmem_limit_bytes=32 * 2**20
+            collective_id=2, has_side_effects=True, vmem_limit_bytes=63 * 2**20
         ),
         name="gather_weights",
     )(*shards, small)
@@ -692,207 +693,682 @@
     )(queries, key_values, q_pos, q_begin, k_pos)
 
 
-def attend_back_kernel(
-    depth,
-    q_ref,
-    grad_ref,
-    out_ref,
-    log_ref,
-    kv_all,
-    q_pos,
-    q_begin,
-    k_pos,
-    q_grad,
-    kv_grad,
-    stacked,
-    grads,
-    delta,
-    summed,
-    bias,
-    part,
-    in_core,
-    kept,
-    out_x,
-    in_x,
-    out_z,
-    in_z,
-    send_core,
-    recv_core,
-    send_x,
-    recv_x,
-    send_z,
-    recv_z,
-):
+ROW_HALVES = (("hidden", 1536, 0), ("lowered_two", 512, 1536), ("mixed_in", 1024, 2048), ("lowered", 512, 3072))
+COLUMN_HALVES = (
+    ("cotangent", 512, 0),
+    ("gate_rows", 1536, 512),
+    ("up_rows", 1536, 2048),
+    ("middle_low", 512, 3584),
+    ("query_low", 1024, 4096),
+    ("key_low", 512, 5120),
+    ("value_low", 512, 5632),
+)
+
+def back_scratch(depth, count, width, heads):
+    dma = pltpu.SemaphoreType.DMA
+    piece = SIDE // depth
+    low = jnp.bfloat16
+    wide = jnp.float32
+    return dict(
+        rows_all=pltpu.VMEM((4 * count, 3584), low),
+        cols_all=pltpu.VMEM((4 * count, 6144), low),
+        query_low=pltpu.VMEM((count, 2048), low),
+        key_low=pltpu.VMEM((count, 1024), low),
+        value_low=pltpu.VMEM((count, 1024), low),
+        kv_all=pltpu.VMEM((4 * depth * count, width), low),
+        stacked=pltpu.VMEM((heads, 2 * count, HEAD_DIM), low),
+        grads=pltpu.VMEM((heads, 2 * count, HEAD_DIM), low),
+        delta=pltpu.VMEM((heads, 2 * count), wide),
+        summed=pltpu.VMEM((heads, 2 * count, HEAD_DIM), wide),
+        bias=pltpu.VMEM((4 * count, 2 * count), wide),
+        part=pltpu.VMEM((depth, 2, 2, count, width), low),
+        kv_core=pltpu.VMEM((depth, 2, count, width), low),
+        kv_x=pltpu.VMEM((depth, count, width), low),
+        kv_z=pltpu.VMEM((depth - 1, count, width), low),
+        small_base=pltpu.VMEM((2, VECTOR_ROWS, 128), wide),
+        small_part=pltpu.VMEM((3, VECTOR_ROWS, 128), wide),
+        small_in=pltpu.VMEM((3, VECTOR_ROWS, 128), wide),
+        small_deep=pltpu.VMEM((depth - 1, VECTOR_ROWS, 128), wide),
+        out_x=pltpu.VMEM((UNITS, SIDE, PART), low),
+        in_x=pltpu.VMEM((UNITS, SIDE, PART), low),
+        in_z=pltpu.VMEM((UNITS, depth - 1, piece, PART), low),
+        done=pltpu.VMEM((UNITS, piece, PART), low),
+        load=dma((depth + 3,)),
+        send_rows=dma((4, 2)),
+        recv_rows=dma((4, 2)),
+        send_cols=dma((7, 3)),
+        recv_cols=dma((7, 3)),
+        kv_send_core=dma((depth,)),
+        kv_recv_core=dma((depth,)),
+        kv_send_x=dma((depth,)),
+        kv_recv_x=dma((depth,)),
+        kv_send_z=dma((depth - 1,)),
+        kv_recv_z=dma((depth - 1,)),
+        small_send=dma((2 + depth,)),
+        small_recv=dma((2 + depth,)),
+        send_x=dma((UNITS,)),
+        recv_x=dma((UNITS,)),
+        send_z=dma((UNITS, depth - 1)),
+        recv_z=dma((UNITS, depth - 1)),
+        send_done=dma((UNITS, depth - 1)),
+        recv_done=dma((UNITS, depth - 1)),
+        keep_done=dma((UNITS,)),
+        send_half=dma((UNITS,)),
+        recv_half=dma((UNITS,)),
+        send_core=dma((UNITS, 2)),
+        recv_core=dma((UNITS, 2)),
+    )
+
+
+def norm_back(raw, grad, gain):
+    scale = lax.rsqrt(jnp.mean(raw * raw, axis=-1, keepdims=True) + EPS)
+    gain_grad = jnp.sum(grad * raw * scale, axis=0, keepdims=True)
+    inner = grad * gain
+    kept = jnp.mean(raw * inner, axis=-1, keepdims=True)
+    return (scale * inner - raw * (scale * scale * scale * kept), gain_grad)
+
+
+def backward_kernel(depth, names, *refs):
+    r = SimpleNamespace(**dict(zip(names, refs)))
     index = lax.axis_index("ctx")
     group = lax.axis_index("fsdp")
     z, x, core = place_of(index)
-    count = q_ref.shape[0]
+    count = r.queries.shape[0]
     wide = 4 * count
-    heads = q_ref.shape[1] // HEAD_DIM // 2
+    heads = r.queries.shape[1] // HEAD_DIM // 2
+    piece = SIDE // depth
 
     def device(at_z, at_x, at_core):
         return ((at_z * 2 + at_x) * 2 + at_core, group)
 
     across = device(z, 1 - x, core)
     beside = device(z, x, 1 - core)
+    over = (index, 1 - group)
+    over_beside = (index + 1 - 2 * core, 1 - group)
     ahead = [lax.rem(z + offset, depth) for offset in range(depth)]
-    greet([device(ahead[offset], x, core) for offset in range(1, depth)] + [across, beside])
-
-    def core_copy(offset):
+    behind = [lax.rem(z + depth - offset, depth) for offset in range(depth)]
+    peers = [device(ahead[offset], x, core) for offset in range(1, depth)]
+    greet(peers + [across, beside, over, over_beside])
+
+    def half_of(ref, at, size):
+        return ref.at[:, pl.ds(pl.multiple_of(at * size, size), size)]
+
+    def rows_over(i):
+        name, size, at = ROW_HALVES[i]
+        return remote(
+            over,
+            half_of(getattr(r, name), 1 - group, size),
+            r.rows_all.at[count : 2 * count, at : at + size],
+            r.send_rows.at[i, 0],
+            r.recv_rows.at[i, 0],
+        )
+
+    def rows_beside(i):
+        name, size, at = ROW_HALVES[i]
         return remote(
             beside,
-            part.at[offset, 1 - core],
-            in_core.at[offset],
-            send_core.at[offset],
-            recv_core.at[offset],
-        )
-
-    def x_copy(offset):
+            r.rows_all.at[: 2 * count, at : at + size],
+            r.rows_all.at[2 * count :, at : at + size],
+            r.send_rows.at[i, 1],
+            r.recv_rows.at[i, 1],
+        )
+
+    def rows_start(i):
+        name, size, at = ROW_HALVES[i]
+        rows_over(i).start()
+        r.rows_all[:count, at : at + size] = half_of(getattr(r, name), group, size)[...]
+
+    def rows_pass(i):
+        rows_over(i).wait_recv()
+        rows_beside(i).start()
+
+    def columns_copy(i, which):
+        name, size, at = COLUMN_HALVES[i]
+        target = (over, beside, over_beside)[which]
+        half = core if which == 0 else 1 - core
         return remote(
-            across, out_x.at[offset], in_x.at[offset], send_x.at[offset], recv_x.at[offset]
-        )
-
-    def z_copy(offset):
+            target,
+            half_of(getattr(r, name), half, size),
+            r.cols_all.at[(which + 1) * count : (which + 2) * count, at : at + size],
+            r.send_cols.at[i, which],
+            r.recv_cols.at[i, which],
+        )
+
+    def columns_start(i):
+        name, size, at = COLUMN_HALVES[i]
+        for which in (0, 2, 1):
+            columns_copy(i, which).start()
+        r.cols_all[:count, at : at + size] = half_of(getattr(r, name), core, size)[...]
+
+    def columns_wait(i):
+        for which in range(3):
+            columns_copy(i, which).wait_recv()
+
+    def kv_load(offset):
+        part = pl.ds(pl.multiple_of(ahead[offset] * wide, wide), wide)
+        return pltpu.make_async_copy(
+            r.kv_hbm.at[part], r.kv_all.at[part], r.load.at[offset]
+        )
+
+    def weight_loads():
+        model = r.query_weight.shape[0]
+        kv = r.kv_all
+        return (
+            pltpu.make_async_copy(r.query_weight, kv.at[:model], r.load.at[depth]),
+            pltpu.make_async_copy(
+                r.key_weight, kv.at[model:, :model], r.load.at[depth + 1]
+            ),
+            pltpu.make_async_copy(
+                r.value_weight, kv.at[model:, model:], r.load.at[depth + 2]
+            ),
+        )
+
+    def kv_core_copy(offset):
+        return remote(
+            beside,
+            r.part.at[offset, 1 - core],
+            r.kv_core.at[offset],
+            r.kv_send_core.at[offset],
+            r.kv_recv_core.at[offset],
+        )
+
+    def kv_x_copy(offset):
+        return remote(
+            across,
+            r.part.at[offset, core, 1 - x],
+            r.kv_x.at[offset],
+            r.kv_send_x.at[offset],
+            r.kv_recv_x.at[offset],
+        )
+
+    def kv_z_copy(offset):
         return remote(
             device(ahead[offset], x, core),
-            out_z.at[offset],
-            in_z.at[offset - 1],
-            send_z.at[offset - 1],
-            recv_z.at[offset - 1],
-        )
-
-    for head in range(heads):
-        for turn in range(2):
-            at = (2 * head + turn) * HEAD_DIM
-            inside = slice(turn * count, (turn + 1) * count)
-            stacked[head, inside] = q_ref[:, at : at + HEAD_DIM]
-            grads[head, inside] = grad_ref[:, at : at + HEAD_DIM]
-            product = grad_ref[:, at : at + HEAD_DIM].astype(jnp.float32) * out_ref[
-                :, at : at + HEAD_DIM
-            ]
-            delta[head : head + 1, inside] = jnp.sum(product.T, axis=0, keepdims=True)
-    summed[...] = jnp.zeros_like(summed)
-
-    def stage_pairs(offset):
+            r.part.at[offset, core, x],
+            r.kv_z.at[offset - 1],
+            r.kv_send_z.at[offset - 1],
+            r.kv_recv_z.at[offset - 1],
+        )
+
+    def prepare_heads():
+        for head in range(heads):
+            for turn in range(2):
+                at = (2 * head + turn) * HEAD_DIM
+                inside = slice(turn * count, (turn + 1) * count)
+                grad = r.heads_grad[:, at : at + HEAD_DIM]
+                r.stacked[head, inside] = r.queries[:, at : at + HEAD_DIM]
+                r.grads[head, inside] = grad
+                product = grad.astype(jnp.float32) * r.heads_out[:, at : at + HEAD_DIM]
+                r.delta[head : head + 1, inside] = jnp.sum(product.T, axis=0, keepdims=True)
+        r.summed[...] = jnp.zeros_like(r.summed)
+
+    def attend_pairs(offset):
+        kv_load(offset).wait()
         first = pl.multiple_of(ahead[offset] * wide, wide)
-        place = k_pos[pl.ds(first, wide), :]
-        allowed = (place >= q_begin[...]) & (place <= q_pos[...])
-        bias[...] = jnp.where(allowed, 0.0, NEG)
+        place = r.k_pos[pl.ds(first, wide), :]
+        allowed = (place >= r.q_begin[...]) & (place <= r.q_pos[...])
+        r.bias[...] = jnp.where(allowed, 0.0, NEG)
 
         def one(head, carry):
             at = pl.multiple_of(head * HEAD_DIM, HEAD_DIM)
             at_v = pl.multiple_of((heads + head) * HEAD_DIM, HEAD_DIM)
-            keys = kv_all[pl.ds(first, wide), pl.ds(at, HEAD_DIM)]
-            values = kv_all[pl.ds(first, wide), pl.ds(at_v, HEAD_DIM)]
+            keys = r.kv_all[pl.ds(first, wide), pl.ds(at, HEAD_DIM)]
+            values = r.kv_all[pl.ds(first, wide), pl.ds(at_v, HEAD_DIM)]
+            query = r.stacked[head]
+            grad = r.grads[head]
             scores = lax.dot_general(
-                keys, stacked[head], (((1,), (1,)), ((), ())), preferred_element_type=jnp.float32
+                keys, query, (((1,), (1,)), ((), ())), preferred_element_type=jnp.float32
             )
-            weights = jnp.exp(scores + bias[...] - log_ref[pl.ds(head, 1), :])
+            weights = jnp.exp(scores + r.bias[...] - r.logs[pl.ds(head, 1), :])
             weight_grad = lax.dot_general(
-                values, grads[head], (((1,), (1,)), ((), ())), preferred_element_type=jnp.float32
+                values, grad, (((1,), (1,)), ((), ())), preferred_element_type=jnp.float32
             )
-            score_grad = (weights * (weight_grad - delta[pl.ds(head, 1), :])).astype(jnp.bfloat16)
-            key_term = jnp.dot(
-                score_grad, stacked[head], preferred_element_type=jnp.float32
-            ).astype(jnp.bfloat16)
+            score_grad = (weights * (weight_grad - r.delta[pl.ds(head, 1), :])).astype(
+                jnp.bfloat16
+            )
+            key_term = jnp.dot(score_grad, query, preferred_element_type=jnp.float32)
             value_term = jnp.dot(
-                weights.astype(jnp.bfloat16), grads[head], preferred_element_type=jnp.float32
-            ).astype(jnp.bfloat16)
+                weights.astype(jnp.bfloat16), grad, preferred_element_type=jnp.float32
+            )
             for at_x in range(2):
                 for at_core in range(2):
                     inside = slice((at_x * 2 + at_core) * count, (at_x * 2 + at_core + 1) * count)
-                    part[offset, at_core, at_x, :, pl.ds(at, HEAD_DIM)] = key_term[inside]
-                    part[offset, at_core, at_x, :, pl.ds(at_v, HEAD_DIM)] = value_term[inside]
-            summed[head] = summed[head] + lax.dot_general(
+                    part = r.part.at[offset, at_core, at_x]
+                    part[:, pl.ds(at, HEAD_DIM)] = key_term[inside].astype(jnp.bfloat16)
+                    part[:, pl.ds(at_v, HEAD_DIM)] = value_term[inside].astype(jnp.bfloat16)
+            r.summed[head] = r.summed[head] + lax.dot_general(
                 score_grad, keys, (((0,), (0,)), ((), ())), preferred_element_type=jnp.float32
             )
             return carry
 
         lax.fori_loop(0, heads, one, 0)
-        core_copy(offset).start()
-
-    def stage_core(offset):
-        core_copy(offset).wait_recv()
-        out_x[offset] = (
-            part[offset, core, 1 - x].astype(jnp.float32)
-            + in_core[offset, 1 - x].astype(jnp.float32)
-        ).astype(jnp.bfloat16)
-        x_copy(offset).start()
-        kept[offset] = part[offset, core, x].astype(jnp.float32) + in_core[offset, x].astype(
+        kv_core_copy(offset).start()
+
+    def attend_core(offset):
+        kv_core_copy(offset).wait_recv()
+        for far in (True, False):
+            at_x = 1 - x if far else x
+            total = r.part[offset, core, at_x].astype(jnp.float32) + r.kv_core[
+                offset, at_x
+            ].astype(jnp.float32)
+            r.part[offset, core, at_x] = total.astype(jnp.bfloat16)
+            if far:
+                kv_x_copy(offset).start()
+
+    def attend_across(offset):
+        kv_x_copy(offset).wait_recv()
+        total = r.part[offset, core, x].astype(jnp.float32) + r.kv_x[offset].astype(
             jnp.float32
         )
-
-    def stage_across(offset):
-        x_copy(offset).wait_recv()
-        total = kept[offset] + in_x[offset].astype(jnp.float32)
+        r.part[offset, core, x] = total.astype(jnp.bfloat16)
         if offset:
-            out_z[offset] = total.astype(jnp.bfloat16)
-            z_copy(offset).start()
-        else:
-            kept[0] = total
+            kv_z_copy(offset).start()
+
+    def head_back(raw, grad, gain):
+        turned = grad * r.cosine[...] + pltpu.roll(grad, HEAD_DIM // 2, 1) * r.sine[...]
+        return norm_back(raw, turned, gain)
+
+    def vector_store(query_gain_grad, key_gain_grad):
+        half = HEAD_DIM // 2
+        for at in range(2):
+            inside = slice(at * half, (at + 1) * half)
+            r.small_base[at, 8:9, :] = jnp.concatenate(
+                [query_gain_grad[:, inside], key_gain_grad[:, inside]], axis=1
+            )
+
+    def query_end():
+        for load in weight_loads():
+            load.start()
+        r.small_base[...] = r.small[...]
+        total = jnp.zeros((1, HEAD_DIM), jnp.float32)
+        for head in range(heads):
+            for turn in range(2):
+                at = (2 * head + turn) * HEAD_DIM
+                grad = r.summed[head, turn * count : (turn + 1) * count] * HEAD_DIM ** (-0.5)
+                raw = r.query_raw[:, at : at + HEAD_DIM]
+                result, gain_grad = head_back(raw, grad, r.query_gain[...])
+                r.query_low[:, at : at + HEAD_DIM] = result.astype(jnp.bfloat16)
+                total = total + gain_grad
+        r.delta[0:1, :HEAD_DIM] = total
+        columns_start(4)
+
+    def key_end():
+        total = jnp.zeros((1, HEAD_DIM), jnp.float32)
+        for offset in range(1, depth):
+            kv_z_copy(offset).wait_recv()
+
+        def sum_at(at):
+            part = r.part[0, core, x, :, at : at + HEAD_DIM].astype(jnp.float32)
+            for offset in range(1, depth):
+                part = part + r.kv_z[offset - 1, :, at : at + HEAD_DIM].astype(jnp.float32)
+            return part
+
+        for head in range(heads):
+            at = head * HEAD_DIM
+            raw = r.key_raw[:, at : at + HEAD_DIM]
+            result, gain_grad = head_back(raw, sum_at(at), r.key_gain[...])
+            r.key_low[:, at : at + HEAD_DIM] = result.astype(jnp.bfloat16)
+            total = total + gain_grad
+            r.value_low[:, at : at + HEAD_DIM] = sum_at((heads + head) * HEAD_DIM).astype(
+                jnp.bfloat16
+            )
+        columns_start(5)
+        columns_start(6)
+        vector_store(r.delta[0:1, :HEAD_DIM], total)
+
+    def token_end():
+        for load in weight_loads():
+            load.wait()
+        model = r.query_weight.shape[0]
+
+        def one(block, carry):
+            first = pl.multiple_of(block * 128, 128)
+            near = pl.ds(first, 128)
+            far = pl.ds(pl.multiple_of(model + block * 128, 128), 128)
+
+            def term(low, weight):
+                return lax.dot_general(
+                    low, weight, (((1,), (1,)), ((), ())), preferred_element_type=jnp.float32
+                )
+
+            r.summed[block, :count] = (
+                r.lowered_part[:, near]
+                + term(r.query_low[...], r.kv_all[near])
+                + term(r.key_low[...], r.kv_all[far, :model])
+                + term(r.value_low[...], r.kv_all[far, model:])
+            )
+            return carry
+
+        lax.fori_loop(0, model // 128, one, 0)
+        grad = jnp.concatenate([r.summed[at, :count] for at in range(model // 128)], axis=1)
+        result, gain_grad = norm_back(
+            r.tokens[...].astype(jnp.float32), grad, r.attention_gain[...]
+        )
+        r.token_grad[...] = (r.middle_grad[...] + result).astype(jnp.bfloat16)
+        for at in range(model // 128):
+            half = at // (model // 256)
+            row = at % (model // 256)
+            r.small_base[half, row : row + 1, :] = gain_grad[:, at * 128 : (at + 1) * 128]
+
+    def product(unit, half):
+        a, g = unit_blocks(unit)
+        left = block_of(r.rows_all, a, SIDE)
+        right = block_of(r.cols_all, g * 2 + half, PART)
+        return lax.dot_general(
+            left, right, (((0,), (0,)), ((), ())), preferred_element_type=jnp.float32
+        )
+
+    def rows_at(at_z):
+        return pl.ds(pl.multiple_of(at_z * piece, piece), piece)
+
+    def columns_at(at_x, at_core):
+        return pl.ds(pl.multiple_of((at_core * 2 + at_x) * PART, PART), PART)
+
+    def x_copy(unit):
+        return remote(
+            across,
+            r.out_x.at[unit],
+            r.in_x.at[unit],
+            r.send_x.at[unit],
+            r.recv_x.at[unit],
+        )
+
+    def z_copy(unit, offset):
+        return remote(
+            device(ahead[offset], x, core),
+            r.in_x.at[unit, rows_at(ahead[offset])],
+            r.in_z.at[unit, offset - 1],
+            r.send_z.at[unit, offset - 1],
+            r.recv_z.at[unit, offset - 1],
+        )
+
+    def done_copy(unit, offset, at_z):
+        return remote(
+            device(ahead[offset], x, core),
+            r.done.at[unit],
+            r.units.at[unit, rows_at(at_z), columns_at(x, core)],
+            r.send_done.at[unit, offset - 1],
+            r.recv_done.at[unit, offset - 1],
+        )
+
+    def keep_copy(unit):
+        return pltpu.make_async_copy(
+            r.done.at[unit],
+            r.units.at[unit, rows_at(z), columns_at(x, core)],
+            r.keep_done.at[unit],
+        )
+
+    def half_copy(unit, at_x):
+        part = r.units.at[unit, :, columns_at(at_x, core)]
+        return remote(across, part, part, r.send_half.at[unit], r.recv_half.at[unit])
+
+    def core_copy(unit, which, at_x, at_core):
+        part = r.units.at[unit, :, columns_at(at_x, at_core)]
+        return remote(
+            beside, part, part, r.send_core.at[unit, which], r.recv_core.at[unit, which]
+        )
+
+    def stage_send(unit):
+        r.out_x[unit] = product(unit, 1 - x).astype(jnp.bfloat16)
+        x_copy(unit).start()
+
+    def stage_pair(unit):
+        own = product(unit, x)
+        x_copy(unit).wait_recv()
+        r.in_x[unit] = (own + r.in_x[unit].astype(jnp.float32)).astype(jnp.bfloat16)
+        for offset in range(1, depth):
+            z_copy(unit, offset).start()
+
+    def stage_total(unit):
+        total = r.in_x[unit, rows_at(z)].astype(jnp.float32)
+        for offset in range(1, depth):
+            z_copy(unit, offset).wait_recv()
+            total = total + r.in_z[unit, offset - 1].astype(jnp.float32)
+        r.done[unit] = total.astype(jnp.bfloat16)
+        for offset in range(1, depth):
+            done_copy(unit, offset, z).start()
+        keep_copy(unit).start()
+
+    def stage_half(unit):
+        keep_copy(unit).wait()
+        for offset in range(1, depth):
+            done_copy(unit, offset, behind[offset]).wait_recv()
+        half_copy(unit, x).start()
+        core_copy(unit, 0, x, core).start()
+
+    def stage_core(unit):
+        half_copy(unit, 1 - x).wait_recv()
+        core_copy(unit, 1, 1 - x, core).start()
+
+    def stage_end(unit):
+        core_copy(unit, 0, x, 1 - core).wait_recv()
+        core_copy(unit, 1, 1 - x, 1 - core).wait_recv()
+        x_copy(unit).wait_send()
+        for offset in range(1, depth):
+            z_copy(unit, offset).wait_send()
+            done_copy(unit, offset, z).wait_send()
+        half_copy(unit, x).wait_send()
+        core_copy(unit, 0, x, core).wait_send()
+        core_copy(unit, 1, 1 - x, core).wait_send()
+
+    def small_copy(at, target, source):
+        return remote(
+            target, source, r.small_in.at[at], r.small_send.at[at], r.small_recv.at[at]
+        )
+
+    def small_over():
+        return small_copy(0, over, r.small_base.at[1 - group])
+
+    def small_along(offset):
+        return remote(
+            device(ahead[offset], x, core),
+            r.small_part.at[2],
+            r.small_deep.at[offset - 1],
+            r.small_send.at[2 + offset],
+            r.small_recv.at[2 + offset],
+        )
+
+    def small_beside():
+        small_over().wait()
+        r.small_part[0] = r.small_base[group] + r.small_in[0]
+        small_copy(1, beside, r.small_part.at[0]).start()
+
+    def small_across():
+        small_copy(1, beside, r.small_part.at[0]).wait()
+        r.small_part[1] = r.small_part[0] + r.small_in[1]
+        small_copy(2, across, r.small_part.at[1]).start()
+
+    def small_spread():
+        small_copy(2, across, r.small_part.at[1]).wait()
+        r.small_part[2] = r.small_part[1] + r.small_in[2]
+        for offset in range(1, depth):
+            small_along(offset).start()
+
+    def small_end():
+        total = r.small_part[2]
+        for offset in range(1, depth):
+            small_along(offset).wait()
+            total = total + r.small_deep[offset - 1]
+        r.small_out[...] = total
 
     order = tuple(range(1, depth)) + (0,)
-    stages = (stage_pairs, stage_core, stage_across)
-    for step in range(depth + len(stages) - 1):
+    for offset in order:
+        kv_load(offset).start()
+    rows_start(0)
+    columns_start(0)
+    prepare_heads()
+
+    def at_steps(step, calls):
+        for at, call in calls:
+
+            @pl.when(step == at)
+            def run(call=call):
+                call()
+
+    lead = 1
+    early = [(at, partial(attend_pairs, order[at])) for at in range(depth)]
+    early += [(at + 1, partial(attend_core, order[at])) for at in range(depth)]
+    early += [(at + 2, partial(attend_across, order[at])) for at in range(depth)]
+    early += [
+        (0, partial(rows_start, 1)),
+        (0, partial(columns_start, 1)),
+        (2, partial(columns_start, 2)),
+        (3, partial(rows_start, 2)),
+        (3, partial(columns_start, 3)),
+        (3, partial(rows_start, 3)),
+        (depth, query_end),
+        (depth + 2, key_end),
+        (depth + 3, token_end),
+        (depth + 4, lambda: small_over().start()),
+        (depth + 6, small_beside),
+        (depth + 7, small_across),
+        (depth + 8, small_spread),
+        (depth + 10, small_end),
+    ]
+    early += [(lead + 0 - 1, partial(rows_pass, 0))]
+    early += [(lead + 3 - 1, partial(rows_pass, 1))]
+    early += [(lead + 9 - 1, partial(rows_pass, 2))]
+    early += [(lead + 11 - 1, partial(rows_pass, 3))]
+    before = [(lead + 0, partial(columns_wait, 0)), (lead + 0, lambda: rows_beside(0).wait_recv())]
+    before += [(lead + 3, partial(columns_wait, 1)), (lead + 3, lambda: rows_beside(1).wait_recv())]
+    before += [(lead + 6, partial(columns_wait, 2))]
+    before += [(lead + 9, partial(columns_wait, 3)), (lead + 9, lambda: rows_beside(2).wait_recv())]
+    before += [
+        (lead + 11, partial(columns_wait, 4)),
+        (lead + 11, lambda: rows_beside(3).wait_recv()),
+        (lead + 13, partial(columns_wait, 5)),
+        (lead + 14, partial(columns_wait, 6)),
+    ]
+    stages = (stage_pair, stage_total, stage_half, stage_core, stage_end)
+
+    def stage_at(step, late, stage):
+        unit = step - lead - late
+
+        @pl.when((unit >= 0) & (unit < UNITS))
+        def run():
+            stage(unit)
+
+    def body(step, carry):
+        at_steps(step, before)
+        stage_at(step, 0, stage_send)
+        at_steps(step, early)
         for late, stage in enumerate(stages):
-            if 0 <= step - late < depth:
-                stage(order[step - late])
-    for head in range(heads):
-        for turn in range(2):
-            at = (2 * head + turn) * HEAD_DIM
-            q_grad[:, at : at + HEAD_DIM] = summed[head, turn * count : (turn + 1) * count]
-    total = kept[0]
-    for offset in range(1, depth):
-        z_copy(offset).wait_recv()
-        total = total + in_z[offset - 1].astype(jnp.float32)
-    kv_grad[...] = total
+            stage_at(step, late + 1, stage)
+        return carry
+
+    lax.fori_loop(0, UNITS + lead + len(stages), body, 0)
+    for i in range(len(ROW_HALVES)):
+        rows_over(i).wait_send()
+        rows_beside(i).wait_send()
+    for i in range(len(COLUMN_HALVES)):
+        for which in range(3):
+            columns_copy(i, which).wait_send()
     for offset in range(depth):
-        core_copy(offset).wait_send()
-        x_copy(offset).wait_send()
+        kv_core_copy(offset).wait_send()
+        kv_x_copy(offset).wait_send()
         if offset:
-            z_copy(offset).wait_send()
-
-
-def attend_back(queries, grads, outs, logs, kv_all, q_pos, q_begin, k_pos):
+            kv_z_copy(offset).wait_send()
+
+
+def backward(near, far):
     depth = lax.axis_size("ctx") // 4
-    count = queries.shape[0]
-    heads = queries.shape[1] // HEAD_DIM // 2
-    width = kv_all.shape[1]
+    count, width = near["queries"].shape
+    heads = width // HEAD_DIM // 2
+    scratch = back_scratch(depth, count, far["kv_hbm"].shape[1], heads)
+    outputs = dict(
+        units=jax.ShapeDtypeStruct((UNITS, SIDE, 2 * SIDE), jnp.bfloat16),
+        token_grad=jax.ShapeDtypeStruct(near["tokens"].shape, jnp.bfloat16),
+        small_out=jax.ShapeDtypeStruct((VECTOR_ROWS, 128), jnp.float32),
+    )
+    vmem = pl.BlockSpec(memory_space=pltpu.VMEM)
+    hbm = pl.BlockSpec(memory_space=pl.ANY)
+    names = tuple(near) + tuple(far) + tuple(outputs) + tuple(scratch)
+    return pl.pallas_call(
+        partial(backward_kernel, depth, names),
+        out_shape=list(outputs.values()),
+        in_specs=[vmem] * len(near) + [hbm] * len(far),
+        out_specs=[hbm, vmem, vmem],
+        scratch_shapes=list(scratch.values()),
+        compiler_params=pltpu.CompilerParams(
+            collective_id=4, has_side_effects=True, vmem_limit_bytes=63 * 2**20
+        ),
+        name="backward",
+    )(*near.values(), *far.values())
+
+
+def widen_kernel(places, *refs):
+    units = refs[0]
+    outs = refs[1 : len(refs) - 4]
+    held, wide, load, store = refs[len(refs) - 4 :]
+    slots = held.shape[0]
+
+    def load_copy(unit):
+        return pltpu.make_async_copy(units.at[unit], held.at[unit % slots], load.at[unit])
+
+    def stores(unit):
+        which, block, blocks, under = places[unit]
+        out = outs[which]
+        source = wide.at[unit % slots]
+        if under:
+            inside = out.at[block * SIDE : (block + 1) * SIDE]
+            return [pltpu.make_async_copy(source, inside, store.at[unit, 0])]
+        return [
+            pltpu.make_async_copy(
+                source.at[:, core * SIDE : (core + 1) * SIDE],
+                out.at[:, (core * blocks + block) * SIDE : (core * blocks + block + 1) * SIDE],
+                store.at[unit, core],
+            )
+            for core in range(2)
+        ]
+
+    for unit in range(slots):
+        load_copy(unit).start()
+    for unit in range(UNITS):
+        load_copy(unit).wait()
+        if unit >= slots:
+            for copy in stores(unit - slots):
+                copy.wait()
+        slot = unit % slots
+
+        def one(step, carry, slot=slot):
+            rows = pl.ds(pl.multiple_of(step * 32, 32), 32)
+            wide[slot, rows] = held[slot, rows].astype(jnp.float32)
+            return carry
+
+        lax.fori_loop(0, SIDE // 32, one, 0)
+        for copy in stores(unit):
+            copy.start()
+        if unit + slots < UNITS:
+            load_copy(unit + slots).start()
+    for unit in range(UNITS - slots, UNITS):
+        for copy in stores(unit):
+            copy.wait()
+
+
+def widen(units, layout):
+    places = []
+    shapes = []
+    for which, (blocks, under) in enumerate(layout):
+        places += [(which, block, blocks, under) for block in range(blocks)]
+        shape = (blocks * SIDE, 2 * SIDE) if under else (SIDE, blocks * 2 * SIDE)
+        shapes.append(jax.ShapeDtypeStruct(shape, jnp.float32))
+    slots = 4
     dma = pltpu.SemaphoreType.DMA
-    vmem = pl.BlockSpec(memory_space=pltpu.VMEM)
+    hbm = pl.BlockSpec(memory_space=pl.ANY)
     return pl.pallas_call(
-        partial(attend_back_kernel, depth),
-        out_shape=[
-            jax.ShapeDtypeStruct(queries.shape, jnp.float32),
-            jax.ShapeDtypeStruct((count, width), jnp.float32),
+        partial(widen_kernel, tuple(places)),
+        out_shape=shapes,
+        in_specs=[hbm],
+        out_specs=[hbm] * len(shapes),
+        scratch_shapes=[
+            pltpu.VMEM((slots, SIDE, 2 * SIDE), jnp.bfloat16),
+            pltpu.VMEM((slots, SIDE, 2 * SIDE), jnp.float32),
+            dma((UNITS,)),
+            dma((UNITS, 2)),
         ],
-        in_specs=[vmem] * 8,
-        out_specs=[vmem] * 2,
-        scratch_shapes=[
-            pltpu.VMEM((heads, 2 * count, HEAD_DIM), jnp.bfloat16),
-            pltpu.VMEM((heads, 2 * count, HEAD_DIM), jnp.bfloat16),
-            pltpu.VMEM((heads, 2 * count), jnp.float32),
-            pltpu.VMEM((heads, 2 * count, HEAD_DIM), jnp.float32),
-            pltpu.VMEM((4 * count, 2 * count), jnp.float32),
-            pltpu.VMEM((depth, 2, 2, count, width), jnp.bfloat16),
-            pltpu.VMEM((depth, 2, count, width), jnp.bfloat16),
-            pltpu.VMEM((depth, count, width), jnp.float32),
-            pltpu.VMEM((depth, count, width), jnp.bfloat16),
-            pltpu.VMEM((depth, count, width), jnp.bfloat16),
-            pltpu.VMEM((depth, count, width), jnp.bfloat16),
-            pltpu.VMEM((depth - 1, count, width), jnp.bfloat16),
-            dma((depth,)),
-            dma((depth,)),
-            dma((depth,)),
-            dma((depth,)),
-            dma((depth - 1,)),
-            dma((depth - 1,)),
-        ],
-        compiler_params=pltpu.CompilerParams(
-            collective_id=4, has_side_effects=True, vmem_limit_bytes=56 * 2**20
-        ),
-        name="attend_back",
-    )(queries, grads, outs, logs, kv_all, q_pos, q_begin, k_pos)
+        compiler_params=pltpu.CompilerParams(vmem_limit_bytes=63 * 2**20),
+        name="widen",
+    )(units)
 
 
 def swap(value, axis, stride):
@@ -1080,62 +1556,128 @@
     headgate_weight_grad = jnp.einsum(
         "td,th->dh", lowered, logit_grad, preferred_element_type=jnp.float32
     )
+    headgate_part = headgate_weight_grad.reshape((2, -1))
     if near:
-        query_grad, kv_grad = attend_back(
-            queries.reshape(count, -1),
-            heads_grad.reshape(count, -1),
-            heads_flat,
-            log_total,
-            kv_all,
-            jnp.tile(q_pos, 2)[None, :],
-            jnp.tile(q_begin, 2)[None, :],
-            place_all[:, None],
-        )
-        key_grad = kv_grad[:, : KV_HEADS * HEAD_DIM].reshape(count, KV_HEADS, HEAD_DIM)
-        value_grad = kv_grad[:, KV_HEADS * HEAD_DIM :].reshape(count, KV_HEADS, HEAD_DIM)
-    else:
-        out_grad = heads_grad.reshape(count, KV_HEADS, groups, HEAD_DIM)
-        delta = jnp.sum(
-            out_grad.astype(jnp.float32) * heads_out.reshape(count, KV_HEADS, groups, HEAD_DIM), axis=-1
-        ).transpose(1, 2, 0)
-        cycle_size = lax.axis_size("ctx")
-        my_index = lax.axis_index("ctx")
-
-        def cycle_step(step, carry):
-            pair_piece, grad_piece, query_sum = carry
-            anchor = lax.rem(my_index - step + cycle_size, cycle_size)
-            key_pos, key_seg = slices(anchor * count, count)
-            allowed = allowed_pairs(my_pos, my_seg, key_pos, key_seg)
-            key_heads = pair_piece[0].reshape(count, KV_HEADS, HEAD_DIM)
-            value_heads = pair_piece[1].reshape(count, KV_HEADS, HEAD_DIM)
-            score_grad, weights = pair_terms(
-                queries, out_grad, log_total, delta, key_heads, value_heads, allowed
-            )
-            key_term = jnp.einsum(
-                "kgts,tkgd->skd", score_grad, queries, preferred_element_type=jnp.float32
-            ).reshape(count, KV_HEADS * HEAD_DIM)
-            value_term = jnp.einsum(
-                "kgts,tkgd->skd", weights, out_grad, preferred_element_type=jnp.float32
-            ).reshape(count, KV_HEADS * HEAD_DIM)
-            query_sum, grad_piece = (
-                query_sum
-                + jnp.einsum(
-                    "kgts,skd->tkgd", score_grad, key_heads, preferred_element_type=jnp.float32
-                ),
-                grad_piece + jnp.stack([key_term, value_term]),
-            )
-            pair_piece = from_behind(pair_piece, "ctx", 1)
-            grad_piece = from_behind(grad_piece.astype(jnp.bfloat16), "ctx", 1).astype(grad_piece.dtype)
-            return (pair_piece, grad_piece, query_sum)
-
-        cycle_start = (
-            jnp.stack([keys, values]),
-            jnp.zeros((2, count, KV_HEADS * HEAD_DIM), jnp.float32),
-            jnp.zeros((count, KV_HEADS, groups, HEAD_DIM), jnp.float32),
-        )
-        last_pair, home_grads, query_grad = lax.fori_loop(0, cycle_size, cycle_step, cycle_start)
-        key_grad = home_grads[0].reshape(count, KV_HEADS, HEAD_DIM)
-        value_grad = home_grads[1].reshape(count, KV_HEADS, HEAD_DIM)
+        zero = jnp.zeros((512,), jnp.float32)
+        small = jnp.stack(
+            [
+                pack_rows(
+                    [zero[:512], gain_two_grad.reshape(2, -1)[half], zero[:128], headgate_part[half]],
+                    VECTOR_ROWS,
+                )
+                for half in (0, 1)
+            ]
+        )
+        logit_part = jnp.einsum(
+            "th,dh->td", logit_grad, headgate_full, preferred_element_type=jnp.float32
+        )
+        units, token_grad, small_total = backward(
+            dict(
+                queries=queries.reshape(count, -1),
+                heads_grad=heads_grad.reshape(count, -1),
+                heads_out=heads_flat,
+                logs=log_total,
+                q_pos=jnp.tile(q_pos, 2)[None, :],
+                q_begin=jnp.tile(q_begin, 2)[None, :],
+                k_pos=place_all[:, None],
+                query_raw=query_raw,
+                key_raw=key_raw,
+                cosine=jnp.concatenate([cosine[:, 0], cosine[:, 0]], axis=1),
+                sine=jnp.concatenate([sine[:, 0], -sine[:, 0]], axis=1),
+                query_gain=gain_query[None, :],
+                key_gain=gain_key[None, :],
+                cotangent=upstream_low,
+                hidden=hidden,
+                lowered_two=lowered_two,
+                gate_rows=gate_rows,
+                up_rows=up_rows,
+                mixed_in=mixed_in,
+                middle_low=middle_low,
+                lowered=lowered,
+                tokens=tokens[0],
+                middle_grad=middle_grad,
+                attention_gain=gain_one[None, :],
+                lowered_part=logit_part,
+                small=small,
+            ),
+            dict(
+                kv_hbm=kv_all,
+                query_weight=query_full,
+                key_weight=key_full,
+                value_weight=value_full,
+            ),
+        )
+        totals = unpack_rows(small_total, vector_shapes)
+        down, gate, up, out, query, key, value = widen(
+            units,
+            (
+                (3, True),
+                (3, False),
+                (3, False),
+                (2, True),
+                (2, False),
+                (1, False),
+                (1, False),
+            ),
+        )
+        return (
+            mixed,
+            token_grad[None],
+            totals[0],
+            query,
+            key,
+            value,
+            totals[4],
+            totals[2],
+            totals[3],
+            out,
+            totals[1],
+            gate,
+            up,
+            down,
+        )
+    out_grad = heads_grad.reshape(count, KV_HEADS, groups, HEAD_DIM)
+    delta = jnp.sum(
+        out_grad.astype(jnp.float32) * heads_out.reshape(count, KV_HEADS, groups, HEAD_DIM), axis=-1
+    ).transpose(1, 2, 0)
+    cycle_size = lax.axis_size("ctx")
+    my_index = lax.axis_index("ctx")
+
+    def cycle_step(step, carry):
+        pair_piece, grad_piece, query_sum = carry
+        anchor = lax.rem(my_index - step + cycle_size, cycle_size)
+        key_pos, key_seg = slices(anchor * count, count)
+        allowed = allowed_pairs(my_pos, my_seg, key_pos, key_seg)
+        key_heads = pair_piece[0].reshape(count, KV_HEADS, HEAD_DIM)
+        value_heads = pair_piece[1].reshape(count, KV_HEADS, HEAD_DIM)
+        score_grad, weights = pair_terms(
+            queries, out_grad, log_total, delta, key_heads, value_heads, allowed
+        )
+        key_term = jnp.einsum(
+            "kgts,tkgd->skd", score_grad, queries, preferred_element_type=jnp.float32
+        ).reshape(count, KV_HEADS * HEAD_DIM)
+        value_term = jnp.einsum(
+            "kgts,tkgd->skd", weights, out_grad, preferred_element_type=jnp.float32
+        ).reshape(count, KV_HEADS * HEAD_DIM)
+        query_sum, grad_piece = (
+            query_sum
+            + jnp.einsum(
+                "kgts,skd->tkgd", score_grad, key_heads, preferred_element_type=jnp.float32
+            ),
+            grad_piece + jnp.stack([key_term, value_term]),
+        )
+        pair_piece = from_behind(pair_piece, "ctx", 1)
+        grad_piece = from_behind(grad_piece.astype(jnp.bfloat16), "ctx", 1).astype(grad_piece.dtype)
+        return (pair_piece, grad_piece, query_sum)
+
+    cycle_start = (
+        jnp.stack([keys, values]),
+        jnp.zeros((2, count, KV_HEADS * HEAD_DIM), jnp.float32),
+        jnp.zeros((count, KV_HEADS, groups, HEAD_DIM), jnp.float32),
+    )
+    last_pair, home_grads, query_grad = lax.fori_loop(0, cycle_size, cycle_step, cycle_start)
+    key_grad = home_grads[0].reshape(count, KV_HEADS, HEAD_DIM)
+    value_grad = home_grads[1].reshape(count, KV_HEADS, HEAD_DIM)
     query_raw_grad, query_gain_grad = query_back(query_grad.reshape(count, HEADS, HEAD_DIM))
     key_raw_grad, key_gain_grad = key_back(key_grad)
     query_low = query_raw_grad.astype(jnp.bfloat16).reshape(count, -1)

time: 736 us -> 512 us (0.70); the launches traced: 726 us -> 512 us
  local copies, waits for them, and re-layouts: 113 us -> 21.1 us
  waiting for transfers between devices: 55.7 us -> 0 us
  other arithmetic: 64.3 us -> 9.55 us
  matrix products: 51.1 us -> 27.2 us
  Pallas kernels: 437 us -> 452 us
    ppermute x4 -> x0, waiting for transfers between devices: 55.7 us -> none  [swap(): return lax.ppermute(value, axis, [(i, i ^ stride) for i in range(count)])]
    unnamed x239 -> x85, local copies, waits for them, and re-layouts: 35.3 us -> 9.68 us
    concatenate x5 -> x2, other arithmetic: 21.9 us -> 0.77 us  [the longest x1 0.76 us: per_device(): jnp.concatenate([cosine[:, 0], cosine[:, 0]], axis=1)]
    reshape x10 -> x0, local copies, waits for them, and re-layouts: 20.8 us -> none  [the longest x6 15.6 us: gather_tokens(): b.reshape(count, -1, 2, SIDE)]
    convert_element_type x7 -> x0, other arithmetic: 19.2 us -> none  [the longest x3 9.55 us: beside_blocks(): jnp.concatenate([units[i] for i in range(units.shape[0])], axis=1)]
    pallas_call x2, Pallas kernels: 285 us -> 299 us  [the longest x1 283 us: backward(): pl.pallas_call(partial(backward_kernel, depth, names), out_shape=list(out...]
    dot_general x2 -> x0, local copies, waits for them, and re-layouts: 10.4 us -> none  [the longest x1 6.43 us: per_device(): query_raw = jnp.dot(lowered, query_full, preferred_element_type=jnp.float32)]
    slice x13 -> x5, local copies, waits for them, and re-layouts: 9.09 us -> 0.26 us  [the longest x3 0.26 us: per_device(): headgate_part[half]]
  transfers between devices with their start and end apart: 4 -> 0, of which waited for: 2 -> 0; matrix products, arithmetic and copies ran while one was open for 7% -> 0% of each run, Pallas kernels for 0% -> 0%
where the time goes in v4:
time: 512 us
  Pallas kernels  452 us (88%)
  matrix products  27.2 us (5%)
  local copies, waits for them, and re-layouts  21.1 us (4%)
  other arithmetic  9.55 us (2%)
    pallas_call x1, Pallas kernels, backward(): pl.pallas_call(partial(backward_kernel, depth, names), out_shape=list(out...  283 us
    pallas_call x1, Pallas kernels, gather_weights(): pl.pallas_call(partial(gather_kernel, count), out_shape=[jax.ShapeDtypeSt...  83.2 us
    pallas_call x1, Pallas kernels, attend(): pl.pallas_call(partial(attend_kernel, depth), out_shape=[jax.ShapeDtypeSt...  70.5 us
    pallas_call x1, Pallas kernels, widen(): pl.pallas_call(partial(widen_kernel, tuple(places)), out_shape=shapes, in...  15.9 us

profile of v4, /device:TPU:0, one launch (start us, length us, event | category | flops | bytes accessed | tf_op | source)
XLA Modules:
  0.0 511.7 jit_solution(13461423352516934776)
XLA Ops:
  0.6 0.8 copy.82
  1.6 2.8 concatenate.100
  4.4 0.6 pad_bitcast_fusion.2.refs_7_
  5.0 83.2 %gather_weights.1 = (bf16[1024,2048]{1,0:T(8,128)(2,1)}, bf16[1024,1024]{1,0:T(8,128)(2,1)}, bf16[1024,1024]{1,0:T(8,128)(2,1)}, bf16[2048,1024]{1,0:T(8,128)(2,...) custom-call(bf16[512,2048]{1,0:T(8,128)(2,1)} %refs_0_.1, ...), custom_call_target="tpu_custom_call" | custom-call | tf_op jit(solution)/shard_map/gather_weights/pallas_call | solution.py:224
  88.3 0.8 slice_bitcast_fusion.1
  89.0 0.6 slice_bitcast_fusion.10
  89.7 1.3 slice_bitcast_fusion.8
  91.0 0.6 maximum_convert_fusion.1
  91.9 3.0 fusion.32.refs_7_
  95.2 0.3 multiply_reduce_fusion
  95.6 0.4 copy-done.7
  96.0 0.3 multiply_multiply_fusion
  96.7 0.5 fusion.25
  97.5 0.4 multiply_subtract_fusion
  97.9 0.3 fusion.8
  98.4 2.3 convolution_convert_fusion
  100.8 0.4 fusion.33.refs_8_
  102.8 70.5 %attend.1 = (f32[128,2048]{1,0:T(8,128)S(1)}, f32[8,256]{1,0:T(8,128)S(1)}, bf16[2048,2048]{1,0:T(8,128)(2,1)S(1)}) custom-call(bf16[128,2048]{1,0:T(8,128)(2,1)S(1)} %bitcast.120, bf16[128,2048]{1,0:T(8,128)(2,1)S(1)} %pad_maximum_fusion.kv_ref, s32[128,1]{1,0:T(8,128)S(1)} %copy.87.q_pos, s32[128,1]{1,0:T(8,128)S(1)} %copy.88.q_begin, s32[1,2048]{1,0:T(1,128)S(1)} %copy-done.3), custom_call_target="tpu_custom_call" | custom-call | tf_op jit(solution)/shard_map/attend/pallas_call | solution.py:668
  173.3 3.3 copy-done.1
  177.4 0.3 mul.297
  177.7 0.5 fusion.6.refs_18_
  178.3 3.2 multiply_reduce_fusion.3
  181.7 3.9 fusion.34
  185.6 0.6 slice-done.1
  186.3 1.0 fusion.35
  187.5 0.8 slice-done.5
  188.3 2.6 multiply_convert_fusion
  191.0 1.8 fusion.2
  192.7 2.2 fusion.36
  195.0 2.4 multiply_reduce_fusion.1
  197.4 1.0 fusion.26
  198.4 2.9 multiply_bitcast_fusion
  201.3 0.5 tile.4
  201.9 0.6 tile.5
  202.5 1.3 copy.96.refs_6_
  203.8 0.8 pad_maximum_fusion.3
  204.6 0.6 maximum_convert_fusion.5.refs_11_
  205.2 0.6 maximum_convert_fusion.6.refs_12_
  205.8 0.6 maximum_convert_fusion.refs_23_
  206.6 0.3 reduce_sum.86
  207.0 1.1 fusion.15.refs_24_
  208.8 0.6 pad_maximum_fusion.2.refs_25_
  209.5 282.8 %backward.1 = (bf16[15,512,1024]{2,1,0:T(8,128)(2,1)}, bf16[128,1024]{1,0:T(8,128)(2,1)}, f32[80,128]{1,0:T(8,128)}) custom-call(bf16[128,2048]{1,0:T(8,128)(2,1)} %bitcast.121, bf16[128,2048]{1,0:T(8,128)(2,1)} %get-tuple-element.152.refs_1_, f32[128,2048]{1,0:T(8,128)} %copy-done, f32[8,256]{1,0:T(8,128)} %copy-done.4, s32[1,256]{1,0:T(1,128)} %bitcast.148, ...), custom_call_target="tpu_custom_call" | custom-call | tf_op jit(solution)/shard_map/backward/pallas_call | solution.py:1286
  492.3 1.3 slice_bitcast_fusion.2
  493.6 15.9 %widen.1 = (f32[1536,1024]{1,0:T(8,128)}, f32[512,3072]{1,0:T(8,128)}, f32[512,3072]{1,0:T(8,128)}, f32[1024,1024]{1,0:T(8,128)}, f32[512,2048]{1,0:T(8,128)}, /*index=5*/f32[512,1024]{1,0:T(8,128)}, f32[512,1024]{1,0:T(8,128)}) custom-call(bf16[15,512,1024]{2,1,0:T(8,128)(2,1)} %get-tuple-element.48.refs_0_), custom_call_target="tpu_custom_call" | custom-call | tf_op jit(solution)/shard_map/widen/pallas_call | solution.py:1358
  509.7 0.7 copy.97
  510.4 0.6 fusion.30
  511.0 0.7 copy.116
  (132 shorter events, 5.4 us)
Async XLA Ops:
  5.0 86.6 %copy-start.12 = (bf16[1,128,1024]{2,1,0:T(8,128)(2,1)S(1)}, bf16[1,128,1024]{2,1,0:T(8,128)(2,1)}, u32[]{:S(2)}) copy-start(bf16[1,128,1024]{2,1,0:T(8,128)(2,1)} %param.16) | copy-start | bytes 786436
  91.9 116.1 %copy-start.6 = (bf16[128,1024]{1,0:T(8,128)(2,1)}, bf16[128,1024]{1,0:T(8,128)(2,1)S(1)}, u32[]{:S(2)}) copy-start(bf16[128,1024]{1,0:T(8,128)(2,1)S(1)} %fusion.11.refs_20_) | copy-start | bytes 786436
  91.9 4.5 copy-start.26
  91.9 4.6 copy-start.3
  95.0 1.0 copy-start.7
  97.2 5.5 %copy-start.24 = (s32[128]{0:T(128)}, s32[128]{0:T(128)S(1)}, u32[]{:S(2)}) copy-start(s32[128]{0:T(128)S(1)} %get-tuple-element.144) | copy-start | bytes 1540
  97.9 2.9 copy-start.8
  98.4 4.4 copy-start.2
  101.3 1.4 copy-start.10
  101.3 75.3 %copy-start.19 = (bf16[2,80,128]{2,1,0:T(8,128)(2,1)S(1)}, bf16[2,80,128]{2,1,0:T(8,128)(2,1)}, u32[]{:S(2)}) copy-start(bf16[2,80,128]{2,1,0:T(8,128)(2,1)} %get-tuple-element.35) | copy-start | bytes 122884
  173.3 3.3 copy-start.1
  176.6 4.9 copy-start.4
  176.6 21.7 %copy-start = (f32[128,2048]{1,0:T(8,128)}, f32[128,2048]{1,0:T(8,128)S(1)}, u32[]{:S(2)}) copy-start(f32[128,2048]{1,0:T(8,128)S(1)} %get-tuple-element.39.refs_2_) | copy-start | bytes 3145732
  177.7 3.8 copy-start.20
  178.2 7.4 %copy-start.11 = (bf16[128,2048]{1,0:T(8,128)(2,1)}, bf16[128,2048]{1,0:T(8,128)(2,1)S(1)}, u32[]{:S(2)}) copy-start(bf16[128,2048]{1,0:T(8,128)(2,1)S(1)} %fusion.6.refs_18_) | copy-start | bytes 1572868
  181.5 4.1 slice-start
  181.6 4.0 copy-start.9
  181.6 4.6 slice-start.1
  181.7 5.8 %slice-start.4 = ((s8[6291456]{0:T(1024)(128)(4,1)}), s8[4194304]{0:T(1024)(128)(4,1)S(1)}, s32[]{:S(2)}) async-start(s8[6291456]{0:T(1024)(128)(4,1)} %bitcast.133), calls=%async_computation.4 | async-start | bytes 8388608
  186.3 2.0 slice-start.5
  186.3 2.0 copy-start.17
  186.3 6.4 %slice-start.2 = ((s8[6291456]{0:T(1024)(128)(4,1)}), s8[4194304]{0:T(1024)(128)(4,1)S(1)}, s32[]{:S(2)}) async-start(s8[6291456]{0:T(1024)(128)(4,1)} %bitcast.127), calls=%async_computation.2 | async-start | bytes 8388608
  188.3 4.4 slice-start.3
  190.9 4.0 copy-start.13
  190.9 4.0 copy-start.15
  191.0 4.0 copy-start.14
  195.0 3.4 copy-start.5
  198.4 5.5 %copy-start.16 = (bf16[128,1024]{1,0:T(8,128)(2,1)}, bf16[128,1024]{1,0:T(8,128)(2,1)S(1)}, u32[]{:S(2)}) copy-start(bf16[128,1024]{1,0:T(8,128)(2,1)S(1)} %get-tuple-element.142.refs_19_) | copy-start | bytes 786436
  198.4 3.0 copy-start.31
  198.4 3.5 copy-start.25
  198.4 6.2 %copy-start.29 = (bf16[1,64]{1,0:T(2,128)(2,1)S(1)}, bf16[1,64]{1,0:T(2,128)(2,1)}, u32[]{:S(2)}) copy-start(bf16[1,64]{1,0:T(2,128)(2,1)} %get-tuple-element.176) | copy-start | bytes 388
  198.4 6.2 %copy-start.30 = (bf16[1,64]{1,0:T(2,128)(2,1)S(1)}, bf16[1,64]{1,0:T(2,128)(2,1)}, u32[]{:S(2)}) copy-start(bf16[1,64]{1,0:T(2,128)(2,1)} %get-tuple-element.190) | copy-start | bytes 388
  198.4 6.8 %copy-start.27 = (bf16[1,64]{1,0:T(2,128)(2,1)S(1)}, bf16[1,64]{1,0:T(2,128)(2,1)}, u32[]{:S(2)}) copy-start(bf16[1,64]{1,0:T(2,128)(2,1)} %get-tuple-element.175) | copy-start | bytes 388
  198.4 6.8 %copy-start.28 = (bf16[1,64]{1,0:T(2,128)(2,1)S(1)}, bf16[1,64]{1,0:T(2,128)(2,1)}, u32[]{:S(2)}) copy-start(bf16[1,64]{1,0:T(2,128)(2,1)} %get-tuple-element.191) | copy-start | bytes 388
  198.4 7.3 %copy-start.22 = (bf16[1,1,4,128]{3,2,1,0:T(4,128)(2,1)S(1)}, bf16[1,1,4,128]{3,2,1,0:T(4,128)(2,1)}, u32[]{:S(2)}) copy-start(bf16[1,1,4,128]{3,2,1,0:T(4,128)(2,1)} %get-tuple-element.161) | copy-start | bytes 3076
  198.4 7.3 %copy-start.23 = (bf16[1,1,4,128]{3,2,1,0:T(4,128)(2,1)S(1)}, bf16[1,1,4,128]{3,2,1,0:T(4,128)(2,1)}, u32[]{:S(2)}) copy-start(bf16[1,1,4,128]{3,2,1,0:T(4,128)(2,1)} %get-tuple-element.162) | copy-start | bytes 3076
  493.6 15.9 %copy-start.21 = (f32[80,128]{1,0:T(8,128)S(1)}, f32[80,128]{1,0:T(8,128)}, u32[]{:S(2)}) copy-start(f32[80,128]{1,0:T(8,128)} %get-tuple-element.47) | copy-start | bytes 122884
  493.6 17.4 %copy-start.18 = (bf16[128,1024]{1,0:T(8,128)(2,1)S(1)}, bf16[128,1024]{1,0:T(8,128)(2,1)}, u32[]{:S(2)}) copy-start(bf16[128,1024]{1,0:T(8,128)(2,1)} %get-tuple-element.46) | copy-start | bytes 786436

commit v5 on v4

--- a/solution.py
+++ b/solution.py
@@ -72,6 +72,7 @@
 MESH = pl.DeviceIdType.MESH
 UNITS = 15
 VECTOR_ROWS = 80
+GATE_ROW = 9
 SIDE = 512
 PART = 256
 
@@ -526,171 +527,6 @@
         ),
         name="sum_grads",
     )(rows, columns, small)
-
-
-def attend_kernel(
-    depth,
-    q_ref,
-    kv_ref,
-    q_pos,
-    q_begin,
-    k_pos,
-    out_ref,
-    log_ref,
-    kv_all,
-    stacked,
-    summed,
-    sums,
-    bias,
-    send_z,
-    recv_z,
-    send_x,
-    recv_x,
-    send_core,
-    recv_core,
-):
-    index = lax.axis_index("ctx")
-    group = lax.axis_index("fsdp")
-    z, x, core = place_of(index)
-    count = q_ref.shape[0]
-    wide = 4 * count
-    heads = q_ref.shape[1] // HEAD_DIM // 2
-
-    def device(at_z, at_x, at_core):
-        return ((at_z * 2 + at_x) * 2 + at_core, group)
-
-    across = device(z, 1 - x, core)
-    beside = device(z, x, 1 - core)
-    ahead = [lax.rem(z + offset, depth) for offset in range(depth)]
-    behind = [lax.rem(z + depth - offset, depth) for offset in range(depth)]
-    greet([device(ahead[offset], x, core) for offset in range(1, depth)] + [across, beside])
-
-    def rows(at_z, at_x, at_core):
-        first = ((at_z * 2 + at_x) * 2 + at_core) * count
-        return kv_all.at[pl.ds(pl.multiple_of(first, count), count)]
-
-    def z_copy(offset, at_z):
-        return remote(
-            device(ahead[offset], x, core),
-            kv_ref,
-            rows(at_z, x, core),
-            send_z.at[offset - 1],
-            recv_z.at[offset - 1],
-        )
-
-    def x_copy(offset, at_x):
-        part = rows(behind[offset], at_x, core)
-        return remote(across, part, part, send_x.at[offset], recv_x.at[offset])
-
-    def core_copy(offset, which, at_core):
-        part = rows(behind[offset], x + which - 2 * x * which, at_core)
-        return remote(
-            beside, part, part, send_core.at[offset, which], recv_core.at[offset, which]
-        )
-
-    for offset in range(1, depth):
-        z_copy(offset, z).start()
-    rows(z, x, core)[...] = kv_ref[...]
-    for head in range(heads):
-        for turn in range(2):
-            at = (2 * head + turn) * HEAD_DIM
-            stacked[head, turn * count : (turn + 1) * count] = q_ref[:, at : at + HEAD_DIM]
-    summed[...] = jnp.zeros_like(summed)
-    sums[...] = jnp.zeros_like(sums)
-
-    def stage_far(offset):
-        if offset:
-            z_copy(offset, behind[offset]).wait_recv()
-        x_copy(offset, x).start()
-        core_copy(offset, 0, core).start()
-
-    def stage_across(offset):
-        x_copy(offset, 1 - x).wait_recv()
-        core_copy(offset, 1, core).start()
-
-    def stage_attend(offset):
-        core_copy(offset, 0, 1 - core).wait_recv()
-        core_copy(offset, 1, 1 - core).wait_recv()
-        first = pl.multiple_of(behind[offset] * wide, wide)
-        place = k_pos[:, pl.ds(first, wide)]
-        allowed = (place >= q_begin[...]) & (place <= q_pos[...])
-        low = jnp.where(allowed, 0.0, NEG)
-        bias[:count] = low
-        bias[count:] = low
-
-        def one(head, carry):
-            at = pl.multiple_of(head * HEAD_DIM, HEAD_DIM)
-            keys = kv_all[pl.ds(first, wide), pl.ds(at, HEAD_DIM)]
-            at_v = pl.multiple_of((heads + head) * HEAD_DIM, HEAD_DIM)
-            values = kv_all[pl.ds(first, wide), pl.ds(at_v, HEAD_DIM)]
-            scores = lax.dot_general(
-                stacked[head], keys, (((1,), (1,)), ((), ())), preferred_element_type=jnp.float32
-            )
-            weights = jnp.exp(scores + bias[...])
-            part = weights[:, :HEAD_DIM]
-            for at_k in range(HEAD_DIM, wide, HEAD_DIM):
-                part = part + weights[:, at_k : at_k + HEAD_DIM]
-            sums[head] = sums[head] + part
-            summed[head] = summed[head] + jnp.dot(
-                weights.astype(jnp.bfloat16), values, preferred_element_type=jnp.float32
-            )
-            return carry
-
-        lax.fori_loop(0, heads, one, 0)
-
-    stages = (stage_far, stage_across, stage_attend)
-    for step in range(depth + len(stages) - 1):
-        for late, stage in enumerate(stages):
-            if 0 <= step - late < depth:
-                stage(step - late)
-    for head in range(heads):
-        total = jnp.sum(sums[head], axis=1, keepdims=True)
-        result = summed[head] / total
-        for turn in range(2):
-            at = (2 * head + turn) * HEAD_DIM
-            out_ref[:, at : at + HEAD_DIM] = result[turn * count : (turn + 1) * count]
-        across_rows = jnp.sum(sums[head].T, axis=0, keepdims=True)
-        log_ref[head : head + 1, :] = jnp.log(across_rows)
-    for offset in range(depth):
-        if offset:
-            z_copy(offset, z).wait_send()
-        x_copy(offset, x).wait_send()
-        core_copy(offset, 0, core).wait_send()
-        core_copy(offset, 1, core).wait_send()
-
-
-def attend(queries, key_values, q_pos, q_begin, k_pos):
-    depth = lax.axis_size("ctx") // 4
-    count = queries.shape[0]
-    heads = queries.shape[1] // HEAD_DIM // 2
-    dma = pltpu.SemaphoreType.DMA
-    vmem = pl.BlockSpec(memory_space=pltpu.VMEM)
-    return pl.pallas_call(
-        partial(attend_kernel, depth),
-        out_shape=[
-            jax.ShapeDtypeStruct(queries.shape, jnp.float32),
-            jax.ShapeDtypeStruct((heads, 2 * count), jnp.float32),
-            jax.ShapeDtypeStruct((4 * depth * count, key_values.shape[1]), jnp.bfloat16),
-        ],
-        in_specs=[vmem] * 5,
-        out_specs=[vmem] * 3,
-        scratch_shapes=[
-            pltpu.VMEM((heads, 2 * count, HEAD_DIM), jnp.bfloat16),
-            pltpu.VMEM((heads, 2 * count, HEAD_DIM), jnp.float32),
-            pltpu.VMEM((heads, 2 * count, HEAD_DIM), jnp.float32),
-            pltpu.VMEM((2 * count, 4 * count), jnp.float32),
-            dma((depth - 1,)),
-            dma((depth - 1,)),
-            dma((depth,)),
-            dma((depth,)),
-            dma((depth, 2)),
-            dma((depth, 2)),
-        ],
-        compiler_params=pltpu.CompilerParams(
-            collective_id=3, has_side_effects=True, vmem_limit_bytes=40 * 2**20
-        ),
-        name="attend",
-    )(queries, key_values, q_pos, q_begin, k_pos)
 
 
 ROW_HALVES = (("hidden", 1536, 0), ("lowered_two", 512, 1536), ("mixed_in", 1024, 2048), ("lowered", 512, 3072))
@@ -768,6 +604,514 @@
     return (scale * inner - raw * (scale * scale * scale * kept), gain_grad)
 
 
+FORWARD_ORDER = ("key", "value", "query", "out", "gate", "up", "down")
+FF_BLOCK = 512
+
+
+def forward_scratch(depth, count, shards, heads):
+    dma = pltpu.SemaphoreType.DMA
+    low = jnp.bfloat16
+    wide = jnp.float32
+    number = len(shards)
+    model = 2 * shards[0].shape[0]
+    scratch = dict(
+        gains=pltpu.VMEM((2, 16, 128), low),
+        gate_all=pltpu.VMEM((model, 128), low),
+        kv_all=pltpu.VMEM((4 * depth * count, 2 * heads * HEAD_DIM), low),
+        stacked=pltpu.VMEM((heads, 2 * count, HEAD_DIM), low),
+        summed=pltpu.VMEM((heads, 2 * count, HEAD_DIM), wide),
+        sums=pltpu.VMEM((heads, 2 * count, HEAD_DIM), wide),
+        bias=pltpu.VMEM((2 * count, 4 * count), wide),
+        total=pltpu.VMEM((count, model), wide),
+        total_back=pltpu.VMEM((count, model), wide),
+        gain_send=dma((2,)),
+        gain_recv=dma((2,)),
+        keep=dma((number + 1,)),
+        store=dma((3,)),
+        kv_store=dma((depth,)),
+        send=dma((number, 6)),
+        recv=dma((number, 6)),
+        kv_send_z=dma((depth, 2)),
+        kv_recv_z=dma((depth,)),
+        kv_send_x=dma((depth,)),
+        kv_recv_x=dma((depth,)),
+        kv_send_core=dma((depth, 2)),
+        kv_recv_core=dma((depth, 2)),
+    )
+    fulls = [pltpu.VMEM((2 * s.shape[0], s.shape[1]), low) for s in shards]
+    return (scratch, fulls)
+
+
+def forward_kernel(depth, names, number, *refs):
+    r = SimpleNamespace(**dict(zip(names, refs)))
+    shards = refs[:number]
+    fulls = refs[len(refs) - number :]
+    index = lax.axis_index("ctx")
+    group = lax.axis_index("fsdp")
+    z, x, core = place_of(index)
+    near = lax.rem(z, 2)
+    pair = z + 1 - 2 * near
+    count, model = r.tokens.shape
+    wide = 4 * count
+    heads = r.stacked.shape[0]
+
+    def device(at_z, at_x, at_core):
+        return ((at_z * 2 + at_x) * 2 + at_core, group)
+
+    over = (index, 1 - group)
+    across = device(z, 1 - x, core)
+    along = device(pair, x, core)
+    beside = device(z, x, 1 - core)
+    ahead = [lax.rem(z + offset, depth) for offset in range(depth)]
+    greet([device(ahead[offset], x, core) for offset in range(1, depth)] + [across, beside, over])
+
+    entry = x + near - 2 * x * near
+
+    def rows(w, start, size, half=None):
+        piece = shards[w].shape[0] // 8
+        first = start * piece
+        if half is not None:
+            first = first + half * shards[w].shape[0]
+        return pl.ds(pl.multiple_of(first, piece), size * piece)
+
+    def over_copy(w, sub):
+        start = core * 4 + entry * 2 + sub
+        return remote(
+            over,
+            shards[w].at[rows(w, start, 1)],
+            fulls[w].at[rows(w, start, 1, group)],
+            r.send.at[w, sub],
+            r.recv.at[w, sub],
+        )
+
+    def over_wait(w, sub):
+        part = fulls[w].at[rows(w, core * 4 + entry * 2 + sub, 1, 1 - group)]
+        remote(over, part, part, r.send.at[w, sub], r.recv.at[w, sub]).wait_recv()
+
+    def pass_on(w, slot, target, start, size):
+        part = fulls[w].at[rows(w, start, size, 1 - group)]
+        return remote(target, part, part, r.send.at[w, slot], r.recv.at[w, slot])
+
+    def x_pass(w, at_entry):
+        return pass_on(w, 2, across, core * 4 + at_entry * 2, 1)
+
+    def z_pass(w, at_entry):
+        return pass_on(w, 3, along, core * 4 + at_entry * 2 + 1, 1)
+
+    def core_pass(w, which, at_core):
+        at_entry = 1 - entry if which else entry
+        return pass_on(w, 4 + which, beside, at_core * 4 + at_entry * 2, 2)
+
+    def keep_copy(w):
+        return pltpu.make_async_copy(shards[w], fulls[w].at[rows(w, 0, 8, group)], r.keep.at[w])
+
+    def weight_one(w):
+        over_wait(w, 0)
+        x_pass(w, entry).start()
+        over_wait(w, 1)
+        z_pass(w, entry).start()
+        core_pass(w, 0, core).start()
+
+    def weight_two(w):
+        x_pass(w, 1 - entry).wait_recv()
+        z_pass(w, 1 - entry).wait_recv()
+        core_pass(w, 1, core).start()
+
+    def weight_end(w):
+        core_pass(w, 0, 1 - core).wait_recv()
+        core_pass(w, 1, 1 - core).wait_recv()
+        keep_copy(w).wait()
+
+    def weight_sent(w):
+        over_copy(w, 0).wait_send()
+        over_copy(w, 1).wait_send()
+        x_pass(w, entry).wait_send()
+        z_pass(w, entry).wait_send()
+        core_pass(w, 0, core).wait_send()
+        core_pass(w, 1, core).wait_send()
+
+    def gain_copy(at):
+        return remote(over, r.vectors, r.gains.at[at], r.gain_send.at[0], r.gain_recv.at[0])
+
+    def gate_copy(at):
+        half = model // 2
+        part = r.gate_all.at[pl.ds(pl.multiple_of(at * half, half), half)]
+        return remote(over, r.gate_shard, part, r.gain_send.at[1], r.gain_recv.at[1])
+
+    def gate_keep():
+        half = model // 2
+        part = r.gate_all.at[pl.ds(pl.multiple_of(group * half, half), half)]
+        return pltpu.make_async_copy(r.gate_shard, part, r.keep.at[number])
+
+    def kv_rows(at_z, at_x, at_core):
+        first = ((at_z * 2 + at_x) * 2 + at_core) * count
+        return r.kv_all.at[pl.ds(pl.multiple_of(first, count), count)]
+
+    def kv_z_copy(origin, way):
+        part = kv_rows(origin, x, core)
+        target = device(lax.rem(z + way + depth, depth), x, core)
+        return remote(
+            target, part, part, r.kv_send_z.at[origin, (way + 1) // 2], r.kv_recv_z.at[origin]
+        )
+
+    def kv_x_copy(origin, at_x):
+        part = kv_rows(origin, at_x, core)
+        return remote(across, part, part, r.kv_send_x.at[origin], r.kv_recv_x.at[origin])
+
+    def kv_core_copy(origin, which, at_core):
+        part = kv_rows(origin, x + which - 2 * x * which, at_core)
+        return remote(
+            beside, part, part, r.kv_send_core.at[origin, which], r.kv_recv_core.at[origin, which]
+        )
+
+    def kv_store(origin):
+        part = pl.ds(pl.multiple_of(origin * wide, wide), wide)
+        return pltpu.make_async_copy(r.kv_all.at[part], r.kv_hbm.at[part], r.kv_store.at[origin])
+
+    def on_line(at_z):
+        return (at_z >= 0) & (at_z < depth)
+
+    def kv_forward(origin, way):
+        @pl.when(on_line(z + way))
+        def run():
+            kv_z_copy(origin, way).start()
+
+    def kv_start():
+        kv_forward(z, 1)
+        kv_forward(z, -1)
+        kv_x_copy(z, x).start()
+        kv_core_copy(z, 0, core).start()
+
+    def at_distance(distance, call):
+        for way in (1, -1):
+
+            @pl.when(on_line(z - way * distance))
+            def run(way=way):
+                call(z - way * distance, way)
+
+    def kv_far(origin, way):
+        kv_z_copy(origin, way).wait_recv()
+        kv_forward(origin, way)
+        kv_x_copy(origin, x).start()
+        kv_core_copy(origin, 0, core).start()
+
+    def kv_across(origin, way):
+        kv_x_copy(origin, 1 - x).wait_recv()
+        kv_core_copy(origin, 1, core).start()
+
+    def vector_row(half, row):
+        return r.gains[half].astype(jnp.float32)[row : row + 1]
+
+    def model_gain(first):
+        pieces = [vector_row(half, first + row) for half in range(2) for row in range(model // 256)]
+        return jnp.concatenate(pieces, axis=1)
+
+    def head_gain(which):
+        half = HEAD_DIM // 2
+        inside = slice(which * half, (which + 1) * half)
+        return jnp.concatenate([vector_row(at, 8)[:, inside] for at in range(2)], axis=1)
+
+    def norm(values, gain):
+        scale = lax.rsqrt(jnp.mean(values * values, axis=-1, keepdims=True) + EPS)
+        return values * scale * gain
+
+    def head_turn(raw, gain):
+        normed = norm(raw, gain)
+        return normed * r.cosine[...] + pltpu.roll(normed, HEAD_DIM // 2, 1) * r.sine[...]
+
+    def project_kv():
+        first = pl.ds(pl.multiple_of(index * count, count), count)
+        r.key_raw[...] = jnp.dot(r.lowered[...], fulls[0][...], preferred_element_type=jnp.float32)
+        gain = r.key_gain[...]
+        for head in range(heads):
+            inside = slice(head * HEAD_DIM, (head + 1) * HEAD_DIM)
+            r.kv_all[first, inside] = head_turn(r.key_raw[:, inside], gain).astype(jnp.bfloat16)
+        r.kv_all[first, heads * HEAD_DIM :] = jnp.dot(
+            r.lowered[...], fulls[1][...], preferred_element_type=jnp.float32
+        ).astype(jnp.bfloat16)
+
+    def project_query():
+        r.query_raw[...] = jnp.dot(
+            r.lowered[...], fulls[2][...], preferred_element_type=jnp.float32
+        )
+        gain = r.query_gain[...]
+        for head in range(heads):
+            for turn in range(2):
+                at = (2 * head + turn) * HEAD_DIM
+                query = head_turn(r.query_raw[:, at : at + HEAD_DIM], gain) * HEAD_DIM ** (-0.5)
+                query = query.astype(jnp.bfloat16)
+                r.stacked[head, turn * count : (turn + 1) * count] = query
+                r.queries[:, at : at + HEAD_DIM] = query
+        r.summed[...] = jnp.zeros_like(r.summed)
+        r.sums[...] = jnp.zeros_like(r.sums)
+
+    def attend(origin, way):
+        kv_core_copy(origin, 0, 1 - core).wait_recv()
+        kv_core_copy(origin, 1, 1 - core).wait_recv()
+        kv_store(origin).start()
+        first = pl.multiple_of(origin * wide, wide)
+        place = r.k_pos[:, pl.ds(first, wide)]
+        allowed = (place >= r.q_begin[...]) & (place <= r.q_pos[...])
+        bias = jnp.where(allowed, 0.0, NEG)
+        r.bias[:count] = bias
+        r.bias[count:] = bias
+
+        def one(head, carry):
+            at = pl.multiple_of(head * HEAD_DIM, HEAD_DIM)
+            at_v = pl.multiple_of((heads + head) * HEAD_DIM, HEAD_DIM)
+            keys = r.kv_all[pl.ds(first, wide), pl.ds(at, HEAD_DIM)]
+            values = r.kv_all[pl.ds(first, wide), pl.ds(at_v, HEAD_DIM)]
+            scores = lax.dot_general(
+                r.stacked[head], keys, (((1,), (1,)), ((), ())), preferred_element_type=jnp.float32
+            )
+            weights = jnp.exp(scores + r.bias[...])
+            part = weights[:, :HEAD_DIM]
+            for at_k in range(HEAD_DIM, wide, HEAD_DIM):
+                part = part + weights[:, at_k : at_k + HEAD_DIM]
+            r.sums[head] = r.sums[head] + part
+            r.summed[head] = r.summed[head] + jnp.dot(
+                weights.astype(jnp.bfloat16), values, preferred_element_type=jnp.float32
+            )
+            return carry
+
+        lax.fori_loop(0, heads, one, 0)
+
+    def attend_end():
+        for head in range(heads):
+            result = r.summed[head] / jnp.sum(r.sums[head], axis=1, keepdims=True)
+            for turn in range(2):
+                at = (2 * head + turn) * HEAD_DIM
+                r.heads_out[:, at : at + HEAD_DIM] = result[turn * count : (turn + 1) * count]
+            r.logs[head : head + 1, :] = jnp.log(jnp.sum(r.sums[head].T, axis=0, keepdims=True))
+
+    def transposed(left, right):
+        return lax.dot_general(
+            left, right, (((1,), (1,)), ((), ())), preferred_element_type=jnp.float32
+        )
+
+    def feed_forward():
+        out_weight, gate_weight, up_weight, down_weight = fulls[3:]
+        gain = model_gain(4)
+        logits = jnp.dot(r.lowered[...], r.gate_all[...], preferred_element_type=jnp.float32)
+        head_gate = jax.nn.sigmoid(logits)
+        for head in range(2 * heads):
+            inside = slice(head * HEAD_DIM, (head + 1) * HEAD_DIM)
+            r.mixed_in[:, inside] = (
+                r.heads_out[:, inside] * head_gate[:, head : head + 1]
+            ).astype(jnp.bfloat16)
+        weight_end(3)
+        r.middle_grad[...] = r.tokens[...].astype(jnp.float32) + jnp.dot(
+            r.mixed_in[...], out_weight[...], preferred_element_type=jnp.float32
+        )
+        r.lowered_two[...] = norm(r.middle_grad[...], gain).astype(jnp.bfloat16)
+        weight_end(4)
+        weight_end(5)
+        weight_end(6)
+        r.total[...] = r.middle_grad[...]
+        r.total_back[...] = jnp.zeros_like(r.total_back)
+
+        def one(block, carry):
+            inside = pl.ds(pl.multiple_of(block * FF_BLOCK, FF_BLOCK), FF_BLOCK)
+            gate_part = gate_weight[:, inside]
+            up_part = up_weight[:, inside]
+            down_part = down_weight[inside, :]
+            gate_proj = jnp.dot(r.lowered_two[...], gate_part, preferred_element_type=jnp.float32)
+            up_proj = jnp.dot(r.lowered_two[...], up_part, preferred_element_type=jnp.float32)
+            sigma = jax.nn.sigmoid(gate_proj)
+            activation = gate_proj * sigma
+            hidden = (activation * up_proj).astype(jnp.bfloat16)
+            r.hidden[:, inside] = hidden
+            hidden_grad = transposed(r.cotangent[...], down_part)
+            gate_rows = hidden_grad * up_proj * sigma * (1.0 + gate_proj * (1.0 - sigma))
+            gate_rows = gate_rows.astype(jnp.bfloat16)
+            up_rows = (hidden_grad * activation).astype(jnp.bfloat16)
+            r.gate_rows[:, inside] = gate_rows
+            r.up_rows[:, inside] = up_rows
+            r.total[...] = r.total[...] + jnp.dot(
+                hidden, down_part, preferred_element_type=jnp.float32
+            )
+            r.total_back[...] = (
+                r.total_back[...] + transposed(gate_rows, gate_part) + transposed(up_rows, up_part)
+            )
+            return carry
+
+        lax.fori_loop(0, gate_weight.shape[1] // FF_BLOCK, one, 0)
+        r.mixed[...] = r.total[...].astype(jnp.bfloat16)
+        middle_part, gain_grad = norm_back(r.middle_grad[...], r.total_back[...], gain)
+        middle_grad = r.cotangent[...].astype(jnp.float32) + middle_part
+        r.middle_grad[...] = middle_grad
+        r.middle_low[...] = middle_grad.astype(jnp.bfloat16)
+        r.small[...] = jnp.zeros_like(r.small)
+        for at in range(model // 128):
+            half = at // (model // 256)
+            row = model // 256 + at % (model // 256)
+            r.small[half, row : row + 1, :] = gain_grad[:, at * 128 : (at + 1) * 128]
+        lane = lax.broadcasted_iota(jnp.int32, (count, 128), 1)
+        logit_grad = jnp.zeros((count, 128), jnp.float32)
+        for head in range(2 * heads):
+            inside = slice(head * HEAD_DIM, (head + 1) * HEAD_DIM)
+            mixed_grad = transposed(r.middle_low[...], out_weight[inside, :])
+            r.heads_grad[:, inside] = (mixed_grad * head_gate[:, head : head + 1]).astype(
+                jnp.bfloat16
+            )
+            moved = jnp.sum(mixed_grad * r.heads_out[:, inside], axis=1, keepdims=True)
+            logit_grad = jnp.where(lane == head, moved, logit_grad)
+        logit_grad = (logit_grad * head_gate * (1.0 - head_gate)).astype(jnp.bfloat16)
+        r.lowered_part[...] = transposed(logit_grad, r.gate_all[...])
+        gate_grad = lax.dot_general(
+            logit_grad, r.lowered[...], (((0,), (0,)), ((), ())), preferred_element_type=jnp.float32
+        )
+        for at in range(model // 128):
+            half = at // (model // 256)
+            row = GATE_ROW + at % (model // 256) * 2 * heads
+            r.small[half, row : row + 2 * heads, :] = gate_grad[
+                : 2 * heads, at * 128 : (at + 1) * 128
+            ]
+
+    gain_copy(group).start()
+    for w in range(3):
+        over_copy(w, 0).start()
+        over_copy(w, 1).start()
+    gate_copy(group).start()
+    for w in range(3, number):
+        over_copy(w, 0).start()
+        over_copy(w, 1).start()
+    for w in range(number):
+        keep_copy(w).start()
+    gate_keep().start()
+    r.gains[group] = r.vectors[...]
+    gain_copy(1 - group).wait_recv()
+    r.query_gain[...] = head_gain(0)
+    r.key_gain[...] = head_gain(1)
+    r.attention_gain[...] = model_gain(0)
+    r.lowered[...] = norm(r.tokens[...].astype(jnp.float32), r.attention_gain[...]).astype(
+        jnp.bfloat16
+    )
+    weight_one(0)
+    weight_one(1)
+    weight_two(0)
+    weight_two(1)
+    weight_end(0)
+    weight_end(1)
+    project_kv()
+    kv_start()
+    stores = [
+        pltpu.make_async_copy(fulls[at], out, r.store.at[at])
+        for at, out in enumerate((r.key_full, r.value_full, r.query_full))
+    ]
+    stores[0].start()
+    stores[1].start()
+    weight_one(2)
+    kv_across(z, 0)
+    at_distance(1, kv_far)
+    weight_two(2)
+    weight_end(2)
+    project_query()
+    stores[2].start()
+    weight_one(3)
+    attend(z, 0)
+    at_distance(1, kv_across)
+    at_distance(2, kv_far)
+    weight_two(3)
+    at_distance(1, attend)
+    weight_one(4)
+    at_distance(2, kv_across)
+    at_distance(3, kv_far)
+    weight_two(4)
+    at_distance(2, attend)
+    at_distance(3, kv_across)
+    weight_one(5)
+    at_distance(3, attend)
+    for distance in range(4, depth):
+        at_distance(distance, kv_far)
+        at_distance(distance, kv_across)
+        at_distance(distance, attend)
+    gate_copy(1 - group).wait_recv()
+    gate_keep().wait()
+    weight_two(5)
+    weight_one(6)
+    weight_two(6)
+    attend_end()
+    feed_forward()
+    for w in range(number):
+        weight_sent(w)
+    gain_copy(group).wait_send()
+    gate_copy(group).wait_send()
+    for store in stores:
+        store.wait()
+    for offset in range(depth):
+        kv_store(offset).wait()
+        kv_x_copy(offset, x).wait_send()
+        kv_core_copy(offset, 0, core).wait_send()
+        kv_core_copy(offset, 1, core).wait_send()
+    for way in (1, -1):
+        for distance in range(depth):
+
+            @pl.when(on_line(z - way * distance) & on_line(z + way))
+            def sent(way=way, distance=distance):
+                kv_z_copy(z - way * distance, way).wait_send()
+
+
+def forward(shards, near):
+    depth = lax.axis_size("ctx") // 4
+    count, model = near["tokens"].shape
+    width = 2 * model
+    heads = width // HEAD_DIM // 2
+    number = len(shards)
+    scratch, fulls = forward_scratch(depth, count, shards, heads)
+
+    def low(*shape):
+        return jax.ShapeDtypeStruct(shape, jnp.bfloat16)
+
+    def wide(*shape):
+        return jax.ShapeDtypeStruct(shape, jnp.float32)
+
+    hidden = shards[4].shape[1]
+    vmem_out = dict(
+        mixed=low(count, model),
+        lowered=low(count, model),
+        query_raw=wide(count, width),
+        key_raw=wide(count, model),
+        queries=low(count, width),
+        heads_out=wide(count, width),
+        logs=wide(heads, 2 * count),
+        hidden=low(count, hidden),
+        lowered_two=low(count, model),
+        gate_rows=low(count, hidden),
+        up_rows=low(count, hidden),
+        mixed_in=low(count, width),
+        middle_low=low(count, model),
+        middle_grad=wide(count, model),
+        heads_grad=low(count, width),
+        lowered_part=wide(count, model),
+        attention_gain=wide(1, model),
+        query_gain=wide(1, HEAD_DIM),
+        key_gain=wide(1, HEAD_DIM),
+        small=wide(2, VECTOR_ROWS, 128),
+    )
+    hbm_out = dict(
+        kv_hbm=low(4 * depth * count, width),
+        query_full=low(model, width),
+        key_full=low(model, model),
+        value_full=low(model, model),
+    )
+    vmem = pl.BlockSpec(memory_space=pltpu.VMEM)
+    hbm = pl.BlockSpec(memory_space=pl.ANY)
+    names = FORWARD_ORDER + tuple(near) + tuple(vmem_out) + tuple(hbm_out) + tuple(scratch)
+    results = pl.pallas_call(
+        partial(forward_kernel, depth, names, number),
+        out_shape=list(vmem_out.values()) + list(hbm_out.values()),
+        in_specs=[hbm] * number + [vmem] * len(near),
+        out_specs=[vmem] * len(vmem_out) + [hbm] * len(hbm_out),
+        scratch_shapes=list(scratch.values()) + fulls,
+        compiler_params=pltpu.CompilerParams(
+            collective_id=3, has_side_effects=True, vmem_limit_bytes=63 * 2**20
+        ),
+        name="forward",
+    )(*shards, *near.values())
+    return dict(zip(tuple(vmem_out) + tuple(hbm_out), results))
+
+
 def backward_kernel(depth, names, *refs):
     r = SimpleNamespace(**dict(zip(names, refs)))
     index = lax.axis_index("ctx")
@@ -965,7 +1309,7 @@
             kv_z_copy(offset).start()
 
     def head_back(raw, grad, gain):
-        turned = grad * r.cosine[...] + pltpu.roll(grad, HEAD_DIM // 2, 1) * r.sine[...]
+        turned = grad * r.cosine[...] - pltpu.roll(grad, HEAD_DIM // 2, 1) * r.sine[...]
         return norm_back(raw, turned, gain)
 
     def vector_store(query_gain_grad, key_gain_grad):
@@ -1402,7 +1746,7 @@
     return units.reshape(-1, units.shape[2]).astype(jnp.float32)
 
 
-def per_device(
+def per_device_far(
     tokens,
     cotangent,
     positions,
@@ -1480,44 +1824,32 @@
     queries = query_val.astype(jnp.bfloat16).reshape(count, KV_HEADS, groups, HEAD_DIM)
     keys = key_val.astype(jnp.bfloat16).reshape(count, KV_HEADS * HEAD_DIM)
     values = value_raw.astype(jnp.bfloat16)
-    near = lax.axis_size("ctx") <= 16
-    if near:
-        q_pos, q_begin = (my_pos, my_pos - my_rel)
-        heads_flat, log_total, kv_all = attend(
-            queries.reshape(count, -1),
-            jnp.concatenate([keys, values], axis=1),
-            q_pos[:, None],
-            q_begin[:, None],
-            place_all[None, :],
-        )
-        heads_out = heads_flat.reshape(count, HEADS, HEAD_DIM)
-    else:
-        key_piece = lax.all_gather(keys, "ctx", axis=0, tiled=True)
-        value_piece = lax.all_gather(values, "ctx", axis=0, tiled=True)
-        size = key_piece.shape[0]
-        key_pos, key_seg = slices(jnp.int32(0), size)
-        allowed = allowed_pairs(my_pos, my_seg, key_pos, key_seg)
-        top = jnp.full((KV_HEADS, groups, count), NEG, jnp.float32)
-        scores = jnp.einsum(
-            "tkgd,skd->kgts",
-            queries,
-            key_piece.reshape(size, KV_HEADS, HEAD_DIM),
-            preferred_element_type=jnp.float32,
-        )
-        scores = jnp.where(allowed, scores, NEG)
-        new_top = jnp.maximum(top, jnp.max(scores, axis=-1))
-        weights = jnp.where(allowed, jnp.exp(scores - new_top[..., None]), 0.0)
-        total = jnp.sum(weights, axis=-1)
-        summed = jnp.einsum(
-            "kgts,skd->kgtd",
-            weights.astype(jnp.bfloat16),
-            value_piece.reshape(size, KV_HEADS, HEAD_DIM),
-            preferred_element_type=jnp.float32,
-        )
-        top, total, summed = (new_top, total, summed)
-        attended = summed / total[..., None]
-        log_total = top + jnp.log(total)
-        heads_out = attended.transpose(2, 0, 1, 3).reshape(count, HEADS, HEAD_DIM)
+    key_piece = lax.all_gather(keys, "ctx", axis=0, tiled=True)
+    value_piece = lax.all_gather(values, "ctx", axis=0, tiled=True)
+    size = key_piece.shape[0]
+    key_pos, key_seg = slices(jnp.int32(0), size)
+    allowed = allowed_pairs(my_pos, my_seg, key_pos, key_seg)
+    top = jnp.full((KV_HEADS, groups, count), NEG, jnp.float32)
+    scores = jnp.einsum(
+        "tkgd,skd->kgts",
+        queries,
+        key_piece.reshape(size, KV_HEADS, HEAD_DIM),
+        preferred_element_type=jnp.float32,
+    )
+    scores = jnp.where(allowed, scores, NEG)
+    new_top = jnp.maximum(top, jnp.max(scores, axis=-1))
+    weights = jnp.where(allowed, jnp.exp(scores - new_top[..., None]), 0.0)
+    total = jnp.sum(weights, axis=-1)
+    summed = jnp.einsum(
+        "kgts,skd->kgtd",
+        weights.astype(jnp.bfloat16),
+        value_piece.reshape(size, KV_HEADS, HEAD_DIM),
+        preferred_element_type=jnp.float32,
+    )
+    top, total, summed = (new_top, total, summed)
+    attended = summed / total[..., None]
+    log_total = top + jnp.log(total)
+    heads_out = attended.transpose(2, 0, 1, 3).reshape(count, HEADS, HEAD_DIM)
     mixed_in = (
         (heads_out * head_gate[:, :, None]).reshape(count, HEADS * HEAD_DIM).astype(jnp.bfloat16)
     )
@@ -1556,86 +1888,6 @@
     headgate_weight_grad = jnp.einsum(
         "td,th->dh", lowered, logit_grad, preferred_element_type=jnp.float32
     )
-    headgate_part = headgate_weight_grad.reshape((2, -1))
-    if near:
-        zero = jnp.zeros((512,), jnp.float32)
-        small = jnp.stack(
-            [
-                pack_rows(
-                    [zero[:512], gain_two_grad.reshape(2, -1)[half], zero[:128], headgate_part[half]],
-                    VECTOR_ROWS,
-                )
-                for half in (0, 1)
-            ]
-        )
-        logit_part = jnp.einsum(
-            "th,dh->td", logit_grad, headgate_full, preferred_element_type=jnp.float32
-        )
-        units, token_grad, small_total = backward(
-            dict(
-                queries=queries.reshape(count, -1),
-                heads_grad=heads_grad.reshape(count, -1),
-                heads_out=heads_flat,
-                logs=log_total,
-                q_pos=jnp.tile(q_pos, 2)[None, :],
-                q_begin=jnp.tile(q_begin, 2)[None, :],
-                k_pos=place_all[:, None],
-                query_raw=query_raw,
-                key_raw=key_raw,
-                cosine=jnp.concatenate([cosine[:, 0], cosine[:, 0]], axis=1),
-                sine=jnp.concatenate([sine[:, 0], -sine[:, 0]], axis=1),
-                query_gain=gain_query[None, :],
-                key_gain=gain_key[None, :],
-                cotangent=upstream_low,
-                hidden=hidden,
-                lowered_two=lowered_two,
-                gate_rows=gate_rows,
-                up_rows=up_rows,
-                mixed_in=mixed_in,
-                middle_low=middle_low,
-                lowered=lowered,
-                tokens=tokens[0],
-                middle_grad=middle_grad,
-                attention_gain=gain_one[None, :],
-                lowered_part=logit_part,
-                small=small,
-            ),
-            dict(
-                kv_hbm=kv_all,
-                query_weight=query_full,
-                key_weight=key_full,
-                value_weight=value_full,
-            ),
-        )
-        totals = unpack_rows(small_total, vector_shapes)
-        down, gate, up, out, query, key, value = widen(
-            units,
-            (
-                (3, True),
-                (3, False),
-                (3, False),
-                (2, True),
-                (2, False),
-                (1, False),
-                (1, False),
-            ),
-        )
-        return (
-            mixed,
-            token_grad[None],
-            totals[0],
-            query,
-            key,
-            value,
-            totals[4],
-            totals[2],
-            totals[3],
-            out,
-            totals[1],
-            gate,
-            up,
-            down,
-        )
     out_grad = heads_grad.reshape(count, KV_HEADS, groups, HEAD_DIM)
     delta = jnp.sum(
         out_grad.astype(jnp.float32) * heads_out.reshape(count, KV_HEADS, groups, HEAD_DIM), axis=-1
@@ -1724,6 +1976,123 @@
     )
 
 
+def per_device_near(
+    tokens,
+    cotangent,
+    positions,
+    seq_lengths,
+    attention_gain,
+    query_weight,
+    key_weight,
+    value_weight,
+    headgate_weight,
+    query_gain,
+    key_gain,
+    out_weight,
+    feedforward_gain,
+    gate_weight,
+    up_weight,
+    down_weight,
+):
+    count = tokens.shape[1]
+    place_all = positions[0]
+    my_pos = lax.dynamic_slice_in_dim(place_all, lax.axis_index("ctx") * count, count)
+    my_rel = sequence_info(my_pos, seq_lengths[0])[1]
+    cosine, sine = rotary(my_rel)
+    cosine = jnp.concatenate([cosine[:, 0], cosine[:, 0]], axis=1)
+    sine = jnp.concatenate([-sine[:, 0], sine[:, 0]], axis=1)
+    begin = my_pos - my_rel
+    vectors = (attention_gain, feedforward_gain, query_gain, key_gain)
+    f = forward(
+        (key_weight, value_weight, query_weight, out_weight, gate_weight, up_weight, down_weight),
+        dict(
+            tokens=tokens[0],
+            cotangent=cotangent[0],
+            cosine=cosine,
+            sine=sine,
+            q_pos=my_pos[:, None],
+            q_begin=begin[:, None],
+            k_pos=place_all[None, :],
+            vectors=pack_rows(vectors, 16),
+            gate_shard=jnp.pad(headgate_weight, ((0, 0), (0, 128 - headgate_weight.shape[1]))),
+        ),
+    )
+    units, token_grad, small_total = backward(
+        dict(
+            queries=f["queries"],
+            heads_grad=f["heads_grad"],
+            heads_out=f["heads_out"],
+            logs=f["logs"],
+            q_pos=jnp.tile(my_pos, 2)[None, :],
+            q_begin=jnp.tile(begin, 2)[None, :],
+            k_pos=place_all[:, None],
+            query_raw=f["query_raw"],
+            key_raw=f["key_raw"],
+            cosine=cosine,
+            sine=sine,
+            query_gain=f["query_gain"],
+            key_gain=f["key_gain"],
+            cotangent=cotangent[0],
+            hidden=f["hidden"],
+            lowered_two=f["lowered_two"],
+            gate_rows=f["gate_rows"],
+            up_rows=f["up_rows"],
+            mixed_in=f["mixed_in"],
+            middle_low=f["middle_low"],
+            lowered=f["lowered"],
+            tokens=tokens[0],
+            middle_grad=f["middle_grad"],
+            attention_gain=f["attention_gain"],
+            lowered_part=f["lowered_part"],
+            small=f["small"],
+        ),
+        dict(
+            kv_hbm=f["kv_hbm"],
+            query_weight=f["query_full"],
+            key_weight=f["key_full"],
+            value_weight=f["value_full"],
+        ),
+    )
+    down, gate, up, out, query, key, value = widen(
+        units,
+        (
+            (3, True),
+            (3, False),
+            (3, False),
+            (2, True),
+            (2, False),
+            (1, False),
+            (1, False),
+        ),
+    )
+    one, two, query_part, key_part = unpack_rows(small_total[:GATE_ROW], [v.shape for v in vectors])
+    blocks, heads = (headgate_weight.shape[0] // 128, headgate_weight.shape[1])
+    headgate = small_total[GATE_ROW : GATE_ROW + blocks * heads].reshape(blocks, heads, 128)
+    headgate = headgate.transpose(0, 2, 1).reshape(headgate_weight.shape)
+    return (
+        f["mixed"][None],
+        token_grad[None],
+        one,
+        query,
+        key,
+        value,
+        headgate,
+        query_part,
+        key_part,
+        out,
+        two,
+        gate,
+        up,
+        down,
+    )
+
+
+def per_device(*args):
+    if lax.axis_size("ctx") <= 16:
+        return per_device_near(*args)
+    return per_device_far(*args)
+
+
 def solution(mesh):
     in_specs = (
         P("fsdp", "ctx", None),

time: 512 us -> 446 us (0.87)
  Pallas kernels: 452 us -> 424 us
  matrix products: 27.2 us -> 0 us
  other arithmetic: 9.55 us -> 2.65 us
  local copies, waits for them, and re-layouts: 21.1 us -> 15.7 us
    dot_general x14 -> x0, matrix products: 27.2 us -> none  [the longest x1 3.94 us: per_device(): jnp.dot(lowered_two, gate_full, preferred_element_type=jnp.float32)]
    pallas_call x2 -> x1, Pallas kernels: 154 us -> 135 us  [forward(): pl.pallas_call(partial(forward_kernel, depth, names, number), out_shape=l...]
    pallas_call x1, Pallas kernels: 283 us -> 273 us  [backward(): pl.pallas_call(partial(backward_kernel, depth, names), out_shape=list(out...]
    unnamed x85 -> x7, local copies, waits for them, and re-layouts: 9.68 us -> 2.25 us
where the time goes in v5:
time: 446 us; the launch traced here: 443 us
  Pallas kernels  424 us (95%)
  local copies, waits for them, and re-layouts  15.7 us (4%)
    pallas_call x1, Pallas kernels, backward(): pl.pallas_call(partial(backward_kernel, depth, names), out_shape=list(out...  273 us
    pallas_call x1, Pallas kernels, forward(): pl.pallas_call(partial(forward_kernel, depth, names, number), out_shape=l...  135 us
    pallas_call x1, Pallas kernels, widen(): pl.pallas_call(partial(widen_kernel, tuple(places)), out_shape=shapes, in...  15.9 us

profile of v5, /device:TPU:0, one launch (start us, length us, event | category | flops | bytes accessed | tf_op | source)
XLA Modules:
  0.0 443.3 jit_solution(4830356299944768643)
XLA Ops:
  0.6 0.8 reduce-window.8
  1.5 0.7 fusion.2
  2.1 0.7 fusion.1
  2.9 0.6 tile.4
  3.5 0.6 tile.5
  4.0 2.8 concatenate.11
  6.8 0.6 pad_bitcast_fusion.refs_14_
  7.4 0.7 copy.40.refs_11_
  8.2 0.7 copy.41.refs_12_
  8.9 0.8 copy.39
  9.7 0.7 pad.9.refs_15_
  10.4 0.3 fusion
  10.7 0.8 pad_maximum_fusion
  11.5 2.0 copy.42.refs_6_
  13.5 135.1 %forward.1 = (bf16[128,1024]{1,0:T(8,128)(2,1)}, bf16[128,1024]{1,0:T(8,128)(2,1)}, f32[128,2048]{1,0:T(8,128)}, f32[128,1024]{1,0:T(8,128)}, bf16[128,2048]{1,0...) custom-call(bf16[512,1024]{1,0:T(8,128)(2,1)} %refs_0_.1, ...), custom_call_target="tpu_custom_call" | custom-call | tf_op jit(solution)/shard_map/forward/pallas_call | solution.py:1101
  148.7 273.2 %backward.1 = (bf16[15,512,1024]{2,1,0:T(8,128)(2,1)}, bf16[128,1024]{1,0:T(8,128)(2,1)}, f32[80,128]{1,0:T(8,128)}) custom-call(bf16[128,2048]{1,0:T(8,128)(2,1)} %get-tuple-element.49.refs_0_, bf16[128,2048]{1,0:T(8,128)(2,1)} %get-tuple-element.50.refs_1_, f32[128,2048]{1,0:T(8,128)} %get-tuple-element.51.refs_2_, f32[8,256]{1,0:T(8,128)} %get-tuple-element.52.refs_3_, ...), custom_call_target="tpu_custom_call" | custom-call | tf_op jit(solution)/shard_map/backward/pallas_call | solution.py:1630
  421.9 1.3 slice_bitcast_fusion.1
  423.2 0.7 slice_bitcast_fusion
  423.9 0.8 slice.28
  424.7 0.6 fusion.4
  425.3 0.6 copy.46
  425.9 0.0 copy-start
  425.9 0.0 copy-start.1
  425.9 15.9 %widen.1 = (f32[1536,1024]{1,0:T(8,128)}, f32[512,3072]{1,0:T(8,128)}, f32[512,3072]{1,0:T(8,128)}, f32[1024,1024]{1,0:T(8,128)}, f32[512,2048]{1,0:T(8,128)}, /*index=5*/f32[512,1024]{1,0:T(8,128)}, f32[512,1024]{1,0:T(8,128)}) custom-call(bf16[15,512,1024]{2,1,0:T(8,128)(2,1)} %get-tuple-element.74.refs_0_), custom_call_target="tpu_custom_call" | custom-call | tf_op jit(solution)/shard_map/widen/pallas_call | solution.py:1702
  441.9 0.0 copy-done
  441.9 0.7 copy.49
  442.6 0.0 copy-done.1
  442.6 0.7 copy.50
  (2 shorter events, 0.0 us)
Async XLA Ops:
  425.9 16.0 %copy-start = (bf16[128,1024]{1,0:T(8,128)(2,1)S(1)}, bf16[128,1024]{1,0:T(8,128)(2,1)}, u32[]{:S(2)}) copy-start(bf16[128,1024]{1,0:T(8,128)(2,1)} %get-tuple-element.48) | copy-start | bytes 786436
  425.9 16.7 %copy-start.1 = (bf16[128,1024]{1,0:T(8,128)(2,1)S(1)}, bf16[128,1024]{1,0:T(8,128)(2,1)}, u32[]{:S(2)}) copy-start(bf16[128,1024]{1,0:T(8,128)(2,1)} %get-tuple-element.72) | copy-start | bytes 786436

commit v6 on v5

--- a/solution.py
+++ b/solution.py
@@ -71,6 +71,11 @@
 
 MESH = pl.DeviceIdType.MESH
 UNITS = 15
+MIX_EVERY = 4
+MIX_AT = 2
+CUTS = 2
+LEAD = 1
+LATE = (2, 4, 6, 8, 10, 12, 13)
 VECTOR_ROWS = 80
 GATE_ROW = 9
 SIDE = 512
@@ -542,7 +547,9 @@
 
 def back_scratch(depth, count, width, heads):
     dma = pltpu.SemaphoreType.DMA
-    piece = SIDE // depth
+    side = SIDE // CUTS
+    piece = side // depth
+    units = CUTS * UNITS
     low = jnp.bfloat16
     wide = jnp.float32
     return dict(
@@ -565,10 +572,10 @@
         small_part=pltpu.VMEM((3, VECTOR_ROWS, 128), wide),
         small_in=pltpu.VMEM((3, VECTOR_ROWS, 128), wide),
         small_deep=pltpu.VMEM((depth - 1, VECTOR_ROWS, 128), wide),
-        out_x=pltpu.VMEM((UNITS, SIDE, PART), low),
-        in_x=pltpu.VMEM((UNITS, SIDE, PART), low),
-        in_z=pltpu.VMEM((UNITS, depth - 1, piece, PART), low),
-        done=pltpu.VMEM((UNITS, piece, PART), low),
+        out_x=pltpu.VMEM((units, side, PART), low),
+        in_x=pltpu.VMEM((units, side, PART), low),
+        in_z=pltpu.VMEM((units, depth - 1, piece, PART), low),
+        done=pltpu.VMEM((units, piece, PART), low),
         load=dma((depth + 3,)),
         send_rows=dma((4, 2)),
         recv_rows=dma((4, 2)),
@@ -582,17 +589,17 @@
         kv_recv_z=dma((depth - 1,)),
         small_send=dma((2 + depth,)),
         small_recv=dma((2 + depth,)),
-        send_x=dma((UNITS,)),
-        recv_x=dma((UNITS,)),
-        send_z=dma((UNITS, depth - 1)),
-        recv_z=dma((UNITS, depth - 1)),
-        send_done=dma((UNITS, depth - 1)),
-        recv_done=dma((UNITS, depth - 1)),
-        keep_done=dma((UNITS,)),
-        send_half=dma((UNITS,)),
-        recv_half=dma((UNITS,)),
-        send_core=dma((UNITS, 2)),
-        recv_core=dma((UNITS, 2)),
+        send_x=dma((units,)),
+        recv_x=dma((units,)),
+        send_z=dma((units, depth - 1)),
+        recv_z=dma((units, depth - 1)),
+        send_done=dma((units, depth, 2)),
+        recv_done=dma((units, depth)),
+        keep_done=dma((units,)),
+        send_half=dma((units,)),
+        recv_half=dma((units,)),
+        send_core=dma((units, 2)),
+        recv_core=dma((units, 2)),
     )
 
 
@@ -1120,7 +1127,8 @@
     count = r.queries.shape[0]
     wide = 4 * count
     heads = r.queries.shape[1] // HEAD_DIM // 2
-    piece = SIDE // depth
+    side = SIDE // CUTS
+    piece = side // depth
 
     def device(at_z, at_x, at_core):
         return ((at_z * 2 + at_x) * 2 + at_core, group)
@@ -1130,7 +1138,6 @@
     over = (index, 1 - group)
     over_beside = (index + 1 - 2 * core, 1 - group)
     ahead = [lax.rem(z + offset, depth) for offset in range(depth)]
-    behind = [lax.rem(z + depth - offset, depth) for offset in range(depth)]
     peers = [device(ahead[offset], x, core) for offset in range(1, depth)]
     greet(peers + [across, beside, over, over_beside])
 
@@ -1395,8 +1402,8 @@
             r.small_base[half, row : row + 1, :] = gain_grad[:, at * 128 : (at + 1) * 128]
 
     def product(unit, half):
-        a, g = unit_blocks(unit)
-        left = block_of(r.rows_all, a, SIDE)
+        a, g = unit_blocks(lax.div(unit, CUTS))
+        left = block_of(r.rows_all, a * CUTS + lax.rem(unit, CUTS), side)
         right = block_of(r.cols_all, g * 2 + half, PART)
         return lax.dot_general(
             left, right, (((0,), (0,)), ((), ())), preferred_element_type=jnp.float32
@@ -1407,6 +1414,10 @@
 
     def columns_at(at_x, at_core):
         return pl.ds(pl.multiple_of((at_core * 2 + at_x) * PART, PART), PART)
+
+    def place(unit, first, size, at_x, at_core):
+        start = pl.multiple_of(lax.rem(unit, CUTS) * side + first, size)
+        return r.units.at[lax.div(unit, CUTS), pl.ds(start, size), columns_at(at_x, at_core)]
 
     def x_copy(unit):
         return remote(
@@ -1426,28 +1437,32 @@
             r.recv_z.at[unit, offset - 1],
         )
 
-    def done_copy(unit, offset, at_z):
+    def on_line(at_z):
+        return (at_z >= 0) & (at_z < depth)
+
+    def done_copy(unit, origin, way, first=False):
+        part = place(unit, origin * piece, piece, x, core)
         return remote(
-            device(ahead[offset], x, core),
-            r.done.at[unit],
-            r.units.at[unit, rows_at(at_z), columns_at(x, core)],
-            r.send_done.at[unit, offset - 1],
-            r.recv_done.at[unit, offset - 1],
+            device(lax.rem(z + way + depth, depth), x, core),
+            r.done.at[unit] if first else part,
+            part,
+            r.send_done.at[unit, origin, (way + 1) // 2],
+            r.recv_done.at[unit, origin],
         )
 
     def keep_copy(unit):
         return pltpu.make_async_copy(
             r.done.at[unit],
-            r.units.at[unit, rows_at(z), columns_at(x, core)],
+            place(unit, z * piece, piece, x, core),
             r.keep_done.at[unit],
         )
 
     def half_copy(unit, at_x):
-        part = r.units.at[unit, :, columns_at(at_x, core)]
+        part = place(unit, 0, side, at_x, core)
         return remote(across, part, part, r.send_half.at[unit], r.recv_half.at[unit])
 
     def core_copy(unit, which, at_x, at_core):
-        part = r.units.at[unit, :, columns_at(at_x, at_core)]
+        part = place(unit, 0, side, at_x, at_core)
         return remote(
             beside, part, part, r.send_core.at[unit, which], r.recv_core.at[unit, which]
         )
@@ -1463,37 +1478,139 @@
         for offset in range(1, depth):
             z_copy(unit, offset).start()
 
+    def by_kind(unit, x_last, x_first):
+        kind = lax.rem(lax.div(unit, CUTS), MIX_EVERY) == MIX_AT
+
+        @pl.when(kind)
+        def run_first():
+            x_first()
+
+        @pl.when(jnp.logical_not(kind))
+        def run_last():
+            x_last()
+
+    def both_ways(distance, call):
+        for way in (1, -1):
+            origin = z - way * distance
+
+            @pl.when(on_line(origin))
+            def run(way=way, origin=origin):
+                call(origin, way)
+
+    def pass_on(way, copy):
+        @pl.when(on_line(z + way))
+        def run():
+            copy.start()
+
+    def wide_place(unit, first, size, at_core):
+        start = pl.multiple_of(lax.rem(unit, CUTS) * side + first, size)
+        columns = pl.ds(pl.multiple_of(at_core * 2 * PART, 2 * PART), 2 * PART)
+        return r.units.at[lax.div(unit, CUTS), pl.ds(start, size), columns]
+
+    def piece_copy(unit, at_x):
+        return remote(
+            across,
+            r.done.at[unit],
+            place(unit, z * piece, piece, at_x, core),
+            r.send_half.at[unit],
+            r.recv_half.at[unit],
+        )
+
+    def wide_copy(unit, origin, way):
+        part = wide_place(unit, origin * piece, piece, core)
+        return remote(
+            device(lax.rem(z + way + depth, depth), x, core),
+            part,
+            part,
+            r.send_done.at[unit, origin, (way + 1) // 2],
+            r.recv_done.at[unit, origin],
+        )
+
+    def wide_core(unit, at_core):
+        part = wide_place(unit, 0, side, at_core)
+        return remote(beside, part, part, r.send_core.at[unit, 0], r.recv_core.at[unit, 0])
+
+    def hop(unit, distance, copy):
+        def run(origin, way):
+            copy(unit, origin, way).wait_recv()
+            pass_on(way, copy(unit, origin, way))
+
+        both_ways(distance, run)
+
+    def sent(unit, copy):
+        for distance in range(depth - 1):
+
+            def run(origin, way):
+                @pl.when(on_line(z + way))
+                def wait():
+                    copy(unit, origin, way).wait_send()
+
+            both_ways(distance, run)
+
     def stage_total(unit):
         total = r.in_x[unit, rows_at(z)].astype(jnp.float32)
         for offset in range(1, depth):
             z_copy(unit, offset).wait_recv()
             total = total + r.in_z[unit, offset - 1].astype(jnp.float32)
         r.done[unit] = total.astype(jnp.bfloat16)
-        for offset in range(1, depth):
-            done_copy(unit, offset, z).start()
         keep_copy(unit).start()
 
-    def stage_half(unit):
-        keep_copy(unit).wait()
-        for offset in range(1, depth):
-            done_copy(unit, offset, behind[offset]).wait_recv()
-        half_copy(unit, x).start()
-        core_copy(unit, 0, x, core).start()
+        def x_last():
+            for way in (1, -1):
+                pass_on(way, done_copy(unit, z, way, True))
+
+        by_kind(unit, x_last, lambda: piece_copy(unit, x).start())
+
+    def stage_hop(number, unit):
+        def x_last():
+            hop(unit, number, done_copy)
+            if number == depth - 1:
+                keep_copy(unit).wait()
+                half_copy(unit, x).start()
+                core_copy(unit, 0, x, core).start()
+
+        def x_first():
+            if number > 1:
+                hop(unit, number - 1, wide_copy)
+            else:
+                piece_copy(unit, 1 - x).wait_recv()
+                keep_copy(unit).wait()
+                for way in (1, -1):
+                    pass_on(way, wide_copy(unit, z, way))
+
+        by_kind(unit, x_last, x_first)
 
     def stage_core(unit):
-        half_copy(unit, 1 - x).wait_recv()
-        core_copy(unit, 1, 1 - x, core).start()
+        def x_last():
+            half_copy(unit, 1 - x).wait_recv()
+            core_copy(unit, 1, 1 - x, core).start()
+
+        def x_first():
+            hop(unit, depth - 1, wide_copy)
+            wide_core(unit, core).start()
+
+        by_kind(unit, x_last, x_first)
 
     def stage_end(unit):
-        core_copy(unit, 0, x, 1 - core).wait_recv()
-        core_copy(unit, 1, 1 - x, 1 - core).wait_recv()
         x_copy(unit).wait_send()
         for offset in range(1, depth):
             z_copy(unit, offset).wait_send()
-            done_copy(unit, offset, z).wait_send()
-        half_copy(unit, x).wait_send()
-        core_copy(unit, 0, x, core).wait_send()
-        core_copy(unit, 1, 1 - x, core).wait_send()
+
+        def x_last():
+            core_copy(unit, 0, x, 1 - core).wait_recv()
+            core_copy(unit, 1, 1 - x, 1 - core).wait_recv()
+            sent(unit, done_copy)
+            half_copy(unit, x).wait_send()
+            core_copy(unit, 0, x, core).wait_send()
+            core_copy(unit, 1, 1 - x, core).wait_send()
+
+        def x_first():
+            wide_core(unit, 1 - core).wait_recv()
+            piece_copy(unit, x).wait_send()
+            sent(unit, wide_copy)
+            wide_core(unit, core).wait_send()
+
+        by_kind(unit, x_last, x_first)
 
     def small_copy(at, target, source):
         return remote(
@@ -1549,46 +1666,45 @@
             def run(call=call):
                 call()
 
-    lead = 1
-    early = [(at, partial(attend_pairs, order[at])) for at in range(depth)]
-    early += [(at + 1, partial(attend_core, order[at])) for at in range(depth)]
-    early += [(at + 2, partial(attend_across, order[at])) for at in range(depth)]
+    def step_of(unit):
+        return LEAD + CUTS * unit
+
+    spread = CUTS
+    end = spread * depth
+    early = [(spread * at, partial(attend_pairs, order[at])) for at in range(depth)]
+    early += [(spread * (at + 1), partial(attend_core, order[at])) for at in range(depth)]
+    early += [(spread * (at + 2), partial(attend_across, order[at])) for at in range(depth)]
     early += [
         (0, partial(rows_start, 1)),
         (0, partial(columns_start, 1)),
-        (2, partial(columns_start, 2)),
-        (3, partial(rows_start, 2)),
-        (3, partial(columns_start, 3)),
-        (3, partial(rows_start, 3)),
-        (depth, query_end),
-        (depth + 2, key_end),
-        (depth + 3, token_end),
-        (depth + 4, lambda: small_over().start()),
-        (depth + 6, small_beside),
-        (depth + 7, small_across),
-        (depth + 8, small_spread),
-        (depth + 10, small_end),
+        (spread * 2, partial(columns_start, 2)),
+        (spread * 3, partial(rows_start, 2)),
+        (spread * 3, partial(columns_start, 3)),
+        (spread * 3, partial(rows_start, 3)),
+        (end, query_end),
+        (end + 2 * spread, key_end),
+        (end + 3 * spread, token_end),
+        (end + 4 * spread, lambda: small_over().start()),
+        (end + 5 * spread, small_beside),
+        (end + 6 * spread, small_across),
+        (end + 7 * spread, small_spread),
+        (end + 8 * spread, small_end),
     ]
-    early += [(lead + 0 - 1, partial(rows_pass, 0))]
-    early += [(lead + 3 - 1, partial(rows_pass, 1))]
-    early += [(lead + 9 - 1, partial(rows_pass, 2))]
-    early += [(lead + 11 - 1, partial(rows_pass, 3))]
-    before = [(lead + 0, partial(columns_wait, 0)), (lead + 0, lambda: rows_beside(0).wait_recv())]
-    before += [(lead + 3, partial(columns_wait, 1)), (lead + 3, lambda: rows_beside(1).wait_recv())]
-    before += [(lead + 6, partial(columns_wait, 2))]
-    before += [(lead + 9, partial(columns_wait, 3)), (lead + 9, lambda: rows_beside(2).wait_recv())]
+    early += [(step_of(unit) - 1, partial(rows_pass, i)) for i, unit in enumerate((0, 3, 9, 11))]
+    before = [
+        (step_of(unit), partial(columns_wait, i)) for i, unit in enumerate((0, 3, 6, 9, 11, 13, 14))
+    ]
     before += [
-        (lead + 11, partial(columns_wait, 4)),
-        (lead + 11, lambda: rows_beside(3).wait_recv()),
-        (lead + 13, partial(columns_wait, 5)),
-        (lead + 14, partial(columns_wait, 6)),
+        (step_of(unit), lambda i=i: rows_beside(i).wait_recv())
+        for i, unit in enumerate((0, 3, 9, 11))
     ]
-    stages = (stage_pair, stage_total, stage_half, stage_core, stage_end)
+    hops = [partial(stage_hop, number) for number in range(1, depth)]
+    stages = (stage_pair, stage_total, *hops, stage_core, stage_end)
 
     def stage_at(step, late, stage):
-        unit = step - lead - late
-
-        @pl.when((unit >= 0) & (unit < UNITS))
+        unit = step - LEAD - late
+
+        @pl.when((unit >= 0) & (unit < CUTS * UNITS))
         def run():
             stage(unit)
 
@@ -1596,11 +1712,11 @@
         at_steps(step, before)
         stage_at(step, 0, stage_send)
         at_steps(step, early)
-        for late, stage in enumerate(stages):
-            stage_at(step, late + 1, stage)
+        for late, stage in zip(LATE, stages):
+            stage_at(step, late, stage)
         return carry
 
-    lax.fori_loop(0, UNITS + lead + len(stages), body, 0)
+    lax.fori_loop(0, CUTS * UNITS + LEAD + LATE[-1], body, 0)
     for i in range(len(ROW_HALVES)):
         rows_over(i).wait_send()
         rows_beside(i).wait_send()

time: 446 us -> 419 us (0.939)
  Pallas kernels: 424 us -> 400 us
    pallas_call x1, Pallas kernels: 273 us -> 249 us  [backward(): pl.pallas_call(partial(backward_kernel, depth, names), out_shape=list(out...]
where the time goes in v6:
time: 419 us
  Pallas kernels  400 us (95%)
  local copies, waits for them, and re-layouts  15.7 us (4%)
    pallas_call x1, Pallas kernels, backward(): pl.pallas_call(partial(backward_kernel, depth, names), out_shape=list(out...  249 us
    pallas_call x1, Pallas kernels, forward(): pl.pallas_call(partial(forward_kernel, depth, names, number), out_shape=l...  135 us
    pallas_call x1, Pallas kernels, widen(): pl.pallas_call(partial(widen_kernel, tuple(places)), out_shape=shapes, in...  15.9 us

profile of v6, /device:TPU:0, one launch (start us, length us, event | category | flops | bytes accessed | tf_op | source)
XLA Modules:
  0.0 418.7 jit_solution(5888622933184347718)
XLA Ops:
  0.6 0.8 reduce-window.8
  1.5 0.7 fusion.2
  2.1 0.7 fusion.1
  2.9 0.6 tile.4
  3.5 0.6 tile.5
  4.0 2.8 concatenate.11
  6.8 0.6 pad_bitcast_fusion.refs_14_
  7.4 0.7 copy.40.refs_11_
  8.2 0.7 copy.41.refs_12_
  8.9 0.8 copy.39
  9.7 0.7 pad.9.refs_15_
  10.4 0.3 fusion
  10.7 0.8 pad_maximum_fusion
  11.5 2.0 copy.42.refs_6_
  13.5 135.0 %forward.1 = (bf16[128,1024]{1,0:T(8,128)(2,1)}, bf16[128,1024]{1,0:T(8,128)(2,1)}, f32[128,2048]{1,0:T(8,128)}, f32[128,1024]{1,0:T(8,128)}, bf16[128,2048]{1,0...) custom-call(bf16[512,1024]{1,0:T(8,128)(2,1)} %refs_0_.1, ...), custom_call_target="tpu_custom_call" | custom-call | tf_op jit(solution)/shard_map/forward/pallas_call | solution.py:1108
  148.5 248.8 %backward.1 = (bf16[15,512,1024]{2,1,0:T(8,128)(2,1)}, bf16[128,1024]{1,0:T(8,128)(2,1)}, f32[80,128]{1,0:T(8,128)}) custom-call(bf16[128,2048]{1,0:T(8,128)(2,1)} %get-tuple-element.49.refs_0_, bf16[128,2048]{1,0:T(8,128)(2,1)} %get-tuple-element.50.refs_1_, f32[128,2048]{1,0:T(8,128)} %get-tuple-element.51.refs_2_, f32[8,256]{1,0:T(8,128)} %get-tuple-element.52.refs_3_, ...), custom_call_target="tpu_custom_call" | custom-call | tf_op jit(solution)/shard_map/backward/pallas_call | solution.py:1746
  397.3 1.3 slice_bitcast_fusion.1
  398.6 0.7 slice_bitcast_fusion
  399.3 0.8 slice.28
  400.1 0.6 fusion.4
  400.7 0.6 copy.46
  401.3 0.0 copy-start
  401.3 0.0 copy-start.1
  401.3 15.9 %widen.1 = (f32[1536,1024]{1,0:T(8,128)}, f32[512,3072]{1,0:T(8,128)}, f32[512,3072]{1,0:T(8,128)}, f32[1024,1024]{1,0:T(8,128)}, f32[512,2048]{1,0:T(8,128)}, /*index=5*/f32[512,1024]{1,0:T(8,128)}, f32[512,1024]{1,0:T(8,128)}) custom-call(bf16[15,512,1024]{2,1,0:T(8,128)(2,1)} %get-tuple-element.74.refs_0_), custom_call_target="tpu_custom_call" | custom-call | tf_op jit(solution)/shard_map/widen/pallas_call | solution.py:1818
  417.3 0.0 copy-done
  417.3 0.7 copy.49
  418.0 0.0 copy-done.1
  418.0 0.7 copy.50
  (2 shorter events, 0.0 us)
Async XLA Ops:
  401.3 16.0 %copy-start = (bf16[128,1024]{1,0:T(8,128)(2,1)S(1)}, bf16[128,1024]{1,0:T(8,128)(2,1)}, u32[]{:S(2)}) copy-start(bf16[128,1024]{1,0:T(8,128)(2,1)} %get-tuple-element.48) | copy-start | bytes 786436
  401.3 16.7 %copy-start.1 = (bf16[128,1024]{1,0:T(8,128)(2,1)S(1)}, bf16[128,1024]{1,0:T(8,128)(2,1)}, u32[]{:S(2)}) copy-start(bf16[128,1024]{1,0:T(8,128)(2,1)} %get-tuple-element.72) | copy-start | bytes 786436

commit v7 on v6

--- a/solution.py
+++ b/solution.py
@@ -3,6 +3,7 @@
 
 import jax
 import jax.numpy as jnp
+import numpy as np
 from jax import lax
 from jax.experimental import pallas as pl
 from jax.experimental.pallas import tpu as pltpu
@@ -611,6 +612,7 @@
     return (scale * inner - raw * (scale * scale * scale * kept), gain_grad)
 
 
+LENGTHS = "lengths"
 FORWARD_ORDER = ("key", "value", "query", "out", "gate", "up", "down")
 FF_BLOCK = 512
 
@@ -622,8 +624,9 @@
     number = len(shards)
     model = 2 * shards[0].shape[0]
     scratch = dict(
-        gains=pltpu.VMEM((2, 16, 128), low),
-        gate_all=pltpu.VMEM((model, 128), low),
+        gains=pltpu.VMEM((2, 2, model // 2), wide),
+        head_gains=pltpu.VMEM((2, 2, HEAD_DIM // 2), wide),
+        gate_all=pltpu.VMEM((model, 2 * heads), low),
         kv_all=pltpu.VMEM((4 * depth * count, 2 * heads * HEAD_DIM), low),
         stacked=pltpu.VMEM((heads, 2 * count, HEAD_DIM), low),
         summed=pltpu.VMEM((heads, 2 * count, HEAD_DIM), wide),
@@ -631,8 +634,8 @@
         bias=pltpu.VMEM((2 * count, 4 * count), wide),
         total=pltpu.VMEM((count, model), wide),
         total_back=pltpu.VMEM((count, model), wide),
-        gain_send=dma((2,)),
-        gain_recv=dma((2,)),
+        gain_send=dma((3,)),
+        gain_recv=dma((3,)),
         keep=dma((number + 1,)),
         store=dma((3,)),
         kv_store=dma((depth,)),
@@ -647,6 +650,24 @@
     )
     fulls = [pltpu.VMEM((2 * s.shape[0], s.shape[1]), low) for s in shards]
     return (scratch, fulls)
+
+
+def own_places(positions, lengths, index, count):
+    row = positions[:, pl.ds(pl.multiple_of(index * count, count), count)]
+    begin = jnp.zeros_like(row)
+    end = 0
+    for at in range(lengths.shape[1]):
+        end = end + lengths[0, at]
+        begin = jnp.where(row >= end, end, begin)
+    square = (count, count)
+    return [
+        jnp.broadcast_to(value.astype(jnp.float32), square).T[:, :1] for value in (row, begin)
+    ]
+
+
+def pair_bias(places, q_pos, q_begin):
+    places = places.astype(jnp.float32)
+    return jnp.where((places >= q_begin) & (places <= q_pos), 0.0, NEG)
 
 
 def forward_kernel(depth, names, number, *refs):
@@ -740,6 +761,11 @@
     def gain_copy(at):
         return remote(over, r.vectors, r.gains.at[at], r.gain_send.at[0], r.gain_recv.at[0])
 
+    def head_gain_copy(at):
+        return remote(
+            over, r.head_vectors, r.head_gains.at[at], r.gain_send.at[2], r.gain_recv.at[2]
+        )
+
     def gate_copy(at):
         half = model // 2
         part = r.gate_all.at[pl.ds(pl.multiple_of(at * half, half), half)]
@@ -806,17 +832,12 @@
         kv_x_copy(origin, 1 - x).wait_recv()
         kv_core_copy(origin, 1, core).start()
 
-    def vector_row(half, row):
-        return r.gains[half].astype(jnp.float32)[row : row + 1]
-
-    def model_gain(first):
-        pieces = [vector_row(half, first + row) for half in range(2) for row in range(model // 256)]
+    def model_gain(which):
+        return jnp.concatenate([r.gains[half, which : which + 1] for half in range(2)], axis=1)
+
+    def head_gain(which):
+        pieces = [r.head_gains[half, which : which + 1] for half in range(2)]
         return jnp.concatenate(pieces, axis=1)
-
-    def head_gain(which):
-        half = HEAD_DIM // 2
-        inside = slice(which * half, (which + 1) * half)
-        return jnp.concatenate([vector_row(at, 8)[:, inside] for at in range(2)], axis=1)
 
     def norm(values, gain):
         scale = lax.rsqrt(jnp.mean(values * values, axis=-1, keepdims=True) + EPS)
@@ -857,9 +878,7 @@
         kv_core_copy(origin, 1, 1 - core).wait_recv()
         kv_store(origin).start()
         first = pl.multiple_of(origin * wide, wide)
-        place = r.k_pos[:, pl.ds(first, wide)]
-        allowed = (place >= r.q_begin[...]) & (place <= r.q_pos[...])
-        bias = jnp.where(allowed, 0.0, NEG)
+        bias = pair_bias(r.positions[:, pl.ds(first, wide)], r.q_pos[...], r.q_begin[...])
         r.bias[:count] = bias
         r.bias[count:] = bias
 
@@ -898,7 +917,7 @@
 
     def feed_forward():
         out_weight, gate_weight, up_weight, down_weight = fulls[3:]
-        gain = model_gain(4)
+        gain = model_gain(1)
         logits = jnp.dot(r.lowered[...], r.gate_all[...], preferred_element_type=jnp.float32)
         head_gate = jax.nn.sigmoid(logits)
         for head in range(2 * heads):
@@ -953,16 +972,20 @@
             half = at // (model // 256)
             row = model // 256 + at % (model // 256)
             r.small[half, row : row + 1, :] = gain_grad[:, at * 128 : (at + 1) * 128]
-        lane = lax.broadcasted_iota(jnp.int32, (count, 128), 1)
-        logit_grad = jnp.zeros((count, 128), jnp.float32)
-        for head in range(2 * heads):
-            inside = slice(head * HEAD_DIM, (head + 1) * HEAD_DIM)
-            mixed_grad = transposed(r.middle_low[...], out_weight[inside, :])
-            r.heads_grad[:, inside] = (mixed_grad * head_gate[:, head : head + 1]).astype(
-                jnp.bfloat16
+        lane = lax.broadcasted_iota(jnp.int32, (count, 2 * heads), 1)
+        logit_grad = jnp.zeros((count, 2 * heads), jnp.float32)
+        for pair in range(heads):
+            both = transposed(
+                r.middle_low[...], out_weight[2 * pair * HEAD_DIM : (2 * pair + 2) * HEAD_DIM, :]
             )
-            moved = jnp.sum(mixed_grad * r.heads_out[:, inside], axis=1, keepdims=True)
-            logit_grad = jnp.where(lane == head, moved, logit_grad)
+            for head in (2 * pair, 2 * pair + 1):
+                inside = slice(head * HEAD_DIM, (head + 1) * HEAD_DIM)
+                mixed_grad = both[:, (head % 2) * HEAD_DIM : (head % 2 + 1) * HEAD_DIM]
+                r.heads_grad[:, inside] = (mixed_grad * head_gate[:, head : head + 1]).astype(
+                    jnp.bfloat16
+                )
+                moved = jnp.sum(mixed_grad * r.heads_out[:, inside], axis=1, keepdims=True)
+                logit_grad = jnp.where(lane == head, moved, logit_grad)
         logit_grad = (logit_grad * head_gate * (1.0 - head_gate)).astype(jnp.bfloat16)
         r.lowered_part[...] = transposed(logit_grad, r.gate_all[...])
         gate_grad = lax.dot_general(
@@ -976,6 +999,7 @@
             ]
 
     gain_copy(group).start()
+    head_gain_copy(group).start()
     for w in range(3):
         over_copy(w, 0).start()
         over_copy(w, 1).start()
@@ -987,7 +1011,9 @@
         keep_copy(w).start()
     gate_keep().start()
     r.gains[group] = r.vectors[...]
+    r.head_gains[group] = r.head_vectors[...]
     gain_copy(1 - group).wait_recv()
+    head_gain_copy(1 - group).wait_recv()
     r.query_gain[...] = head_gain(0)
     r.key_gain[...] = head_gain(1)
     r.attention_gain[...] = model_gain(0)
@@ -995,6 +1021,13 @@
         jnp.bfloat16
     )
     weight_one(0)
+    own_pos, own_begin = own_places(r.positions, r.lengths, index, count)
+    r.q_pos[...] = own_pos
+    r.q_begin[...] = own_begin
+    angles = (own_pos - own_begin) * r.freqs[...]
+    side = lax.broadcasted_iota(jnp.int32, angles.shape, 1) < HEAD_DIM // 2
+    r.cosine[...] = jnp.cos(angles)
+    r.sine[...] = jnp.where(side, -1.0, 1.0) * jnp.sin(angles)
     weight_one(1)
     weight_two(0)
     weight_two(1)
@@ -1043,6 +1076,7 @@
     for w in range(number):
         weight_sent(w)
     gain_copy(group).wait_send()
+    head_gain_copy(group).wait_send()
     gate_copy(group).wait_send()
     for store in stores:
         store.wait()
@@ -1059,7 +1093,7 @@
                 kv_z_copy(z - way * distance, way).wait_send()
 
 
-def forward(shards, near):
+def forward(shards, near, lengths):
     depth = lax.axis_size("ctx") // 4
     count, model = near["tokens"].shape
     width = 2 * model
@@ -1094,6 +1128,10 @@
         attention_gain=wide(1, model),
         query_gain=wide(1, HEAD_DIM),
         key_gain=wide(1, HEAD_DIM),
+        q_pos=wide(count, 1),
+        q_begin=wide(count, 1),
+        cosine=wide(count, HEAD_DIM),
+        sine=wide(count, HEAD_DIM),
         small=wide(2, VECTOR_ROWS, 128),
     )
     hbm_out = dict(
@@ -1104,18 +1142,20 @@
     )
     vmem = pl.BlockSpec(memory_space=pltpu.VMEM)
     hbm = pl.BlockSpec(memory_space=pl.ANY)
-    names = FORWARD_ORDER + tuple(near) + tuple(vmem_out) + tuple(hbm_out) + tuple(scratch)
+    names = FORWARD_ORDER + tuple(near) + (LENGTHS,) + tuple(vmem_out) + tuple(hbm_out) + tuple(scratch)
     results = pl.pallas_call(
         partial(forward_kernel, depth, names, number),
         out_shape=list(vmem_out.values()) + list(hbm_out.values()),
-        in_specs=[hbm] * number + [vmem] * len(near),
+        in_specs=[hbm] * number
+        + [vmem] * len(near)
+        + [pl.BlockSpec(memory_space=pltpu.SMEM)],
         out_specs=[vmem] * len(vmem_out) + [hbm] * len(hbm_out),
         scratch_shapes=list(scratch.values()) + fulls,
         compiler_params=pltpu.CompilerParams(
             collective_id=3, has_side_effects=True, vmem_limit_bytes=63 * 2**20
         ),
         name="forward",
-    )(*shards, *near.values())
+    )(*shards, *near.values(), lengths)
     return dict(zip(tuple(vmem_out) + tuple(hbm_out), results))
 
 
@@ -1256,9 +1296,9 @@
     def attend_pairs(offset):
         kv_load(offset).wait()
         first = pl.multiple_of(ahead[offset] * wide, wide)
-        place = r.k_pos[pl.ds(first, wide), :]
-        allowed = (place >= r.q_begin[...]) & (place <= r.q_pos[...])
-        r.bias[...] = jnp.where(allowed, 0.0, NEG)
+        bias = pair_bias(r.k_pos[:, pl.ds(first, wide)], r.q_pos[...], r.q_begin[...]).T
+        r.bias[:, :count] = bias
+        r.bias[:, count:] = bias
 
         def one(head, carry):
             at = pl.multiple_of(head * HEAD_DIM, HEAD_DIM)
@@ -2110,28 +2150,21 @@
     up_weight,
     down_weight,
 ):
-    count = tokens.shape[1]
-    place_all = positions[0]
-    my_pos = lax.dynamic_slice_in_dim(place_all, lax.axis_index("ctx") * count, count)
-    my_rel = sequence_info(my_pos, seq_lengths[0])[1]
-    cosine, sine = rotary(my_rel)
-    cosine = jnp.concatenate([cosine[:, 0], cosine[:, 0]], axis=1)
-    sine = jnp.concatenate([-sine[:, 0], sine[:, 0]], axis=1)
-    begin = my_pos - my_rel
+    freqs = THETA ** (-np.arange(0, HEAD_DIM, 2, dtype=np.float64) / HEAD_DIM)
+    freqs = jnp.asarray(np.concatenate([freqs, freqs])[None], jnp.float32)
     vectors = (attention_gain, feedforward_gain, query_gain, key_gain)
     f = forward(
         (key_weight, value_weight, query_weight, out_weight, gate_weight, up_weight, down_weight),
         dict(
             tokens=tokens[0],
             cotangent=cotangent[0],
-            cosine=cosine,
-            sine=sine,
-            q_pos=my_pos[:, None],
-            q_begin=begin[:, None],
-            k_pos=place_all[None, :],
-            vectors=pack_rows(vectors, 16),
-            gate_shard=jnp.pad(headgate_weight, ((0, 0), (0, 128 - headgate_weight.shape[1]))),
+            positions=positions,
+            freqs=freqs,
+            vectors=jnp.stack([attention_gain, feedforward_gain]).astype(jnp.float32),
+            head_vectors=jnp.stack([query_gain, key_gain]).astype(jnp.float32),
+            gate_shard=headgate_weight,
         ),
+        seq_lengths,
     )
     units, token_grad, small_total = backward(
         dict(
@@ -2139,13 +2172,13 @@
             heads_grad=f["heads_grad"],
             heads_out=f["heads_out"],
             logs=f["logs"],
-            q_pos=jnp.tile(my_pos, 2)[None, :],
-            q_begin=jnp.tile(begin, 2)[None, :],
-            k_pos=place_all[:, None],
+            q_pos=f["q_pos"],
+            q_begin=f["q_begin"],
+            k_pos=positions,
             query_raw=f["query_raw"],
             key_raw=f["key_raw"],
-            cosine=cosine,
-            sine=sine,
+            cosine=f["cosine"],
+            sine=f["sine"],
             query_gain=f["query_gain"],
             key_gain=f["key_gain"],
             cotangent=cotangent[0],

time: 419 us -> 411 us (0.981)
  local copies, waits for them, and re-layouts: 15.7 us -> 8.26 us
where the time goes in v7:
time: 411 us; the launch traced here: 410 us
  Pallas kernels  399 us (97%)
  local copies, waits for them, and re-layouts  8.26 us (2%)
    pallas_call x1, Pallas kernels, backward(): pl.pallas_call(partial(backward_kernel, depth, names), out_shape=list(out...  248 us
    pallas_call x1, Pallas kernels, forward(): pl.pallas_call(partial(forward_kernel, depth, names, number), out_shape=l...  135 us
    pallas_call x1, Pallas kernels, widen(): pl.pallas_call(partial(widen_kernel, tuple(places)), out_shape=shapes, in...  15.9 us

profile of v7, /device:TPU:0, one launch (start us, length us, event | category | flops | bytes accessed | tf_op | source)
XLA Modules:
  0.0 410.2 jit_solution(12385401488835926679)
XLA Ops:
  0.6 1.2 maximum_convert_fusion.1.refs_12_
  1.9 0.7 stack.18
  2.6 0.7 stack.19
  3.3 0.6 maximum_convert_fusion.refs_11_
  3.9 1.5 copy.31.refs_13_
  5.3 135.2 %forward.1 = (bf16[128,1024]{1,0:T(8,128)(2,1)}, bf16[128,1024]{1,0:T(8,128)(2,1)}, f32[128,2048]{1,0:T(8,128)}, f32[128,1024]{1,0:T(8,128)}, bf16[128,2048]{1,0...) custom-call(bf16[512,1024]{1,0:T(8,128)(2,1)} %refs_0_.1, ...), custom_call_target="tpu_custom_call" | custom-call | tf_op jit(solution)/shard_map/forward/pallas_call | solution.py:1146
  140.5 248.4 %backward.1 = (bf16[15,512,1024]{2,1,0:T(8,128)(2,1)}, bf16[128,1024]{1,0:T(8,128)(2,1)}, f32[80,128]{1,0:T(8,128)}) custom-call(bf16[128,2048]{1,0:T(8,128)(2,1)} %get-tuple-element.53.refs_0_, bf16[128,2048]{1,0:T(8,128)(2,1)} %get-tuple-element.54.refs_1_, f32[128,2048]{1,0:T(8,128)} %get-tuple-element.55.refs_2_, f32[8,256]{1,0:T(8,128)} %get-tuple-element.56.refs_3_, ...), custom_call_target="tpu_custom_call" | custom-call | tf_op jit(solution)/shard_map/backward/pallas_call | solution.py:1786
  388.9 1.3 slice_bitcast_fusion.1
  390.2 0.7 slice_bitcast_fusion
  390.9 0.8 slice.28
  391.7 0.6 fusion
  392.2 0.6 copy.35
  392.9 0.0 copy-start
  392.9 0.0 copy-start.1
  392.9 15.9 %widen.1 = (f32[1536,1024]{1,0:T(8,128)}, f32[512,3072]{1,0:T(8,128)}, f32[512,3072]{1,0:T(8,128)}, f32[1024,1024]{1,0:T(8,128)}, f32[512,2048]{1,0:T(8,128)}, /*index=5*/f32[512,1024]{1,0:T(8,128)}, f32[512,1024]{1,0:T(8,128)}) custom-call(bf16[15,512,1024]{2,1,0:T(8,128)(2,1)} %get-tuple-element.82.refs_0_), custom_call_target="tpu_custom_call" | custom-call | tf_op jit(solution)/shard_map/widen/pallas_call | solution.py:1858
  408.8 0.0 copy-done
  408.8 0.7 copy.38
  409.5 0.0 copy-done.1
  409.5 0.7 copy.39
Async XLA Ops:
  392.9 16.0 %copy-start = (bf16[128,1024]{1,0:T(8,128)(2,1)S(1)}, bf16[128,1024]{1,0:T(8,128)(2,1)}, u32[]{:S(2)}) copy-start(bf16[128,1024]{1,0:T(8,128)(2,1)} %get-tuple-element.52) | copy-start | bytes 786436
  392.9 16.7 %copy-start.1 = (bf16[128,1024]{1,0:T(8,128)(2,1)S(1)}, bf16[128,1024]{1,0:T(8,128)(2,1)}, u32[]{:S(2)}) copy-start(bf16[128,1024]{1,0:T(8,128)(2,1)} %get-tuple-element.80) | copy-start | bytes 786436

commit v8 on v7

--- a/solution.py
+++ b/solution.py
@@ -578,6 +578,7 @@
         in_z=pltpu.VMEM((units, depth - 1, piece, PART), low),
         done=pltpu.VMEM((units, piece, PART), low),
         load=dma((depth + 3,)),
+        late_load=dma((5,)),
         send_rows=dma((4, 2)),
         recv_rows=dma((4, 2)),
         send_cols=dma((7, 3)),
@@ -612,6 +613,7 @@
     return (scale * inner - raw * (scale * scale * scale * kept), gain_grad)
 
 
+HBM = "_hbm"
 LENGTHS = "lengths"
 FORWARD_ORDER = ("key", "value", "query", "out", "gate", "up", "down")
 FF_BLOCK = 512
@@ -1241,6 +1243,19 @@
             r.kv_hbm.at[part], r.kv_all.at[part], r.load.at[offset]
         )
 
+    def late_loads():
+        pairs = (
+            (r.query_raw_hbm, r.query_raw),
+            (r.key_raw_hbm, r.key_raw),
+            (r.tokens_hbm, r.tokens),
+            (r.middle_grad_hbm, r.middle_grad),
+            (r.lowered_part_hbm, r.lowered_part),
+        )
+        return [
+            pltpu.make_async_copy(source, target, r.late_load.at[at])
+            for at, (source, target) in enumerate(pairs)
+        ]
+
     def weight_loads():
         model = r.query_weight.shape[0]
         kv = r.kv_all
@@ -1370,6 +1385,8 @@
     def query_end():
         for load in weight_loads():
             load.start()
+        for load in late_loads():
+            load.wait()
         r.small_base[...] = r.small[...]
         total = jnp.zeros((1, HEAD_DIM), jnp.float32)
         for head in range(heads):
@@ -1690,13 +1707,19 @@
         for offset in range(1, depth):
             small_along(offset).wait()
             total = total + r.small_deep[offset - 1]
-        r.small_out[...] = total
+        first = GATE_ROW // 2
+        r.grad_one[...] = total[:first]
+        r.grad_two[...] = total[first : 2 * first]
+        r.grad_heads[...] = total[2 * first : GATE_ROW]
+        r.grad_gates[...] = total[GATE_ROW : GATE_ROW + r.grad_gates.shape[0]]
 
     order = tuple(range(1, depth)) + (0,)
     for offset in order:
         kv_load(offset).start()
     rows_start(0)
     columns_start(0)
+    for load in late_loads():
+        load.start()
     prepare_heads()
 
     def at_steps(step, calls):
@@ -1775,10 +1798,16 @@
     count, width = near["queries"].shape
     heads = width // HEAD_DIM // 2
     scratch = back_scratch(depth, count, far["kv_hbm"].shape[1], heads)
+    for name, value in far.items():
+        if value.shape[0] == count:
+            scratch[name[: -len(HBM)]] = pltpu.VMEM(value.shape, value.dtype)
     outputs = dict(
         units=jax.ShapeDtypeStruct((UNITS, SIDE, 2 * SIDE), jnp.bfloat16),
-        token_grad=jax.ShapeDtypeStruct(near["tokens"].shape, jnp.bfloat16),
-        small_out=jax.ShapeDtypeStruct((VECTOR_ROWS, 128), jnp.float32),
+        token_grad=jax.ShapeDtypeStruct(far["tokens_hbm"].shape, jnp.bfloat16),
+        grad_one=jax.ShapeDtypeStruct((GATE_ROW // 2, 128), jnp.float32),
+        grad_two=jax.ShapeDtypeStruct((GATE_ROW // 2, 128), jnp.float32),
+        grad_heads=jax.ShapeDtypeStruct((1, 128), jnp.float32),
+        grad_gates=jax.ShapeDtypeStruct((GATE_ROW // 2 * 2 * heads, 128), jnp.float32),
     )
     vmem = pl.BlockSpec(memory_space=pltpu.VMEM)
     hbm = pl.BlockSpec(memory_space=pl.ANY)
@@ -1787,7 +1816,7 @@
         partial(backward_kernel, depth, names),
         out_shape=list(outputs.values()),
         in_specs=[vmem] * len(near) + [hbm] * len(far),
-        out_specs=[hbm, vmem, vmem],
+        out_specs=[hbm] + [vmem] * (len(outputs) - 1),
         scratch_shapes=list(scratch.values()),
         compiler_params=pltpu.CompilerParams(
             collective_id=4, has_side_effects=True, vmem_limit_bytes=63 * 2**20
@@ -2166,7 +2195,7 @@
         ),
         seq_lengths,
     )
-    units, token_grad, small_total = backward(
+    units, token_grad, one, two, both, gates = backward(
         dict(
             queries=f["queries"],
             heads_grad=f["heads_grad"],
@@ -2175,8 +2204,6 @@
             q_pos=f["q_pos"],
             q_begin=f["q_begin"],
             k_pos=positions,
-            query_raw=f["query_raw"],
-            key_raw=f["key_raw"],
             cosine=f["cosine"],
             sine=f["sine"],
             query_gain=f["query_gain"],
@@ -2189,13 +2216,15 @@
             mixed_in=f["mixed_in"],
             middle_low=f["middle_low"],
             lowered=f["lowered"],
-            tokens=tokens[0],
-            middle_grad=f["middle_grad"],
             attention_gain=f["attention_gain"],
-            lowered_part=f["lowered_part"],
             small=f["small"],
         ),
         dict(
+            query_raw_hbm=f["query_raw"],
+            key_raw_hbm=f["key_raw"],
+            tokens_hbm=tokens[0],
+            middle_grad_hbm=f["middle_grad"],
+            lowered_part_hbm=f["lowered_part"],
             kv_hbm=f["kv_hbm"],
             query_weight=f["query_full"],
             key_weight=f["key_full"],
@@ -2214,9 +2243,10 @@
             (1, False),
         ),
     )
-    one, two, query_part, key_part = unpack_rows(small_total[:GATE_ROW], [v.shape for v in vectors])
-    blocks, heads = (headgate_weight.shape[0] // 128, headgate_weight.shape[1])
-    headgate = small_total[GATE_ROW : GATE_ROW + blocks * heads].reshape(blocks, heads, 128)
+    half = HEAD_DIM // 2
+    one, two = (one.reshape(-1), two.reshape(-1))
+    query_part, key_part = (both[0, :half], both[0, half:])
+    headgate = gates.reshape(headgate_weight.shape[0] // 128, headgate_weight.shape[1], 128)
     headgate = headgate.transpose(0, 2, 1).reshape(headgate_weight.shape)
     return (
         f["mixed"][None],

time: 411 us -> 408 us (level)
  no operation moved by 1% of the time
where the time goes in v8:
time: 408 us
  Pallas kernels  399 us (98%)
  local copies, waits for them, and re-layouts  6.63 us (2%)
    pallas_call x1, Pallas kernels, backward(): pl.pallas_call(partial(backward_kernel, depth, names), out_shape=list(out...  248 us
    pallas_call x1, Pallas kernels, forward(): pl.pallas_call(partial(forward_kernel, depth, names, number), out_shape=l...  135 us
    pallas_call x1, Pallas kernels, widen(): pl.pallas_call(partial(widen_kernel, tuple(places)), out_shape=shapes, in...  15.9 us

profile of v8, /device:TPU:0, one launch (start us, length us, event | category | flops | bytes accessed | tf_op | source)
XLA Modules:
  0.0 407.9 jit_solution(14719668694562910556)
XLA Ops:
  0.6 0.7 stack.19
  1.3 0.7 stack.18
  2.0 0.6 maximum_convert_fusion.refs_11_
  2.6 1.2 maximum_convert_fusion.1.refs_12_
  3.9 1.5 copy.31.refs_13_
  5.3 135.1 %forward.1 = (bf16[128,1024]{1,0:T(8,128)(2,1)}, bf16[128,1024]{1,0:T(8,128)(2,1)}, f32[128,2048]{1,0:T(8,128)}, f32[128,1024]{1,0:T(8,128)}, bf16[128,2048]{1,0...) custom-call(bf16[512,1024]{1,0:T(8,128)(2,1)} %refs_0_.1, ...), custom_call_target="tpu_custom_call" | custom-call | tf_op jit(solution)/shard_map/forward/pallas_call | solution.py:1148
  140.5 247.6 %backward.1 = (bf16[15,512,1024]{2,1,0:T(8,128)(2,1)}, bf16[128,1024]{1,0:T(8,128)(2,1)}, f32[4,128]{1,0:T(4,128)}, f32[4,128]{1,0:T(4,128)}, f32[1,128]{1,0:T(1,128)}, /*index=5*/f32[64,128]{1,0:T(8,128)}) custom-call(bf16[128,2048]{1,0:T(8,128)(2,1)} %get-tuple-element.56.refs_0_, bf16[128,2048]{1,0:T(8,128)(2,1)} %get-tuple-element.57.refs_1_, ...), custom_call_target="tpu_custom_call" | custom-call | tf_op jit(solution)/shard_map/backward/pallas_call | solution.py:1815
  388.1 0.0 copy-start.2
  388.1 0.0 copy-start.5
  388.1 0.0 copy-start
  388.1 0.0 copy-start.1
  388.1 0.0 copy-start.4
  388.1 0.0 copy-start.3
  388.1 15.9 %widen.1 = (f32[1536,1024]{1,0:T(8,128)}, f32[512,3072]{1,0:T(8,128)}, f32[512,3072]{1,0:T(8,128)}, f32[1024,1024]{1,0:T(8,128)}, f32[512,2048]{1,0:T(8,128)}, /*index=5*/f32[512,1024]{1,0:T(8,128)}, f32[512,1024]{1,0:T(8,128)}) custom-call(bf16[15,512,1024]{2,1,0:T(8,128)(2,1)} %get-tuple-element.85.refs_0_), custom_call_target="tpu_custom_call" | custom-call | tf_op jit(solution)/shard_map/widen/pallas_call | solution.py:1887
  404.1 0.0 copy-done.2
  404.1 0.6 copy.35
  404.7 0.0 copy-done.5
  404.7 0.6 slice_bitcast_fusion
  405.3 0.0 copy-done
  405.3 0.7 copy.40
  406.0 0.0 copy-done.1
  406.0 0.7 copy.41
  406.7 0.0 copy-done.4
  406.7 0.6 copy.42
  407.3 0.0 copy-done.3
  407.3 0.6 copy.43
Async XLA Ops:
  388.1 16.0 %copy-start.2 = (f32[64,128]{1,0:T(8,128)S(1)}, f32[64,128]{1,0:T(8,128)}, u32[]{:S(2)}) copy-start(f32[64,128]{1,0:T(8,128)} %get-tuple-element.89) | copy-start | bytes 98308
  388.1 16.6 %copy-start.5 = (f32[1,128]{1,0:T(1,128)S(1)}, f32[1,128]{1,0:T(1,128)}, u32[]{:S(2)}) copy-start(f32[1,128]{1,0:T(1,128)} %get-tuple-element.90) | copy-start | bytes 1540
  388.1 17.2 %copy-start = (bf16[128,1024]{1,0:T(8,128)(2,1)S(1)}, bf16[128,1024]{1,0:T(8,128)(2,1)}, u32[]{:S(2)}) copy-start(bf16[128,1024]{1,0:T(8,128)(2,1)} %get-tuple-element.55) | copy-start | bytes 786436
  388.1 17.9 %copy-start.1 = (bf16[128,1024]{1,0:T(8,128)(2,1)S(1)}, bf16[128,1024]{1,0:T(8,128)(2,1)}, u32[]{:S(2)}) copy-start(bf16[128,1024]{1,0:T(8,128)(2,1)} %get-tuple-element.83) | copy-start | bytes 786436
  388.1 18.6 %copy-start.4 = (f32[4,128]{1,0:T(4,128)S(1)}, f32[4,128]{1,0:T(4,128)}, u32[]{:S(2)}) copy-start(f32[4,128]{1,0:T(4,128)} %get-tuple-element.84) | copy-start | bytes 6148
  388.1 19.2 %copy-start.3 = (f32[4,128]{1,0:T(4,128)S(1)}, f32[4,128]{1,0:T(4,128)}, u32[]{:S(2)}) copy-start(f32[4,128]{1,0:T(4,128)} %get-tuple-element.92) | copy-start | bytes 6148
